TPU v7x, 32 devices: a whole 2x2x4 slice. The times are simulated.
32 devices in a mesh: wide: 8 (over z, x), narrow: 4 (over y, core).
Axes of the slice: x: 2, y: 2, z: 4, core: 2. Of those that a mesh axis runs over, the one named last changes fastest.
Arguments:
- tokens: bfloat16 [4, 2048, 2048], P('narrow', 'wide'), may hold values from -6 to 6
- gain_one: float32 [2048], replicated, may hold values from 0.5 to 1.5
- w_qkv: bfloat16 [2048, 6144], P(('wide', 'narrow')), may hold values from -0.125 to 0.125
- w_out: bfloat16 [2048, 2048], P(('wide', 'narrow')), may hold values from -1 to 1
- gain_two: float32 [2048], replicated, may hold values from 0.5 to 1.5
- bias_two: float32 [2048], replicated, may hold values from -2 to 2
- router: float32 [2048, 4], replicated, may hold values from -0.13258252 to 0.13258252
- w_up: bfloat16 [2048, 8192], P(('wide', 'narrow')), may hold values from -0.125 to 0.125
- w_down: bfloat16 [8192, 2048], P(('wide', 'narrow')), may hold values from -0.125 to 0.125
- doc_split: int32 [4], P('narrow'), may hold values from 1 to 2048, as said below
- head_count: int32 [4, 2], P('narrow'), may hold values from 4 to 16
- width_choice: int32 [4, 2048], P('narrow', 'wide'), may hold values from 0 to 3
- out_grad: bfloat16 [4, 2048, 2048], P('narrow', 'wide'), may hold values from -6 to 6
Outputs:
- block_out: bfloat16 [4, 2048, 2048], P('narrow', 'wide')
- input_grad: float32 [4, 2048, 2048], P('narrow', 'wide')
- qkv_grad: float32 [2048, 6144], P(('wide', 'narrow'))
- out_proj_grad: float32 [2048, 2048], P(('wide', 'narrow'))
- up_grad: float32 [2048, 8192], P(('wide', 'narrow'))
- down_grad: float32 [8192, 2048], P(('wide', 'narrow'))
- gain_one_grad: float32 [2048], replicated
- gain_two_grad: float32 [2048], replicated
- bias_two_grad: float32 [2048], replicated
- router_grad: float32 [2048, 4], replicated
- width_counts: int32 [4], replicated
Inputs may be any that keep to these rules, and one draw needn't show every extreme that they name: `doc_split`: in each aligned block of 1 row one row has a value of at most 64 or of more than 1984; the other rows have values from 512 to 2048.
All inputs are finite; a program needn't handle non-finite values.
Results may differ from a plain program's by a relative error of at most 0.03.
Values may be sent and summed in bfloat16 or wider, within the bound.
A program may use at most 576 MiB of HBM per device.

v0:
```python
import jax
import jax.numpy as jnp
from jax import lax
from jax.sharding import PartitionSpec as P

HEAD_DIM = 128
FF = 8192
WIDTHS = 4


highest = lax.Precision.HIGHEST
norm_eps = 1e-05
rope_base = 10000.0
masked_score = -1e30


def rotary_tables(positions, head_size):
    half_size = head_size // 2
    exponent = jnp.arange(half_size, dtype=jnp.float32) * (2.0 / head_size)
    frequency = jnp.power(rope_base, -exponent)
    angles = positions.astype(jnp.float32)[:, None] * frequency[None, :]
    return (jnp.cos(angles), jnp.sin(angles))


def rotate(values, cosine, sine):
    half_size = values.shape[-1] // 2
    cos_part = cosine[:, None, :]
    sin_part = sine[:, None, :]
    lower = values[..., :half_size]
    upper = values[..., half_size:]
    return jnp.concatenate(
        [lower * cos_part - upper * sin_part, upper * cos_part + lower * sin_part], axis=-1
    )


def unrotate(grads, cosine, sine):
    half_size = grads.shape[-1] // 2
    cos_part = cosine[:, None, :]
    sin_part = sine[:, None, :]
    lower = grads[..., :half_size]
    upper = grads[..., half_size:]
    return jnp.concatenate(
        [lower * cos_part + upper * sin_part, upper * cos_part - lower * sin_part], axis=-1
    )


def ffn_pass(act_rows, grad_rows, up_weight, down_weight, mask_cols):
    pre = jnp.einsum("rcd,df->rcf", act_rows, up_weight, preferred_element_type=jnp.float32)
    hidden = (jnp.square(jnp.maximum(pre, 0.0)) * mask_cols).astype(jnp.bfloat16)
    mixed = jnp.einsum("rcf,fd->rcd", hidden, down_weight, preferred_element_type=jnp.float32)
    grad_down = jnp.einsum("rcf,rcd->fd", hidden, grad_rows, preferred_element_type=jnp.float32)
    grad_hidden = jnp.einsum(
        "rcd,fd->rcf", grad_rows, down_weight, preferred_element_type=jnp.float32
    )
    grad_pre = (grad_hidden * mask_cols * 2.0 * jnp.maximum(pre, 0.0)).astype(jnp.bfloat16)
    grad_up = jnp.einsum("rcd,rcf->df", act_rows, grad_pre, preferred_element_type=jnp.float32)
    grad_act = jnp.einsum("rcf,df->rcd", grad_pre, up_weight, preferred_element_type=jnp.float32)
    return (mixed, grad_act, grad_up, grad_down)


def on_device(
    tokens,
    gain_one,
    w_qkv,
    w_out,
    gain_two,
    bias_two,
    router,
    w_up,
    w_down,
    doc_split,
    head_count,
    width_choice,
    out_grad,
):
    row_count, local_len, model_dim = tokens.shape
    head_size = HEAD_DIM
    head_total = model_dim // head_size
    scale = head_size ** (-0.5)
    first_pos = lax.axis_index("wide") * local_len
    query_pos = first_pos + jnp.arange(local_len, dtype=jnp.int32)
    query_doc = (query_pos[None, :] >= doc_split[:, None]).astype(jnp.int32)
    head_limit = jnp.where(query_doc == 0, head_count[:, 0:1], head_count[:, 1:2])
    active = (
        jnp.arange(head_total, dtype=jnp.int32)[None, None, :] < head_limit[:, :, None]
    ).astype(jnp.float32)
    width_onehot = (
        width_choice[:, :, None] == jnp.arange(WIDTHS, dtype=jnp.int32)[None, None, :]
    ).astype(jnp.float32)
    cosine, sine = rotary_tables(query_pos, head_size)

    def allowed_mask(query_at, query_in, key_at):
        key_in = (key_at[None, :] >= doc_split[:, None]).astype(jnp.int32)
        return (key_at[None, None, :] <= query_at[None, :, None]) & (
            key_in[:, None, :] == query_in[:, :, None]
        )

    inputs = tokens.astype(jnp.float32)
    qkv_full, out_full = (
        lax.all_gather(w_qkv, ("wide", "narrow"), axis=0, tiled=True),
        lax.all_gather(w_out, ("wide", "narrow"), axis=0, tiled=True),
    )
    inv_one = lax.rsqrt(jnp.mean(inputs * inputs, axis=-1, keepdims=True) + norm_eps)
    normed_one = inputs * inv_one
    act_one = (normed_one * gain_one).astype(jnp.bfloat16)
    projected = jnp.einsum("rcd,de->rce", act_one, qkv_full, preferred_element_type=jnp.float32)
    split_qkv = projected.reshape(row_count, local_len, 3, head_total, head_size)
    queries = rotate(split_qkv[:, :, 0], cosine, sine).astype(jnp.bfloat16)
    keys = rotate(split_qkv[:, :, 1], cosine, sine).astype(jnp.bfloat16)
    values = split_qkv[:, :, 2].astype(jnp.bfloat16)
    start_max = jnp.full((row_count, head_total, local_len), masked_score, jnp.float32)
    running_max = start_max
    key_piece = lax.all_gather(keys, "wide", axis=1, tiled=True)
    value_piece = lax.all_gather(values, "wide", axis=1, tiled=True)
    key_at = jnp.arange(key_piece.shape[1], dtype=jnp.int32)
    allowed = allowed_mask(query_pos, query_doc, key_at)[:, None]
    scores = (
        jnp.einsum("rqhe,rkhe->rhqk", queries, key_piece, preferred_element_type=jnp.float32)
        * scale
    )
    scores = jnp.where(allowed, scores, masked_score)
    new_max = jnp.maximum(running_max, jnp.max(scores, axis=-1))
    weights = jnp.where(allowed, jnp.exp(scores - new_max[..., None]), 0.0)
    totals = jnp.sum(weights, axis=-1)
    update = jnp.einsum(
        "rhqk,rkhe->rqhe",
        weights.astype(jnp.bfloat16),
        value_piece,
        preferred_element_type=jnp.float32,
    )
    weighted = update
    running_max, totals, weighted = (new_max, totals, weighted)
    attended = weighted / jnp.transpose(totals, (0, 2, 1))[..., None]
    log_total = running_max + jnp.log(totals)
    att_low = (
        (attended * active[..., None]).astype(jnp.bfloat16).reshape(row_count, local_len, model_dim)
    )
    branch = jnp.einsum("rcd,de->rce", att_low, out_full, preferred_element_type=jnp.float32)
    x_one = inputs + branch
    center = x_one - jnp.mean(x_one, axis=-1, keepdims=True)
    inv_two = lax.rsqrt(jnp.mean(center * center, axis=-1, keepdims=True) + norm_eps)
    normed_two = center * inv_two
    ln_out = normed_two * gain_two + bias_two
    logits = jnp.einsum("rcd,dw->rcw", ln_out, router, precision=highest)
    router_prob = jax.nn.softmax(logits, axis=-1)
    chosen = jnp.sum(router_prob * width_onehot, axis=-1)
    act_two = ln_out.astype(jnp.bfloat16)
    grad_top = out_grad.astype(jnp.float32)
    grad_mixed = (grad_top * chosen[..., None]).astype(jnp.bfloat16)
    counts_here = jnp.sum(width_onehot, axis=(0, 1))
    up_full, down_full = (
        lax.all_gather(w_up, ("wide", "narrow"), axis=0, tiled=True),
        lax.all_gather(w_down, ("wide", "narrow"), axis=0, tiled=True),
    )
    column_block = jnp.arange(FF, dtype=jnp.int32) // (FF // WIDTHS)
    column_mask = (column_block[None, None, :] <= width_choice[:, :, None]).astype(jnp.float32)
    mixed, grad_act_two, grad_up, grad_down = ffn_pass(
        act_two, grad_mixed, up_full, down_full, column_mask
    )
    up_grad, down_grad = (
        lax.psum_scatter(grad_up, ("wide", "narrow"), scatter_dimension=0, tiled=True),
        lax.psum_scatter(grad_down, ("wide", "narrow"), scatter_dimension=0, tiled=True),
    )
    block_out = (x_one + mixed * chosen[..., None]).astype(jnp.bfloat16)
    grad_prob = jnp.sum(grad_top * mixed, axis=-1)
    grad_logits = grad_prob[..., None] * chosen[..., None] * (width_onehot - router_prob)
    grad_router = jnp.einsum("rcd,rcw->dw", ln_out, grad_logits, precision=highest)
    grad_ln = grad_act_two + jnp.einsum("rcw,dw->rcd", grad_logits, router, precision=highest)
    grad_gain_two = jnp.sum(grad_ln * normed_two, axis=(0, 1))
    grad_bias_two = jnp.sum(grad_ln, axis=(0, 1))
    grad_normed = grad_ln * gain_two
    grad_x_one = grad_top + inv_two * (
        grad_normed
        - jnp.mean(grad_normed, axis=-1, keepdims=True)
        - normed_two * jnp.mean(grad_normed * normed_two, axis=-1, keepdims=True)
    )
    grad_branch = grad_x_one.astype(jnp.bfloat16)
    grad_out = jnp.einsum("rcd,rce->de", att_low, grad_branch, preferred_element_type=jnp.float32)
    grad_att = jnp.einsum("rce,de->rcd", grad_branch, out_full, preferred_element_type=jnp.float32)
    grad_heads = grad_att.astype(jnp.bfloat16).reshape(
        row_count, local_len, head_total, head_size
    ) * active[..., None].astype(jnp.bfloat16)
    delta = jnp.sum(grad_heads.astype(jnp.float32) * attended, axis=-1)
    delta_hq = jnp.transpose(delta, (0, 2, 1))
    lse_all, delta_all = (
        lax.all_gather(
            jnp.transpose(log_total, (0, 2, 1)).astype(jnp.bfloat16), "wide", axis=1, tiled=True
        ).astype(jnp.float32),
        lax.all_gather(delta.astype(jnp.bfloat16), "wide", axis=1, tiled=True).astype(delta.dtype),
    )
    key_piece = lax.all_gather(keys, "wide", axis=1, tiled=True)
    value_piece = lax.all_gather(values, "wide", axis=1, tiled=True)
    key_at = jnp.arange(key_piece.shape[1], dtype=jnp.int32)
    allowed = allowed_mask(query_pos, query_doc, key_at)[:, None]
    scores = (
        jnp.einsum("rqhe,rkhe->rhqk", queries, key_piece, preferred_element_type=jnp.float32)
        * scale
    )
    scores = jnp.where(allowed, scores, masked_score)
    chance = jnp.where(allowed, jnp.exp(scores - log_total[..., None]), 0.0)
    grad_chance = jnp.einsum(
        "rqhe,rkhe->rhqk", grad_heads, value_piece, preferred_element_type=jnp.float32
    )
    grad_scores = (chance * (grad_chance - delta_hq[..., None])).astype(jnp.bfloat16)
    grad_queries = (
        jnp.einsum("rhqk,rkhe->rqhe", grad_scores, key_piece, preferred_element_type=jnp.float32)
        * scale
    )
    query_piece = lax.all_gather(queries, "wide", axis=1, tiled=True)
    grad_piece = lax.all_gather(grad_heads, "wide", axis=1, tiled=True)
    count_here = query_piece.shape[1]
    query_at = jnp.arange(count_here, dtype=jnp.int32)
    query_in = (query_at[None, :] >= doc_split[:, None]).astype(jnp.int32)
    allowed = allowed_mask(query_at, query_in, query_pos)[:, None]
    scores = (
        jnp.einsum("rqhe,rkhe->rhqk", query_piece, keys, preferred_element_type=jnp.float32) * scale
    )
    scores = jnp.where(allowed, scores, masked_score)
    lse_piece = jnp.transpose(lse_all, (0, 2, 1))
    delta_piece = jnp.transpose(delta_all, (0, 2, 1))
    chance = jnp.where(allowed, jnp.exp(scores - lse_piece[..., None]), 0.0)
    grad_values = jnp.einsum(
        "rhqk,rqhe->rkhe",
        chance.astype(jnp.bfloat16),
        grad_piece,
        preferred_element_type=jnp.float32,
    )
    grad_chance = jnp.einsum(
        "rqhe,rkhe->rhqk", grad_piece, values, preferred_element_type=jnp.float32
    )
    grad_scores = (chance * (grad_chance - delta_piece[..., None])).astype(jnp.bfloat16)
    grad_keys = jnp.einsum(
        "rhqk,rqhe->rkhe", grad_scores, query_piece, preferred_element_type=jnp.float32
    )
    grad_keys, grad_values = (grad_keys, grad_values)
    grad_q_raw = unrotate(grad_queries, cosine, sine)
    grad_k_raw = unrotate(grad_keys * scale, cosine, sine)
    grad_proj = (
        jnp.stack([grad_q_raw, grad_k_raw, grad_values], axis=2)
        .reshape(row_count, local_len, 3 * model_dim)
        .astype(jnp.bfloat16)
    )
    grad_qkv = jnp.einsum("rcd,rce->de", act_one, grad_proj, preferred_element_type=jnp.float32)
    grad_act_one = jnp.einsum(
        "rce,de->rcd", grad_proj, qkv_full, preferred_element_type=jnp.float32
    )
    qkv_grad, out_proj_grad = (
        lax.psum_scatter(grad_qkv, ("wide", "narrow"), scatter_dimension=0, tiled=True),
        lax.psum_scatter(grad_out, ("wide", "narrow"), scatter_dimension=0, tiled=True),
    )
    grad_gain_one = jnp.sum(grad_act_one * normed_one, axis=(0, 1))
    grad_scaled = grad_act_one * gain_one
    input_grad = grad_x_one + inv_one * (
        grad_scaled - normed_one * jnp.mean(grad_scaled * normed_one, axis=-1, keepdims=True)
    )
    router_grad, gain_one_grad, gain_two_grad, bias_two_grad, counts_all = lax.psum(
        (grad_router, grad_gain_one, grad_gain_two, grad_bias_two, counts_here), ("wide", "narrow")
    )
    return (
        block_out,
        input_grad,
        qkv_grad,
        out_proj_grad,
        up_grad,
        down_grad,
        gain_one_grad,
        gain_two_grad,
        bias_two_grad,
        router_grad,
        counts_all.astype(jnp.int32),
    )


def solution(mesh):
    in_specs = (
        P("narrow", "wide", None),
        P(),
        P(("wide", "narrow"), None),
        P(("wide", "narrow"), None),
        P(),
        P(),
        P(),
        P(("wide", "narrow"), None),
        P(("wide", "narrow"), None),
        P("narrow"),
        P("narrow", None),
        P("narrow", "wide"),
        P("narrow", "wide", None),
    )
    out_specs = (
        P("narrow", "wide", None),
        P("narrow", "wide", None),
        P(("wide", "narrow"), None),
        P(("wide", "narrow"), None),
        P(("wide", "narrow"), None),
        P(("wide", "narrow"), None),
        P(),
        P(),
        P(),
        P(),
        P(),
    )
    return jax.shard_map(
        on_device, mesh=mesh, in_specs=in_specs, out_specs=out_specs, check_vma=False
    )
```

profile of v0, /device:TPU:8, one launch (start us, length us, event | category | flops | bytes accessed | tf_op | source)
XLA Modules:
  0.0 3236.3 jit_solution(4263275376613446644)
XLA Ops:
  13.1 151.8 %all-gather.10.cloned.1.call-done = bf16[2048,6144]{1,0:T(8,128)(2,1)} async-done(((bf16[64,6144]{1,0:T(8,128)(2,1)}), bf16[2048,6144]{1,0:T(8,128)(2,1)}) %all-gather.10.cloned.1.call-update) | async-done | bytes 25165840 | tf_op jit(solution)/shard_map/all_gather | solution.py:100
  164.9 32.6 %copy.31 = bf16[6144,2048]{1,0:T(8,128)(2,1)} copy(bf16[6144,2048]{0,1:T(8,128)(2,1)} %bitcast.201) | data formatting | bytes 50331648 | tf_op jit(solution)/shard_map/rcd,de->rce/dot_general | solution.py:106
  197.5 12.3 convolution_bitcast_fusion.1
  221.8 117.1 %all-gather.12.cloned.1.call-done = bf16[1,2048,16,128]{1,3,2,0:T(8,128)(2,1)} async-done(((bf16[1,256,16,128]{1,3,2,0:T(8,128)(2,1)}), bf16[1,2048,16,128]{1,3,2,0:T(8,128)(2,1)}) %all-gather.12.cloned.1.call-update) | async-done | bytes 8388624 | tf_op jit(solution)/shard_map/all_gather | solution.py:113
  338.9 18.8 fusion.3
  357.7 15.7 fusion
  373.4 91.7 %all-gather.24.cloned.1.call-done = bf16[1,2048,1,16,128]{1,4,3,2,0:T(8,128)(2,1)} async-done(((bf16[1,256,1,16,128]{1,4,3,2,0:T(8,128)(2,1)}), bf16[1,2048,1,16,128]{1,4,3,2,0:T(8,128)(2,1)}) %all-gather.24.cloned.1.call-update) | async-done | bytes 8388624 | tf_op jit(solution)/shard_map/all_gather | solution.py:114
  465.2 18.8 multiply_convert_fusion.4
  483.9 61.6 %all-gather.14.cloned.1.call-done = bf16[2048,2048]{1,0:T(8,128)(2,1)} async-done(((bf16[64,2048]{1,0:T(8,128)(2,1)}), bf16[2048,2048]{1,0:T(8,128)(2,1)}) %all-gather.14.cloned.1.call-update) | async-done | bytes 8388624 | tf_op jit(solution)/shard_map/all_gather | solution.py:101
  554.2 185.5 %all-gather.16.cloned.1.call-done = bf16[2048,8192]{1,0:T(8,128)(2,1)} async-done(((bf16[64,8192]{1,0:T(8,128)(2,1)}), bf16[2048,8192]{1,0:T(8,128)(2,1)}) %all-gather.16.cloned.1.call-update) | async-done | bytes 33554448 | tf_op jit(solution)/shard_map/all_gather | solution.py:152
  739.8 17.4 convolution_maximum_fusion
  757.2 178.3 %all-gather.18.cloned.1.call-done = bf16[8192,2048]{1,0:T(8,128)(2,1)} async-done(((bf16[256,2048]{1,0:T(8,128)(2,1)}), bf16[8192,2048]{1,0:T(8,128)(2,1)}) %all-gather.18.cloned.1.call-update) | async-done | bytes 33554448 | tf_op jit(solution)/shard_map/all_gather | solution.py:153
  935.5 19.8 fusion.46
  955.3 18.3 fusion.20
  973.5 17.4 fusion.146
  1008.3 8.2 fusion.86
  1017.8 29.7 all_gather.39
  1047.5 14.5 all-gather.20.cloned.1.call-done
  1062.1 16.3 fusion.26
  1078.6 30.0 all_gather.41
  1110.4 23.3 multiply_bitcast_fusion.1
  1133.7 55.3 %all-gather.22.cloned.1.call-done = bf16[1,2048,16,128]{1,3,2,0:T(8,128)(2,1)} async-done(((bf16[1,256,16,128]{1,3,2,0:T(8,128)(2,1)}), bf16[1,2048,16,128]{1,3,2,0:T(8,128)(2,1)}) %all-gather.22.cloned.1.call-update) | async-done | bytes 8388624 | tf_op jit(solution)/shard_map/all_gather | solution.py:210
  1189.0 23.0 multiply_bitcast_fusion
  1216.1 14.7 fusion.61
  1232.9 22.4 fusion.89
  1256.9 26.3 fusion.104
  1284.0 28.1 fusion.99
  1314.3 14.1 fusion.43
  1328.4 45.5 %all-reduce = (f32[2048]{0:T(1024)}, f32[2048]{0:T(1024)}, f32[2048]{0:T(1024)}, f32[2048,4]{0,1:T(4,128)}, f32[4]{0:T(128)S(1)}) all-reduce(f32[2048]{0:T(1024)S(1)} %get-tuple-element.13, f32[2048]{0:T(1024)S(1)} %copy-done.45, f32[2048]{0:T(1024)S(1)} %copy-done.46, ...), channel_id=1, replica_groups=mesh['wide'=8,'narrow'=4] {'wide','narrow'}, use_global_device_ids=true, to_apply=%region_18.19 | all-reduce | flops 14340 | bytes 114720 | tf_op jit(solution)/shard_map/psum | solution.py:256
  1377.9 437.6 %reduce-scatter.5.cloned.1.call-done = f32[64,6144]{1,0:T(8,128)} async-done(((f32[2048,6144]{1,0:T(8,128)}), f32[64,6144]{1,0:T(8,128)}) %reduce-scatter.5.cloned.1.call-update) | async-done | bytes 1572880 | tf_op jit(solution)/shard_map/reduce_scatter | solution.py:248
  1815.5 705.0 %reduce-scatter.9.cloned.1.call-done = f32[64,8192]{1,0:T(8,128)} async-done(((f32[2048,8192]{1,0:T(8,128)}), f32[64,8192]{1,0:T(8,128)}) %reduce-scatter.9.cloned.1.call-update) | async-done | bytes 2097168 | tf_op jit(solution)/shard_map/reduce_scatter | solution.py:161
  2520.5 708.7 %reduce-scatter.11.cloned.1.call-done = f32[256,2048]{1,0:T(8,128)} async-done(((f32[8192,2048]{1,0:T(8,128)}), f32[256,2048]{1,0:T(8,128)}) %reduce-scatter.11.cloned.1.call-update) | async-done | bytes 2097168 | tf_op jit(solution)/shard_map/reduce_scatter | solution.py:162
  (194 shorter events, 61.0 us)
Async XLA Ops:
  7.2 544.9 %copy-start = (f32[2048,4]{0,1:T(4,128)S(1)}, f32[2048,4]{0,1:T(4,128)}, u32[]{:S(2)}) copy-start(f32[2048,4]{0,1:T(4,128)} %param.19) | copy-start | bytes 98308
  7.2 157.7 %all-gather.10.cloned.1.call-start = ((), (), s32[]{:S(2)}) async-start(), calls=%async_computation.4 | async-start | bytes 25952256 | tf_op jit(solution)/shard_map/all_gather | solution.py:100
  7.9 331.0 %all-gather.12.cloned.1.call-start = ((), (), s32[]{:S(2)}) async-start(), calls=%async_computation.5 | async-start | bytes 9437184 | tf_op jit(solution)/shard_map/all_gather | solution.py:113
  12.8 184.7 %copy-start.41 = (f32[256]{0:T(256)}, f32[256]{0:T(256)S(1)}, u32[]{:S(2)}) copy-start(f32[256]{0:T(256)S(1)} %add_rsqrt_fusion.1) | copy-start | bytes 3076
  13.1 199.4 %copy-start.23 = (f32[256,64]{0,1:T(8,128)}, f32[256,64]{0,1:T(8,128)S(1)}, u32[]{:S(2)}) copy-start(f32[256,64]{0,1:T(8,128)S(1)} %get-tuple-element.42) | copy-start | bytes 196612
  13.1 199.4 %copy-start.25 = (f32[256,64]{0,1:T(8,128)}, f32[256,64]{0,1:T(8,128)S(1)}, u32[]{:S(2)}) copy-start(f32[256,64]{0,1:T(8,128)S(1)} %get-tuple-element.43) | copy-start | bytes 196612
  215.2 250.0 %all-gather.24.cloned.1.call-start = ((), (), s32[]{:S(2)}) async-start(), calls=%async_computation.15 | async-start | bytes 9437184 | tf_op jit(solution)/shard_map/all_gather | solution.py:114
  217.9 327.6 %all-gather.14.cloned.1.call-start = ((), (), s32[]{:S(2)}) async-start(), calls=%async_computation.6 | async-start | bytes 8650752 | tf_op jit(solution)/shard_map/all_gather | solution.py:101
  218.5 521.2 %all-gather.16.cloned.1.call-start = ((), (), s32[]{:S(2)}) async-start(), calls=%async_computation.7 | async-start | bytes 34603008 | tf_op jit(solution)/shard_map/all_gather | solution.py:152
  219.1 716.4 %all-gather.18.cloned.1.call-start = ((), (), s32[]{:S(2)}) async-start(), calls=%async_computation.8 | async-start | bytes 34603008 | tf_op jit(solution)/shard_map/all_gather | solution.py:153
  219.7 842.4 %all-gather.20.cloned.1.call-start = ((), (), s32[]{:S(2)}) async-start(), calls=%async_computation.9 | async-start | bytes 9437184 | tf_op jit(solution)/shard_map/all_gather | solution.py:209
  219.8 138.0 %copy-start.53 = (s32[256]{0:T(256)}, s32[256]{0:T(256)S(1)}, u32[]{:S(2)}) copy-start(s32[256]{0:T(256)S(1)} %iota_add_fusion) | copy-start | bytes 3076
  219.8 138.0 %copy-start.49 = (s32[256]{0:T(256)}, s32[256]{0:T(256)S(1)}, u32[]{:S(2)}) copy-start(s32[256]{0:T(256)S(1)} %compare_convert_fusion) | copy-start | bytes 3076
  219.8 137.9 %copy-start.37 = (s32[2048]{0:T(1024)}, s32[2048]{0:T(1024)S(1)}, u32[]{:S(2)}) copy-start(s32[2048]{0:T(1024)S(1)} %fusion.113) | copy-start | bytes 24580
  219.8 735.4 %copy-start.29 = (s32[8192]{0:T(1024)}, s32[8192]{0:T(1024)S(1)}, u32[]{:S(2)}) copy-start(s32[8192]{0:T(1024)S(1)} %add_select_fusion) | copy-start | bytes 98308
  220.4 244.8 %copy-start.9 = (pred[256,2048]{1,0:T(8,128)(4,1)}, pred[256,2048]{1,0:T(8,128)(4,1)S(1)}, u32[]{:S(2)}) copy-start(pred[256,2048]{1,0:T(8,128)(4,1)S(1)} %fusion.55) | copy-start | bytes 1572868
  221.6 967.4 %all-gather.22.cloned.1.call-start = ((), (), s32[]{:S(2)}) async-start(), calls=%async_computation.10 | async-start | bytes 9437184 | tf_op jit(solution)/shard_map/all_gather | solution.py:210
  551.7 445.1 %copy-start.2 = (f32[1,256,2048]{2,1,0:T(8,128)}, f32[1,256,2048]{2,1,0:T(8,128)S(1)}, u32[]{:S(2)}) copy-start(f32[1,256,2048]{2,1,0:T(8,128)S(1)} %get-tuple-element.53) | copy-start | bytes 6291460
  551.7 445.0 %copy-start.33 = (f32[256]{0:T(256)}, f32[256]{0:T(256)S(1)}, u32[]{:S(2)}) copy-start(f32[256]{0:T(256)S(1)} %broadcast_multiply_fusion.4) | copy-start | bytes 3076
  552.1 444.6 %copy-start.35 = (f32[256]{0:T(256)}, f32[256]{0:T(256)S(1)}, u32[]{:S(2)}) copy-start(f32[256]{0:T(256)S(1)} %add_rsqrt_fusion) | copy-start | bytes 3076
  554.2 436.7 %copy-start.43 = (f32[256,4]{0,1:T(4,128)}, f32[256,4]{0,1:T(4,128)S(1)}, u32[]{:S(2)}) copy-start(f32[256,4]{0,1:T(4,128)S(1)} %get-tuple-element.25) | copy-start | bytes 12292
  554.2 442.6 %copy-start.47 = (f32[256]{0:T(256)}, f32[256]{0:T(256)S(1)}, u32[]{:S(2)}) copy-start(f32[256]{0:T(256)S(1)} %get-tuple-element.24) | copy-start | bytes 3076
  554.2 381.3 %copy-start.17 = (bf16[1,256,2048]{2,1,0:T(8,128)(2,1)S(1)}, bf16[1,256,2048]{2,1,0:T(8,128)(2,1)}, u32[]{:S(2)}) copy-start(bf16[1,256,2048]{2,1,0:T(8,128)(2,1)} %param.25) | copy-start | bytes 3145732
  1008.2 369.7 %reduce-scatter.7.cloned.1.call-start = ((), (), s32[]{:S(2)}) async-start(), calls=%async_computation.12 | async-start | bytes 17301504 | tf_op jit(solution)/shard_map/reduce_scatter | solution.py:249
  1016.5 45.6 %copy-start.13 = (bf16[1,256,16,64]{1,3,2,0:T(8,128)(2,1)S(1)}, bf16[1,256,16,64]{1,3,2,0:T(8,128)(2,1)}, u32[]{:S(2)}) copy-start(bf16[1,256,16,64]{1,3,2,0:T(8,128)(2,1)} %copy-done.12) | copy-start | bytes 1572868
  1016.5 799.0 %reduce-scatter.5.cloned.1.call-start = ((), (), s32[]{:S(2)}) async-start(), calls=%async_computation.11 | async-start | bytes 51904512 | tf_op jit(solution)/shard_map/reduce_scatter | solution.py:248
  1133.7 78.3 %copy-start.24 = (f32[256,64]{0,1:T(8,128)S(1)}, f32[256,64]{0,1:T(8,128)}, u32[]{:S(2)}) copy-start(f32[256,64]{0,1:T(8,128)} %copy-done.23) | copy-start | bytes 196612
  1133.7 78.3 %copy-start.26 = (f32[256,64]{0,1:T(8,128)S(1)}, f32[256,64]{0,1:T(8,128)}, u32[]{:S(2)}) copy-start(f32[256,64]{0,1:T(8,128)} %copy-done.25) | copy-start | bytes 196612
  1255.3 1265.2 %reduce-scatter.9.cloned.1.call-start = ((), (), s32[]{:S(2)}) async-start(), calls=%async_computation.13 | async-start | bytes 69206016 | tf_op jit(solution)/shard_map/reduce_scatter | solution.py:161
  1283.2 1946.0 %reduce-scatter.11.cloned.1.call-start = ((), (), s32[]{:S(2)}) async-start(), calls=%async_computation.14 | async-start | bytes 69206016 | tf_op jit(solution)/shard_map/reduce_scatter | solution.py:162
  1314.3 60.1 %copy-start.8 = (f32[1,256,2048]{2,1,0:T(8,128)S(1)}, f32[1,256,2048]{2,1,0:T(8,128)}, u32[]{:S(2)}) copy-start(f32[1,256,2048]{2,1,0:T(8,128)} %copy-done.6) | copy-start | bytes 6291460
  1374.4 1854.8 %copy-start.1 = (f32[2048,4]{0,1:T(4,128)S(1)}, f32[2048,4]{0,1:T(4,128)}, u32[]{:S(2)}) copy-start(f32[2048,4]{0,1:T(4,128)} %param.19) | copy-start | bytes 98308
  (38 other events, 295.0 us)
Sparse Core Ops, SparseCore 0:
  10.9 153.9 all-gather.9
  215.3 123.5 all-gather.11
  341.5 123.5 all-gather.23
  467.9 77.6 all-gather.13
  548.2 191.4 all-gather.15
  742.5 192.9 all-gather.17
  937.5 124.4 all-gather.19
  1064.7 124.2 all-gather.21
  1191.9 185.0 reduce-scatter.6
  1383.8 431.7 reduce-scatter.4
  1818.4 702.0 reduce-scatter.8
  2523.3 705.8 reduce-scatter.10
where the time goes:
time: 3250 us; the launch traced here: 3240 us
  waiting for transfers between devices  2710 us (83%)
  matrix products  316 us (10%)
  blocking collectives  105 us (3%)
  local copies, waits for them, and re-layouts  49.2 us (2%)
  other arithmetic  40 us (1%)
    reduce_scatter x1, waiting for transfers between devices, on_device(): lax.psum_scatter(grad_down, ('wide', 'narrow'), scatter_dimension=0, tile...  709 us
    reduce_scatter x1, waiting for transfers between devices, on_device(): lax.psum_scatter(grad_up, ('wide', 'narrow'), scatter_dimension=0, tiled=...  705 us
    reduce_scatter x1, waiting for transfers between devices, on_device(): lax.psum_scatter(grad_qkv, ('wide', 'narrow'), scatter_dimension=0, tiled...  438 us
    all_gather x1, waiting for transfers between devices, on_device(): lax.all_gather(w_up, ('wide', 'narrow'), axis=0, tiled=True)  186 us
    all_gather x1, waiting for transfers between devices, on_device(): lax.all_gather(w_down, ('wide', 'narrow'), axis=0, tiled=True)  178 us
    all_gather x1, waiting for transfers between devices, on_device(): lax.all_gather(w_qkv, ('wide', 'narrow'), axis=0, tiled=True)  152 us
    all_gather x1, waiting for transfers between devices, on_device(): key_piece = lax.all_gather(keys, 'wide', axis=1, tiled=True)  117 us
    all_gather x1, waiting for transfers between devices, on_device(): value_piece = lax.all_gather(values, 'wide', axis=1, tiled=True)  91.7 us
  transfers between devices with their start and end apart: 12, of which 11 were waited for; matrix products, arithmetic and copies ran while one was open for 11% of the time, Pallas kernels for 0%

commit v1 on v0

v1 whole, which is shorter than its diff:
```python
import functools

import jax
import jax.numpy as jnp
from jax import lax
from jax.experimental import pallas as pl
from jax.experimental.pallas import tpu as pltpu
from jax.sharding import PartitionSpec as P

HEAD_DIM = 128
WIDTHS = 4
BLOCK = 512

highest = lax.Precision.HIGHEST
norm_eps = 1e-05
rope_base = 10000.0
masked_score = -1e30
f32 = jnp.float32
bf16 = jnp.bfloat16


def dot(a, b, contract):
    return lax.dot_general(a, b, (contract, ((), ())), preferred_element_type=f32)


def turn(u, cos2, sin2):
    return u * cos2 + pltpu.roll(u, HEAD_DIM // 2, 1) * sin2


def first_key(split, row):
    return jnp.where(row >= split, split, 0)


def attend_kernel(heads, length, split_ref, limit_ref, proj_ref, cos_ref, sin_ref, qkv_ref, att_ref, low_ref, lse_ref):
    row = pl.program_id(0)
    split = split_ref[row]
    scale = HEAD_DIM ** (-0.5)
    block = min(BLOCK, length)
    blocks = length // block
    width = heads * HEAD_DIM

    def rotate_block(i, carry):
        rows = pl.ds(pl.multiple_of(i * block, block), block)
        cos2 = cos_ref[rows, :]
        sin2 = sin_ref[rows, :]
        for part in range(2 * heads):
            cols = pl.ds(part * HEAD_DIM, HEAD_DIM)
            qkv_ref[rows, cols] = turn(proj_ref[rows, cols], cos2, sin2).astype(bf16)
        cols = pl.ds(2 * width, width)
        qkv_ref[rows, cols] = proj_ref[rows, cols].astype(bf16)
        return carry

    lax.fori_loop(0, blocks, rotate_block, 0)
    for h in range(heads):
        qcol = pl.ds(h * HEAD_DIM, HEAD_DIM)
        kcol = pl.ds(width + h * HEAD_DIM, HEAD_DIM)
        vcol = pl.ds(2 * width + h * HEAD_DIM, HEAD_DIM)

        def query_block(i, carry):
            rows = pl.ds(pl.multiple_of(i * block, block), block)
            q = qkv_ref[rows, qcol]
            at = i * block + lax.broadcasted_iota(jnp.int32, (block, 1), 0)
            low = first_key(split, at)

            def key_block(j, state):
                top, total, acc = state
                keys = pl.ds(pl.multiple_of(j * block, block), block)
                s = dot(q, qkv_ref[keys, kcol], ((1,), (1,))) * scale
                kat = j * block + lax.broadcasted_iota(jnp.int32, (block, block), 1)
                ok = (kat <= at) & (kat >= low)
                s = jnp.where(ok, s, masked_score)
                new_top = jnp.maximum(top, jnp.max(s, axis=1, keepdims=True))
                p = jnp.where(ok, jnp.exp(s - new_top), 0.0)
                fade = jnp.exp(top - new_top)
                total = total * fade + jnp.sum(p, axis=1, keepdims=True)
                acc = acc * fade + dot(p.astype(bf16), qkv_ref[keys, vcol], ((1,), (0,)))
                return new_top, total, acc

            start = jnp.where(i * block >= split, split // block, 0)
            top, total, acc = lax.fori_loop(
                start,
                i + 1,
                key_block,
                (
                    jnp.full((block, 1), masked_score, f32),
                    jnp.zeros((block, 1), f32),
                    jnp.zeros((block, HEAD_DIM), f32),
                ),
            )
            att = acc / total
            limit = jnp.where(at < split, limit_ref[row, 0], limit_ref[row, 1])
            active = (limit_ref[row, 2] + h < limit).astype(f32)
            att_ref[rows, qcol] = att
            low_ref[rows, qcol] = (att * active).astype(bf16)
            lse_ref[rows, qcol] = jnp.broadcast_to(top + jnp.log(total), (block, HEAD_DIM))
            return carry

        lax.fori_loop(0, blocks, query_block, 0)


def attend(proj, split, limits, cos2, sin2, heads):
    rows, length, _ = proj.shape
    width = heads * HEAD_DIM
    smem = pl.BlockSpec(memory_space=pltpu.SMEM)
    table = pl.BlockSpec((length, HEAD_DIM), lambda r: (0, 0))

    def whole(cols):
        return pl.BlockSpec((None, length, cols), lambda r: (r, 0, 0))

    flops = rows * heads * 4 * length * length * HEAD_DIM
    return pl.pallas_call(
        functools.partial(attend_kernel, heads, length),
        grid=(rows,),
        in_specs=[smem, smem, whole(3 * width), table, table],
        out_specs=[whole(3 * width), whole(width), whole(width), whole(width)],
        out_shape=[
            jax.ShapeDtypeStruct((rows, length, 3 * width), bf16),
            jax.ShapeDtypeStruct((rows, length, width), f32),
            jax.ShapeDtypeStruct((rows, length, width), bf16),
            jax.ShapeDtypeStruct((rows, length, width), f32),
        ],
        compiler_params=pltpu.CompilerParams(vmem_limit_bytes=56 * 2**20),
        cost_estimate=pl.CostEstimate(flops=flops, bytes_accessed=2**24, transcendentals=flops // 512),
    )(split, limits, proj, cos2, sin2)


def attend_back_kernel(heads, length, split_ref, limit_ref, qkv_ref, att_ref, lse_ref, dat_ref, cos_ref, sin_ref, dproj_ref, datt_ref, delta_ref, dq_ref):
    row = pl.program_id(0)
    split = split_ref[row]
    scale = HEAD_DIM ** (-0.5)
    block = min(BLOCK, length)
    blocks = length // block
    width = heads * HEAD_DIM
    for h in range(heads):
        qcol = pl.ds(h * HEAD_DIM, HEAD_DIM)
        kcol = pl.ds(width + h * HEAD_DIM, HEAD_DIM)
        vcol = pl.ds(2 * width + h * HEAD_DIM, HEAD_DIM)

        def prepare(i, carry):
            rows = pl.ds(pl.multiple_of(i * block, block), block)
            at = i * block + lax.broadcasted_iota(jnp.int32, (block, 1), 0)
            limit = jnp.where(at < split, limit_ref[row, 0], limit_ref[row, 1])
            active = (limit_ref[row, 2] + h < limit).astype(f32)
            datt = dat_ref[rows, qcol].astype(f32) * active
            datt_ref[rows, :] = datt.astype(bf16)
            delta = jnp.sum(datt * att_ref[rows, qcol], axis=1, keepdims=True)
            delta_ref[rows, :] = jnp.broadcast_to(delta, (block, HEAD_DIM))
            dq_ref[rows, :] = jnp.zeros((block, HEAD_DIM), f32)
            return carry

        lax.fori_loop(0, blocks, prepare, 0)

        def key_block(j, carry):
            keys = pl.ds(pl.multiple_of(j * block, block), block)
            k = qkv_ref[keys, kcol]
            v = qkv_ref[keys, vcol]
            kat = j * block + lax.broadcasted_iota(jnp.int32, (block, block), 1)

            def query_block(i, state):
                dk, dv = state
                rows = pl.ds(pl.multiple_of(i * block, block), block)
                q = qkv_ref[rows, qcol]
                datt = datt_ref[rows, :]
                at = i * block + lax.broadcasted_iota(jnp.int32, (block, 1), 0)
                low = first_key(split, at)
                ok = (kat <= at) & (kat >= low)
                s = dot(q, k, ((1,), (1,))) * scale
                lse = lse_ref[rows, qcol][:, :1]
                p = jnp.where(ok, jnp.exp(s - lse), 0.0)
                dp = dot(datt, v, ((1,), (1,)))
                ds = (p * (dp - delta_ref[rows, :][:, :1])).astype(bf16)
                dv = dv + dot(p.astype(bf16), datt, ((0,), (0,)))
                dk = dk + dot(ds, q, ((0,), (0,)))
                dq_ref[rows, :] += dot(ds, k, ((1,), (0,)))
                return dk, dv

            stop = jnp.where((j + 1) * block <= split, (split - 1) // block + 1, blocks)
            zero = jnp.zeros((block, HEAD_DIM), f32)
            dk, dv = lax.fori_loop(j, stop, query_block, (zero, zero))
            dproj_ref[keys, kcol] = turn(dk * scale, cos_ref[keys, :], -sin_ref[keys, :]).astype(bf16)
            dproj_ref[keys, vcol] = dv.astype(bf16)
            return carry

        lax.fori_loop(0, blocks, key_block, 0)

        def finish(i, carry):
            rows = pl.ds(pl.multiple_of(i * block, block), block)
            dq = dq_ref[rows, :] * scale
            dproj_ref[rows, qcol] = turn(dq, cos_ref[rows, :], -sin_ref[rows, :]).astype(bf16)
            return carry

        lax.fori_loop(0, blocks, finish, 0)


def attend_back(qkv, att, lse, dat, split, limits, cos2, sin2, heads):
    rows, length, _ = qkv.shape
    width = heads * HEAD_DIM
    smem = pl.BlockSpec(memory_space=pltpu.SMEM)
    table = pl.BlockSpec((length, HEAD_DIM), lambda r: (0, 0))

    def whole(cols):
        return pl.BlockSpec((None, length, cols), lambda r: (r, 0, 0))

    flops = rows * heads * 10 * length * length * HEAD_DIM
    return pl.pallas_call(
        functools.partial(attend_back_kernel, heads, length),
        grid=(rows,),
        in_specs=[smem, smem, whole(3 * width), whole(width), whole(width), whole(width), table, table],
        out_specs=whole(3 * width),
        out_shape=jax.ShapeDtypeStruct((rows, length, 3 * width), bf16),
        scratch_shapes=[
            pltpu.VMEM((length, HEAD_DIM), bf16),
            pltpu.VMEM((length, HEAD_DIM), f32),
            pltpu.VMEM((length, HEAD_DIM), f32),
        ],
        compiler_params=pltpu.CompilerParams(vmem_limit_bytes=56 * 2**20),
        cost_estimate=pl.CostEstimate(flops=flops, bytes_accessed=2**24, transcendentals=flops // 1280),
    )(split, limits, qkv, att, lse, dat, cos2, sin2)


class Ring:
    def __init__(self, axis, size):
        self.axis = axis
        self.size = size
        self.order = list(range(0, size, 2)) + list(range(1, size, 2))[::-1]
        place = {w: p for p, w in enumerate(self.order)}
        self.right = [(w, self.order[(place[w] + 1) % size]) for w in range(size)]
        self.left = [(w, self.order[(place[w] - 1) % size]) for w in range(size)]
        self.places = [place[w] for w in range(size)]

    def at(self, shift):
        here = jnp.array(self.places, jnp.int32)[lax.axis_index(self.axis)]
        return jnp.array(self.order, jnp.int32)[(here + shift) % self.size]

    def gather(self, part):
        found = [(self.at(0), part)]
        onward, back = part, part
        half = self.size // 2
        for step in range(1, half):
            onward = lax.ppermute(onward, self.axis, self.right)
            back = lax.ppermute(back, self.axis, self.left)
            found += [(self.at(-step), onward), (self.at(step), back)]
        cut = part.shape[0] // 2
        first = lax.ppermute(onward[:cut], self.axis, self.right)
        second = lax.ppermute(back[cut:], self.axis, self.left)
        found.append((self.at(half), jnp.concatenate([first, second], axis=0)))
        return found

    def gather_rows(self, part):
        rows = part.shape[0]
        whole = jnp.zeros((self.size * rows,) + part.shape[1:], part.dtype)
        for owner, piece in self.gather(part):
            whole = lax.dynamic_update_slice_in_dim(whole, piece, owner * rows, 0)
        return whole

    def scatter(self, term):
        sums = [term(self.at(-1), 0), term(self.at(1), 1)]
        for step in range(2, self.size + 1):
            for side, perm, sign in ((0, self.right, -1), (1, self.left, 1)):
                come = lax.ppermute(sums[side].astype(bf16), self.axis, perm)
                sums[side] = come.astype(f32) + term(self.at(sign * step), side)
        return sums


def swap(array, axis, size, bits):
    return lax.ppermute(array, axis, [(i, i ^ bits) for i in range(size)])


def on_device(
    wide,
    narrow,
    tokens,
    gain_one,
    w_qkv,
    w_out,
    gain_two,
    bias_two,
    router,
    w_up,
    w_down,
    doc_split,
    head_count,
    width_choice,
    out_grad,
):
    rows, part_len, dim = tokens.shape
    length = part_len * wide
    heads = dim // HEAD_DIM
    hidden = w_up.shape[1]
    head_groups = wide if heads % wide == 0 else heads
    row_groups = wide // head_groups
    my_heads = heads // head_groups
    my_rows = rows // row_groups
    cols = my_heads * HEAD_DIM
    count = rows * part_len
    w_at = lax.axis_index("wide")
    n_at = lax.axis_index("narrow")
    head_at = w_at % head_groups
    row_at = (w_at // head_groups) * my_rows
    ring = Ring("wide", wide)
    slots = (0, 2, 1, 3)

    def pick_rows(array):
        return lax.dynamic_slice_in_dim(array, row_at, my_rows, 0) if row_groups > 1 else array

    def put_rows(array):
        if row_groups == 1:
            return array
        whole = jnp.zeros((rows,) + array.shape[1:], array.dtype)
        return lax.dynamic_update_slice_in_dim(whole, array, row_at, 0)

    def narrow_gather(part):
        other = swap(part, "narrow", narrow, 2)
        both = jnp.stack([part, other])
        return jnp.concatenate([both, swap(both, "narrow", narrow, 1)])

    def narrow_scatter(terms):
        come = swap(terms[2:].astype(bf16), "narrow", narrow, 1)
        pair = terms[:2] + come.astype(f32)
        return pair[0] + swap(pair[1].astype(bf16), "narrow", narrow, 2).astype(f32)

    def in_order(parts):
        whole = jnp.zeros(parts.shape, parts.dtype)
        for place, slot in enumerate(slots):
            whole = lax.dynamic_update_slice_in_dim(whole, parts[place : place + 1], n_at ^ slot, 0)
        return whole

    def out_of_order(whole):
        return jnp.concatenate([lax.dynamic_slice_in_dim(whole, n_at ^ slot, 1, 0) for slot in slots])

    def narrow_all_to_all(blocks):
        return lax.all_to_all(blocks, "narrow", 0, 0, tiled=True)

    exponent = jnp.arange(HEAD_DIM // 2, dtype=f32) * (2.0 / HEAD_DIM)
    angles = jnp.arange(length, dtype=f32)[:, None] * jnp.power(rope_base, -exponent)[None, :]
    cosine, sine = jnp.cos(angles), jnp.sin(angles)
    cos2 = jnp.concatenate([cosine, cosine], axis=1)
    sin2 = jnp.concatenate([-sine, sine], axis=1)
    split = pick_rows(doc_split)
    limits = jnp.concatenate(
        [pick_rows(head_count), jnp.full((my_rows, 1), head_at * my_heads, jnp.int32)], axis=1
    )

    inputs = tokens.astype(f32)
    inv_one = lax.rsqrt(jnp.mean(inputs * inputs, axis=-1, keepdims=True) + norm_eps)
    normed_one = inputs * inv_one
    act_one = (normed_one * gain_one).astype(bf16)

    shard = w_qkv.shape[0]
    blocks = w_qkv.reshape(shard, 3, head_groups, cols).transpose(2, 0, 1, 3)
    blocks = jnp.tile(blocks.reshape(head_groups, shard, 3 * cols), (row_groups, 1, 1))
    blocks = lax.all_to_all(blocks, "wide", 0, 0, tiled=True)
    my_qkv = in_order(narrow_gather(blocks)).transpose(1, 0, 2, 3).reshape(dim, 3 * cols)

    act_all = jnp.zeros((my_rows, length, dim), bf16)
    for owner, piece in ring.gather(act_one.transpose(1, 0, 2)):
        piece = pick_rows(piece.transpose(1, 0, 2))
        act_all = lax.dynamic_update_slice_in_dim(act_all, piece, owner * part_len, 1)
    act_flat = act_all.reshape(my_rows * length, dim)
    proj = dot(act_flat, my_qkv, ((1,), (0,))).reshape(my_rows, length, 3 * cols)
    qkv, att, att_part, lse = attend(proj, split, limits, cos2, sin2, my_heads)

    sends = att_part.reshape(my_rows, wide, part_len, cols).transpose(1, 0, 2, 3)
    come = lax.all_to_all(sends, "wide", 0, 0, tiled=True)
    come = come.reshape(row_groups, head_groups, my_rows, part_len, cols)
    att_low = come.transpose(0, 2, 3, 1, 4).reshape(count, dim)
    out_full = lax.all_gather(w_out, ("wide", "narrow"), axis=0, tiled=True)
    x_one = inputs.reshape(count, dim) + dot(att_low, out_full, ((1,), (0,)))

    center = x_one - jnp.mean(x_one, axis=-1, keepdims=True)
    inv_two = lax.rsqrt(jnp.mean(center * center, axis=-1, keepdims=True) + norm_eps)
    normed_two = center * inv_two
    ln_out = normed_two * gain_two + bias_two
    width_flat = width_choice.reshape(count)
    onehot = (width_flat[:, None] == jnp.arange(WIDTHS, dtype=jnp.int32)[None, :]).astype(f32)
    router_prob = jax.nn.softmax(jnp.dot(ln_out, router, precision=highest), axis=-1)
    chosen = jnp.sum(router_prob * onehot, axis=-1)
    act_two = ln_out.astype(bf16)
    grad_top = out_grad.reshape(count, dim).astype(f32)

    piece_rows = w_down.shape[0]
    up_blocks = w_up.reshape(shard, wide, narrow, piece_rows).transpose(2, 0, 1, 3)
    up_part = narrow_all_to_all(up_blocks.reshape(narrow, shard, wide * piece_rows))
    up_mine = ring.gather_rows(up_part.reshape(narrow * shard, wide * piece_rows))
    down_mine = ring.gather_rows(w_down)
    top_all = narrow_gather(out_grad.reshape(count, dim)).reshape(narrow * count, dim)
    facts = narrow_gather(jnp.stack([chosen, width_flat.astype(f32)]))
    chosen_all = facts[:, 0].reshape(narrow * count, 1)
    width_all = facts[:, 1].reshape(narrow * count, 1)
    act_many = narrow_gather(act_two).reshape(narrow * count, dim)
    units = (jnp.arange(wide, dtype=jnp.int32)[:, None] * narrow + n_at) * piece_rows
    units = (units + jnp.arange(piece_rows, dtype=jnp.int32)[None, :]).reshape(-1)
    need = (units // (hidden // WIDTHS)).astype(f32)
    mask = need[None, :] <= width_all

    pre = jnp.maximum(dot(act_many, up_mine, ((1,), (0,))), 0.0)
    pre = jnp.where(mask, pre, 0.0)
    hid = (pre * pre).astype(bf16)
    dmix = (top_all.astype(f32) * chosen_all).astype(bf16)
    mixed = dot(hid, down_mine, ((1,), (0,)))
    dhid = dot(dmix, down_mine, ((1,), (1,)))
    dpre = (dhid * 2.0 * pre).astype(bf16)
    dact = dot(dpre, up_mine, ((1,), (1,)))
    mixed = narrow_scatter(mixed.reshape(narrow, count, dim))
    grad_act_two = narrow_scatter(dact.reshape(narrow, count, dim))

    half = dim // 2

    def up_term(owner, side):
        rows_of = lax.dynamic_slice_in_dim(act_many, owner * (narrow * shard), narrow * shard, 1)
        wide_half = dpre.shape[1] // 2
        return dot(rows_of, dpre[:, side * wide_half : (side + 1) * wide_half], ((0,), (0,)))

    def down_term(owner, side):
        rows_of = lax.dynamic_slice_in_dim(hid, owner * piece_rows, piece_rows, 1)
        return dot(rows_of, dmix[:, side * half : (side + 1) * half], ((0,), (0,)))

    down_grad = jnp.concatenate(ring.scatter(down_term), axis=1)
    up_sum = jnp.concatenate(ring.scatter(up_term), axis=1).astype(bf16)
    up_sum = narrow_all_to_all(up_sum.reshape(narrow, shard, wide * piece_rows))
    up_grad = up_sum.reshape(narrow, shard, wide, piece_rows).transpose(1, 2, 0, 3)
    up_grad = up_grad.reshape(shard, hidden).astype(f32)

    block_out = (x_one + mixed * chosen[:, None]).astype(bf16)
    grad_prob = jnp.sum(grad_top * mixed, axis=-1)
    grad_logits = (grad_prob * chosen)[:, None] * (onehot - router_prob)
    grad_router = lax.dot_general(ln_out, grad_logits, (((0,), (0,)), ((), ())), precision=highest)
    grad_ln = grad_act_two + jnp.dot(grad_logits, router.T, precision=highest)
    grad_gain_two = jnp.sum(grad_ln * normed_two, axis=0)
    grad_bias_two = jnp.sum(grad_ln, axis=0)
    grad_normed = grad_ln * gain_two
    grad_x_one = grad_top + inv_two * (
        grad_normed
        - jnp.mean(grad_normed, axis=-1, keepdims=True)
        - normed_two * jnp.mean(grad_normed * normed_two, axis=-1, keepdims=True)
    )

    grad_branch = grad_x_one.astype(bf16)
    grad_att = dot(grad_branch, out_full, ((1,), (1,))).astype(bf16)
    sends = grad_att.reshape(row_groups, my_rows, part_len, head_groups, cols)
    sends = sends.transpose(0, 3, 1, 2, 4).reshape(wide, my_rows, part_len, cols)
    come = lax.all_to_all(sends, "wide", 0, 0, tiled=True)
    dat = come.transpose(1, 0, 2, 3).reshape(my_rows, length, cols)
    dproj = attend_back(qkv, att, lse, dat, split, limits, cos2, sin2, my_heads)
    grad_out = dot(att_low, grad_branch, ((0,), (0,))).astype(bf16)
    out_proj_grad = lax.psum_scatter(
        grad_out, ("wide", "narrow"), scatter_dimension=0, tiled=True
    ).astype(f32)

    def one_term(owner, side):
        rows_of = lax.dynamic_slice_in_dim(dproj, owner * part_len, part_len, 1)
        rows_of = rows_of.reshape(my_rows * part_len, 3 * cols)
        term = dot(rows_of, my_qkv[side * half : (side + 1) * half], ((1,), (1,)))
        return put_rows(term.reshape(my_rows, part_len, half)).reshape(count, half)

    grad_act_one = jnp.concatenate(ring.scatter(one_term), axis=1)

    grad_qkv = dot(act_flat, dproj.reshape(my_rows * length, 3 * cols), ((0,), (0,)))
    grad_qkv = grad_qkv.reshape(wide, narrow, shard, 3 * cols).transpose(1, 0, 2, 3)
    grad_qkv = narrow_scatter(out_of_order(grad_qkv)).astype(bf16)
    grad_qkv = lax.all_to_all(grad_qkv, "wide", 0, 0, tiled=True).astype(f32)
    grad_qkv = jnp.sum(grad_qkv.reshape(row_groups, head_groups, shard, 3, cols), axis=0)
    qkv_grad = grad_qkv.transpose(1, 2, 0, 3).reshape(shard, 3 * dim)

    normed_flat = normed_one.reshape(count, dim)
    grad_gain_one = jnp.sum(grad_act_one * normed_flat, axis=0)
    grad_scaled = grad_act_one * gain_one
    input_grad = grad_x_one + inv_one.reshape(count, 1) * (
        grad_scaled - normed_flat * jnp.mean(grad_scaled * normed_flat, axis=-1, keepdims=True)
    )
    router_grad, gain_one_grad, gain_two_grad, bias_two_grad, counts_all = lax.psum(
        (grad_router, grad_gain_one, grad_gain_two, grad_bias_two, jnp.sum(onehot, axis=0)),
        ("wide", "narrow"),
    )
    return (
        block_out.reshape(rows, part_len, dim),
        input_grad.reshape(rows, part_len, dim),
        qkv_grad,
        out_proj_grad,
        up_grad,
        down_grad,
        gain_one_grad,
        gain_two_grad,
        bias_two_grad,
        router_grad,
        counts_all.astype(jnp.int32),
    )


def solution(mesh):
    in_specs = (
        P("narrow", "wide", None),
        P(),
        P(("wide", "narrow"), None),
        P(("wide", "narrow"), None),
        P(),
        P(),
        P(),
        P(("wide", "narrow"), None),
        P(("wide", "narrow"), None),
        P("narrow"),
        P("narrow", None),
        P("narrow", "wide"),
        P("narrow", "wide", None),
    )
    out_specs = (
        P("narrow", "wide", None),
        P("narrow", "wide", None),
        P(("wide", "narrow"), None),
        P(("wide", "narrow"), None),
        P(("wide", "narrow"), None),
        P(("wide", "narrow"), None),
        P(),
        P(),
        P(),
        P(),
        P(),
    )
    step = functools.partial(on_device, mesh.shape["wide"], mesh.shape["narrow"])
    return jax.shard_map(step, mesh=mesh, in_specs=in_specs, out_specs=out_specs, check_vma=False)
```

time: 3250 us -> 917 us (0.28)
  waiting for transfers between devices: 2710 us -> 301 us
  matrix products: 316 us -> 168 us
  starting transfers between devices: 0.66 us -> 122 us
  local copies, waits for them, and re-layouts: 49.2 us -> 121 us
  Pallas kernels: 0 us -> 61.3 us
  blocking collectives: 105 us -> 44 us
    reduce_scatter x3 -> x0, waiting for transfers between devices: 1850 us -> none  [the longest x1 709 us: on_device(): lax.psum_scatter(grad_down, ('wide', 'narrow'), scatter_dimension=0, tile...]
    all_gather x8 -> x1, waiting for transfers between devices: 856 us -> 0.01 us  [on_device(): out_full = lax.all_gather(w_out, ('wide', 'narrow'), axis=0, tiled=True)]
    ppermute x0 -> x80, waiting for transfers between devices: none -> 289 us  [the longest x42 141 us: scatter(): come = lax.ppermute(sums[side].astype(bf16), self.axis, perm)]
    dot_general x21 -> x60, matrix products: 316 us -> 168 us  [the longest x57 161 us: dot(): lax.dot_general(a, b, (contract, ((), ())), preferred_element_type=f32)]
    ppermute x0 -> x80, starting transfers between devices: none -> 90.7 us  [the longest x42 55.1 us: scatter(): come = lax.ppermute(sums[side].astype(bf16), self.axis, perm)]
    dynamic_update_slice x0 -> x26, local copies, waits for them, and re-layouts: none -> 62.7 us  [the longest x14 30.5 us: gather_rows(): whole = lax.dynamic_update_slice_in_dim(whole, piece, owner * rows, 0)]
    pallas_call x0 -> x2, Pallas kernels: none -> 61.3 us  [the longest x1 33.6 us: attend_back(): pl.pallas_call(functools.partial(attend_back_kernel, heads, length), grid...]
    all_gather x2 -> x0, blocking collectives: 59.7 us -> none  [the longest x1 30 us: on_device(): lax.all_gather(delta.astype(jnp.bfloat16), 'wide', axis=1, tiled=True)]
  transfers between devices with their start and end apart: 12 -> 88, of which waited for: 11 -> 35; matrix products, arithmetic and copies ran while one was open for 11% -> 30% of each run, Pallas kernels for 0% -> 7%
where the time goes in v1:
time: 917 us; the launch traced here: 903 us
  waiting for transfers between devices  301 us (33%)
  matrix products  168 us (18%)
  starting transfers between devices  122 us (13%)
  local copies, waits for them, and re-layouts  121 us (13%)
  Pallas kernels  61.3 us (7%)
  other arithmetic  46.9 us (5%)
  blocking collectives  44 us (5%)
  between operations  39.3 us (4%)
    dot_general x57, matrix products, dot(): lax.dot_general(a, b, (contract, ((), ())), preferred_element_type=f32)  161 us
    ppermute x42, waiting for transfers between devices, scatter(): come = lax.ppermute(sums[side].astype(bf16), self.axis, perm)  141 us
    ppermute x42, starting transfers between devices, scatter(): come = lax.ppermute(sums[side].astype(bf16), self.axis, perm)  55.1 us
    ppermute x9, waiting for transfers between devices, gather(): back = lax.ppermute(back, self.axis, self.left)  50.3 us
    ppermute x14, waiting for transfers between devices, swap(): return lax.ppermute(array, axis, [(i, i ^ bits) for i in range(size)])  44.6 us
    psum x1, blocking collectives, on_device(): lax.psum((grad_router, grad_gain_one, grad_gain_two, grad_bias_two, jnp.s...  44 us
    ppermute x3, waiting for transfers between devices, gather(): second = lax.ppermute(back[cut:], self.axis, self.left)  34 us
    pallas_call x1, Pallas kernels, attend_back(): pl.pallas_call(functools.partial(attend_back_kernel, heads, length), grid...  33.6 us
  transfers between devices with their start and end apart: 88, of which 35 were waited for; matrix products, arithmetic and copies ran while one was open for 30% of the time, Pallas kernels for 7%

profile of v1, /device:TPU:8, one launch (start us, length us, event | category | flops | bytes accessed | tf_op | source)
XLA Modules:
  0.0 902.8 jit_solution(1516445504418947766)
XLA Ops:
  78.4 6.0 all-to-all-start
  104.2 11.1 %all-to-all-done = bf16[8,64,768]{2,1,0:T(8,128)(2,1)S(1)} async-done(((bf16[8,64,768]{2,1,0:T(8,128)(2,1)}), bf16[8,64,768]{2,1,0:T(8,128)(2,1)S(1)}, u32[]{:S(2)}, u32[]{:S(2)}) %all-to-all-start) | async-done | bytes 786464 | tf_op jit(solution)/shard_map/all_to_all | solution.py:352
  118.4 19.4 %collective-permute-done.14 = bf16[256,2048]{1,0:T(8,128)(2,1)} collective-permute-done((bf16[256,2048]{1,0:T(8,128)(2,1)}, bf16[256,2048]{1,0:T(8,128)(2,1)}, u32[]{:S(2)}, u32[]{:S(2)}) %collective-permute-start.14) | collective-permute-done | bytes 1048608 | tf_op jit(solution)/shard_map/ppermute | solution.py:240
  146.5 14.6 %collective-permute-done.3 = bf16[256,1,2048]{2,0,1:T(8,128)(2,1)} collective-permute-done((bf16[256,1,2048]{2,0,1:T(8,128)(2,1)}, bf16[256,1,2048]{2,0,1:T(8,128)(2,1)}, u32[]{:S(2)}, u32[]{:S(2)}) %collective-permute-start.3) | collective-permute-done | bytes 1048608 | tf_op jit(solution)/shard_map/ppermute | solution.py:241
  170.1 35.7 %collective-permute-done.5 = bf16[256,1,2048]{2,0,1:T(8,128)(2,1)S(1)} collective-permute-done((bf16[256,1,2048]{2,0,1:T(8,128)(2,1)}, bf16[256,1,2048]{2,0,1:T(8,128)(2,1)S(1)}, u32[]{:S(2)}, u32[]{:S(2)}) %collective-permute-start.5) | collective-permute-done | bytes 1048608 | tf_op jit(solution)/shard_map/ppermute | solution.py:241
  210.1 12.3 %copy.202 = bf16[2048,2048]{0,1:T(8,128)(2,1)} copy(bf16[2048,2048]{1,0:T(8,128)(2,1)} %bitcast_dynamic-update-slice_fusion) | data formatting | bytes 16777216 | tf_op jit(solution)/shard_map/dynamic_update_slice | solution.py:358
  236.0 11.8 %convolution_bitcast_fusion.proj_ref = f32[1,2048,768]{2,1,0:T(8,128)} fusion(bf16[2048,2048]{0,1:T(8,128)(2,1)} %constant_dynamic-update-slice_fusion.14, bf16[2048,768]{1,0:T(8,128)(2,1)} %bitcast.35), kind=kOutput, calls=%fused_computation.12 | convolution fusion | flops 6442450944 | bytes 17825792 | tf_op jit(solution)/shard_map/dot_general | solution.py:23
  247.8 27.7 %shard_map.1508 = (bf16[1,2048,768]{2,1,0:T(8,128)(2,1)}, f32[1,2048,256]{2,1,0:T(8,128)}, bf16[1,2048,256]{2,1,0:T(8,128)(2,1)}, f32[1,2048,256]{2,1,0:T(8,128)}) custom-call(s32[1]{0:T(128)S(6)} %copy.260.split_ref, s32[1,3]{1,0:T(1,128)} %pad_add_fusion.limit_ref, f32[1,2048,768]{2,1,0:T(8,128)} %convolution_bitcast_fusion.proj_ref, ...), custom_call_target="tpu_custom_call" | custom-call | flops 4294967296 | bytes 16777216 | tf_op jit(solution)/shard_map/pallas_call | solution.py:111
  306.9 34.0 %collective-permute-done.29 = bf16[128,2048]{1,0:T(8,128)(2,1)S(1)} collective-permute-done((bf16[128,2048]{1,0:T(8,128)(2,1)S(1)}, bf16[128,2048]{1,0:T(8,128)(2,1)S(1)}, u32[]{:S(2)}, u32[]{:S(2)}) %collective-permute-start.29) | collective-permute-done | bytes 524320 | tf_op jit(solution)/shard_map/ppermute | solution.py:245
  343.0 6.2 fusion.333
  362.8 10.9 %collective-permute-done.12 = bf16[256,2048]{1,0:T(8,128)(2,1)S(1)} collective-permute-done((bf16[256,2048]{1,0:T(8,128)(2,1)S(1)}, bf16[256,2048]{1,0:T(8,128)(2,1)S(1)}, u32[]{:S(2)}, u32[]{:S(2)}) %collective-permute-start.12) | collective-permute-done | bytes 1048608 | tf_op jit(solution)/shard_map/ppermute | solution.py:266
  382.7 11.1 %multiply_convert_fusion.1 = (bf16[1024,2048]{1,0:T(8,128)(2,1)S(1)}, f32[1024,2048]{1,0:T(8,128)}) fusion(f32[2048]{0:T(1024)S(1)} %fusion.314, f32[1024]{0:T(1024)S(1)} %bitcast.398, bf16[1024,2048]{1,0:T(8,128)(2,1)S(1)} %bitcast.359, bf16[2048,2048]{1,0:T(8,128)(2,1)S(1)} %maximum_dynamic-update-slice_fusion), kind=kOutput, calls=%fused_computation.3 | convolution fusion | flops 8600420352 | bytes 25178112 | tf_op jit(solution)/shard_map/dot_general | solution.py:23
  396.7 12.5 %fusion.335 = f32[1024,2048]{1,0:T(8,128)S(1)} fusion(bf16[1024,2048]{1,0:T(8,128)(2,1)} %copy-done.35, bf16[2048,2048]{1,0:T(8,128)(2,1)} %maximum_dynamic-update-slice_fusion.1), kind=kOutput, calls=%fused_computation.397 | convolution fusion | flops 8589934592 | bytes 20971520 | tf_op jit(solution)/shard_map/dot_general | solution.py:23
  409.2 18.1 %multiply_convert_fusion = bf16[1024,2048]{1,0:T(8,128)(2,1)} fusion(f32[1024,2048]{1,0:T(8,128)} %get-tuple-element.70, bf16[1024,2048]{1,0:T(8,128)(2,1)S(1)} %fusion, bf16[2048,2048]{1,0:T(8,128)(2,1)} %maximum_dynamic-update-slice_fusion.1, f32[2048]{0:T(1024)S(1)} %fusion.314, f32[1024]{0:T(1024)S(1)} %bitcast.399), kind=kOutput, calls=%fused_computation.2 | convolution fusion | flops 8602517504 | bytes 25178112 | tf_op jit(solution)/shard_map/dot_general | solution.py:23
  427.3 12.8 %fusion.336 = f32[1024,2048]{1,0:T(8,128)S(1)} fusion(bf16[1024,2048]{1,0:T(8,128)(2,1)} %multiply_convert_fusion, bf16[2048,2048]{1,0:T(8,128)(2,1)} %copy-done.26), kind=kOutput, calls=%fused_computation.398 | convolution fusion | flops 8589934592 | bytes 20971520 | tf_op jit(solution)/shard_map/dot_general | solution.py:23
  451.4 7.7 collective-permute-done.66
  461.9 8.5 collective-permute-done.52
  474.0 7.6 collective-permute-done.67
  485.2 7.6 collective-permute-done.53
  510.0 14.1 %collective-permute-done.31 = bf16[256,2048]{1,0:T(8,128)(2,1)S(1)} collective-permute-done((bf16[256,2048]{1,0:T(8,128)(2,1)S(1)}, bf16[256,2048]{1,0:T(8,128)(2,1)S(1)}, u32[]{:S(2)}, u32[]{:S(2)}) %collective-permute-start.31) | collective-permute-done | bytes 1048608 | tf_op jit(solution)/shard_map/ppermute | solution.py:266
  525.6 17.9 %collective-permute-done.35 = bf16[256,2048]{1,0:T(8,128)(2,1)S(1)} collective-permute-done((bf16[256,2048]{1,0:T(8,128)(2,1)S(1)}, bf16[256,2048]{1,0:T(8,128)(2,1)S(1)}, u32[]{:S(2)}, u32[]{:S(2)}) %collective-permute-start.35) | collective-permute-done | bytes 1048608 | tf_op jit(solution)/shard_map/ppermute | solution.py:266
  568.4 6.6 collective-permute-done.55
  582.5 7.7 collective-permute-done.70
  631.4 9.7 %collective-permute-done.57 = bf16[256,1024]{1,0:T(8,128)(2,1)} collective-permute-done((bf16[256,1024]{1,0:T(8,128)(2,1)}, bf16[256,1024]{1,0:T(8,128)(2,1)}, u32[]{:S(2)}, u32[]{:S(2)}) %collective-permute-start.57) | collective-permute-done | bytes 524320 | tf_op jit(solution)/shard_map/ppermute | solution.py:260
  660.5 31.2 %collective-permute-done.58 = bf16[256,1024]{1,0:T(8,128)(2,1)S(1)} collective-permute-done((bf16[256,1024]{1,0:T(8,128)(2,1)S(1)}, bf16[256,1024]{1,0:T(8,128)(2,1)S(1)}, u32[]{:S(2)}, u32[]{:S(2)}) %collective-permute-start.58) | collective-permute-done | bytes 524320 | tf_op jit(solution)/shard_map/ppermute | solution.py:260
  701.4 33.6 %shard_map.1509 = bf16[1,2048,768]{2,1,0:T(8,128)(2,1)} custom-call(s32[1]{0:T(128)S(6)} %copy.260.split_ref, s32[1,3]{1,0:T(1,128)} %pad_add_fusion.limit_ref, bf16[1,2048,768]{2,1,0:T(8,128)(2,1)} %get-tuple-element.16.qkv_ref, f32[1,2048,256]{2,1,0:T(8,128)} %get-tuple-element.17.att_ref, f32[1,2048,256]{2,1,0:T(8,128)} %get-tuple-element.18.lse_ref, ...), custom_call_target="tpu_custom_call" | custom-call | flops 10737418240 | bytes 16777216 | tf_op jit(solution)/shard_map/pallas_call | solution.py:205
  741.0 9.1 %fusion.1 = f32[8,4,64,768]{3,2,1,0:T(8,128)S(1)} fusion(bf16[8,4,64,2048]{3,2,1,0:T(8,128)(2,1)} %bitcast.353, bf16[1,2048,768]{2,1,0:T(8,128)(2,1)S(1)} %copy-done.19), kind=kOutput, calls=%fused_computation.14 | convolution fusion | flops 6442450944 | bytes 17825792 | tf_op jit(solution)/shard_map/dot_general | solution.py:23
  756.4 8.9 collective-permute-done.37
  772.8 5.8 collective-permute-done.38
  784.3 7.1 collective-permute-done.39
  797.5 6.0 collective-permute-done.40
  840.2 44.0 %all-reduce = (f32[2048]{0:T(1024)}, f32[2048]{0:T(1024)}, f32[2048]{0:T(1024)}, f32[2048,4]{0,1:T(4,128)}, f32[4]{0:T(128)S(1)}) all-reduce(f32[2048]{0:T(1024)S(1)} %get-tuple-element.21, f32[2048]{0:T(1024)S(1)} %get-tuple-element.19, f32[2048]{0:T(1024)S(1)} %get-tuple-element.24, ...), channel_id=1, replica_groups=mesh['wide'=8,'narrow'=4] {'wide','narrow'}, use_global_device_ids=true, to_apply=%region_12.13 | all-reduce | flops 14340 | bytes 114720 | tf_op jit(solution)/shard_map/psum | solution.py:471
  (430 shorter events, 386.2 us)
Async XLA Ops:
  7.2 334.8 %all-gather.2.cloned.1.call-start = ((), (), s32[]{:S(2)}) async-start(), calls=%async_computation.7 | async-start | bytes 8650752 | tf_op jit(solution)/shard_map/all_gather | solution.py:367
  12.0 78.5 %collective-permute-start.1 = (bf16[256,1,2048]{2,0,1:T(8,128)(2,1)}, bf16[256,1,2048]{2,0,1:T(8,128)(2,1)}, u32[]{:S(2)}, u32[]{:S(2)}) collective-permute-start(bf16[256,1,2048]{2,0,1:T(8,128)(2,1)} %fusion.264), channel_id=1, source_target_pairs={{0,4},{4,12},{8,0},{12,20},{16,8},{20,28},{24,16},{28,24},{1,5},{5... | collective-permute-start | bytes 3145736 | tf_op jit(solution)/shard_map/ppermute | solution.py:241
  12.0 74.8 %collective-permute-start = (bf16[256,1,2048]{2,0,1:T(8,128)(2,1)}, bf16[256,1,2048]{2,0,1:T(8,128)(2,1)}, u32[]{:S(2)}, u32[]{:S(2)}) collective-permute-start(bf16[256,1,2048]{2,0,1:T(8,128)(2,1)} %fusion.264), channel_id=1, source_target_pairs={{0,8},{4,0},{8,16},{12,4},{16,24},{20,12},{24,28},{28,20},{1,9},{5... | collective-permute-start | bytes 3145736 | tf_op jit(solution)/shard_map/ppermute | solution.py:240
  14.0 83.1 %collective-permute-start.23 = (bf16[256,2048]{1,0:T(8,128)(2,1)}, bf16[256,2048]{1,0:T(8,128)(2,1)}, u32[]{:S(2)}, u32[]{:S(2)}) collective-permute-start(bf16[256,2048]{1,0:T(8,128)(2,1)} %param.165), channel_id=1, source_target_pairs={{0,4},{4,12},{8,0},{12,20},{16,8},{20,28},{24,16},{28,24},{1,5},{5... | collective-permute-start | bytes 3145736 | tf_op jit(solution)/shard_map/ppermute | solution.py:241
  14.0 80.3 %collective-permute-start.22 = (bf16[256,2048]{1,0:T(8,128)(2,1)}, bf16[256,2048]{1,0:T(8,128)(2,1)}, u32[]{:S(2)}, u32[]{:S(2)}) collective-permute-start(bf16[256,2048]{1,0:T(8,128)(2,1)} %param.165), channel_id=1, source_target_pairs={{0,8},{4,0},{8,16},{12,4},{16,24},{20,12},{24,28},{28,20},{1,9},{5... | collective-permute-start | bytes 3145736 | tf_op jit(solution)/shard_map/ppermute | solution.py:240
  18.3 60.1 %all-to-all-start.2 = ((bf16[4,64,2048]{2,1,0:T(8,128)(2,1)}), bf16[4,64,2048]{2,1,0:T(8,128)(2,1)}, u32[]{:S(2)}, u32[]{:S(2)}) async-start(bf16[4,64,2048]{2,1,0:T(8,128)(2,1)} %reshape.614), calls=%async_computation.2 | async-start | bytes 2097152 | tf_op jit(solution)/shard_map/all_to_all | solution.py:332
  22.6 78.4 %collective-permute-start.32 = (bf16[256,2048]{1,0:T(8,128)(2,1)S(1)}, bf16[256,2048]{1,0:T(8,128)(2,1)}, u32[]{:S(2)}, u32[]{:S(2)}) collective-permute-start(bf16[256,2048]{1,0:T(8,128)(2,1)S(1)} %bitcast.347), channel_id=1, source_target_pairs={{0,2},{1,3},{2,0},{3,1},{4,6},{5,7},{6,4},{7,5},{8,10},{9,11},{10,... | collective-permute-start | bytes 3145736 | tf_op jit(solution)/shard_map/ppermute | solution.py:266
  86.8 55.7 %collective-permute-start.15 = (bf16[256,2048]{1,0:T(8,128)(2,1)}, bf16[256,2048]{1,0:T(8,128)(2,1)}, u32[]{:S(2)}, u32[]{:S(2)}) collective-permute-start(bf16[256,2048]{1,0:T(8,128)(2,1)} %bitcast.50), channel_id=1, source_target_pairs={{0,4},{4,12},{8,0},{12,20},{16,8},{20,28},{24,16},{28,24},{1,5},{5... | collective-permute-start | bytes 3145736 | tf_op jit(solution)/shard_map/ppermute | solution.py:241
  94.4 66.7 %collective-permute-start.3 = (bf16[256,1,2048]{2,0,1:T(8,128)(2,1)}, bf16[256,1,2048]{2,0,1:T(8,128)(2,1)}, u32[]{:S(2)}, u32[]{:S(2)}) collective-permute-start(bf16[256,1,2048]{2,0,1:T(8,128)(2,1)} %collective-permute-done.1), channel_id=1, source_target_pairs={{0,4},{4,12},{8,0},{12,20},{16,8},{20,28},{24,16},{28,24},{1,5},{5... | collective-permute-start | bytes 3145736 | tf_op jit(solution)/shard_map/ppermute | solution.py:241
  97.1 63.9 %collective-permute-start.2 = (bf16[256,1,2048]{2,0,1:T(8,128)(2,1)}, bf16[256,1,2048]{2,0,1:T(8,128)(2,1)}, u32[]{:S(2)}, u32[]{:S(2)}) collective-permute-start(bf16[256,1,2048]{2,0,1:T(8,128)(2,1)} %collective-permute-done), channel_id=1, source_target_pairs={{0,8},{4,0},{8,16},{12,4},{16,24},{20,12},{24,28},{28,20},{1,9},{5... | collective-permute-start | bytes 3145736 | tf_op jit(solution)/shard_map/ppermute | solution.py:240
  101.0 126.8 %collective-permute-start.25 = (bf16[256,2048]{1,0:T(8,128)(2,1)}, bf16[256,2048]{1,0:T(8,128)(2,1)}, u32[]{:S(2)}, u32[]{:S(2)}) collective-permute-start(bf16[256,2048]{1,0:T(8,128)(2,1)} %collective-permute-done.23), channel_id=1, source_target_pairs={{0,4},{4,12},{8,0},{12,20},{16,8},{20,28},{24,16},{28,24},{1,5},{5... | collective-permute-start | bytes 3145736 | tf_op jit(solution)/shard_map/ppermute | solution.py:241
  137.8 92.1 %collective-permute-start.24 = (bf16[256,2048]{1,0:T(8,128)(2,1)}, bf16[256,2048]{1,0:T(8,128)(2,1)}, u32[]{:S(2)}, u32[]{:S(2)}) collective-permute-start(bf16[256,2048]{1,0:T(8,128)(2,1)} %collective-permute-done.22), channel_id=1, source_target_pairs={{0,8},{4,0},{8,16},{12,4},{16,24},{20,12},{24,28},{28,20},{1,9},{5... | collective-permute-start | bytes 3145736 | tf_op jit(solution)/shard_map/ppermute | solution.py:240
  169.1 60.8 %collective-permute-start.9 = (bf16[2,8,64,768]{3,2,1,0:T(8,128)(2,1)}, bf16[2,8,64,768]{3,2,1,0:T(8,128)(2,1)}, u32[]{:S(2)}, u32[]{:S(2)}) collective-permute-start(bf16[2,8,64,768]{3,2,1,0:T(8,128)(2,1)} %pad_maximum_fusion.6), channel_id=1, source_target_pairs={{0,1},{1,0},{2,3},{3,2},{4,5},{5,4},{6,7},{7,6},{8,9},{9,8},{10,11... | collective-permute-start | bytes 4718600 | tf_op jit(solution)/shard_map/ppermute | solution.py:266
  222.4 81.0 %collective-permute-start.33 = (bf16[2,256,2048]{2,1,0:T(8,128)(2,1)}, bf16[2,256,2048]{2,1,0:T(8,128)(2,1)}, u32[]{:S(2)}, u32[]{:S(2)}) collective-permute-start(bf16[2,256,2048]{2,1,0:T(8,128)(2,1)} %pad_maximum_fusion.3), channel_id=1, source_target_pairs={{0,1},{1,0},{2,3},{3,2},{4,5},{5,4},{6,7},{7,6},{8,9},{9,8},{10,11... | collective-permute-start | bytes 6291464 | tf_op jit(solution)/shard_map/ppermute | solution.py:266
  222.4 65.2 %collective-permute-start.17 = (bf16[256,2048]{1,0:T(8,128)(2,1)}, bf16[256,2048]{1,0:T(8,128)(2,1)}, u32[]{:S(2)}, u32[]{:S(2)}) collective-permute-start(bf16[256,2048]{1,0:T(8,128)(2,1)} %collective-permute-done.15), channel_id=1, source_target_pairs={{0,4},{4,12},{8,0},{12,20},{16,8},{20,28},{24,16},{28,24},{1,5},{5... | collective-permute-start | bytes 3145736 | tf_op jit(solution)/shard_map/ppermute | solution.py:241
  227.9 59.9 %collective-permute-start.16 = (bf16[256,2048]{1,0:T(8,128)(2,1)}, bf16[256,2048]{1,0:T(8,128)(2,1)}, u32[]{:S(2)}, u32[]{:S(2)}) collective-permute-start(bf16[256,2048]{1,0:T(8,128)(2,1)} %collective-permute-done.14), channel_id=1, source_target_pairs={{0,8},{4,0},{8,16},{12,4},{16,24},{20,12},{24,28},{28,20},{1,9},{5... | collective-permute-start | bytes 3145736 | tf_op jit(solution)/shard_map/ppermute | solution.py:240
  229.9 64.5 %collective-permute-start.27 = (bf16[256,2048]{1,0:T(8,128)(2,1)}, bf16[256,2048]{1,0:T(8,128)(2,1)}, u32[]{:S(2)}, u32[]{:S(2)}) collective-permute-start(bf16[256,2048]{1,0:T(8,128)(2,1)} %collective-permute-done.25), channel_id=1, source_target_pairs={{0,4},{4,12},{8,0},{12,20},{16,8},{20,28},{24,16},{28,24},{1,5},{5... | collective-permute-start | bytes 3145736 | tf_op jit(solution)/shard_map/ppermute | solution.py:241
  229.9 65.7 %collective-permute-start.26 = (bf16[256,2048]{1,0:T(8,128)(2,1)}, bf16[256,2048]{1,0:T(8,128)(2,1)}, u32[]{:S(2)}, u32[]{:S(2)}) collective-permute-start(bf16[256,2048]{1,0:T(8,128)(2,1)} %collective-permute-done.24), channel_id=1, source_target_pairs={{0,8},{4,0},{8,16},{12,4},{16,24},{20,12},{24,28},{28,20},{1,9},{5... | collective-permute-start | bytes 3145736 | tf_op jit(solution)/shard_map/ppermute | solution.py:240
  277.8 64.2 %all-to-all-start.1 = ((bf16[8,1,256,256]{2,3,1,0:T(8,128)(2,1)}), bf16[8,1,256,256]{2,3,1,0:T(8,128)(2,1)S(1)}, u32[]{:S(2)}, u32[]{:S(2)}) async-start(bf16[8,1,256,256]{2,3,1,0:T(8,128)(2,1)} %copy.210), calls=%async_computation.1 | async-start | bytes 2097152 | tf_op jit(solution)/shard_map/all_to_all | solution.py:364
  283.0 611.0 %reduce-scatter.2.cloned.1.call-start = ((), (), s32[]{:S(2)}) async-start(), calls=%async_computation.8 | async-start | bytes 8650752 | tf_op jit(solution)/shard_map/reduce_scatter | solution.py:446
  287.7 67.9 %collective-permute-start.19 = (bf16[256,2048]{1,0:T(8,128)(2,1)}, bf16[256,2048]{1,0:T(8,128)(2,1)}, u32[]{:S(2)}, u32[]{:S(2)}) collective-permute-start(bf16[256,2048]{1,0:T(8,128)(2,1)} %collective-permute-done.17), channel_id=1, source_target_pairs={{0,4},{4,12},{8,0},{12,20},{16,8},{20,28},{24,16},{28,24},{1,5},{5... | collective-permute-start | bytes 3145736 | tf_op jit(solution)/shard_map/ppermute | solution.py:241
  287.8 68.9 %collective-permute-start.18 = (bf16[256,2048]{1,0:T(8,128)(2,1)}, bf16[256,2048]{1,0:T(8,128)(2,1)}, u32[]{:S(2)}, u32[]{:S(2)}) collective-permute-start(bf16[256,2048]{1,0:T(8,128)(2,1)} %collective-permute-done.16), channel_id=1, source_target_pairs={{0,8},{4,0},{8,16},{12,4},{16,24},{20,12},{24,28},{28,20},{1,9},{5... | collective-permute-start | bytes 3145736 | tf_op jit(solution)/shard_map/ppermute | solution.py:240
  494.4 59.9 %collective-permute-start.54 = (bf16[256,1024]{1,0:T(8,128)(2,1)}, bf16[256,1024]{1,0:T(8,128)(2,1)}, u32[]{:S(2)}, u32[]{:S(2)}) collective-permute-start(bf16[256,1024]{1,0:T(8,128)(2,1)} %add_convert_fusion.25), channel_id=1, source_target_pairs={{0,8},{4,0},{8,16},{12,4},{16,24},{20,12},{24,28},{28,20},{1,9},{5... | collective-permute-start | bytes 1572872 | tf_op jit(solution)/shard_map/ppermute | solution.py:260
  504.8 53.5 %collective-permute-start.61 = (bf16[256,1024]{1,0:T(8,128)(2,1)}, bf16[256,1024]{1,0:T(8,128)(2,1)}, u32[]{:S(2)}, u32[]{:S(2)}) collective-permute-start(bf16[256,1024]{1,0:T(8,128)(2,1)} %add_convert_fusion.18), channel_id=1, source_target_pairs={{0,4},{4,12},{8,0},{12,20},{16,8},{20,28},{24,16},{28,24},{1,5},{5... | collective-permute-start | bytes 1572872 | tf_op jit(solution)/shard_map/ppermute | solution.py:260
  506.4 55.6 %collective-permute-start.69 = (bf16[256,1024]{1,0:T(8,128)(2,1)}, bf16[256,1024]{1,0:T(8,128)(2,1)}, u32[]{:S(2)}, u32[]{:S(2)}) collective-permute-start(bf16[256,1024]{1,0:T(8,128)(2,1)} %add_convert_fusion.10), channel_id=1, source_target_pairs={{0,8},{4,0},{8,16},{12,4},{16,24},{20,12},{24,28},{28,20},{1,9},{5... | collective-permute-start | bytes 1572872 | tf_op jit(solution)/shard_map/ppermute | solution.py:260
  600.0 55.6 %collective-permute-start.78 = (bf16[256,1024]{1,0:T(8,128)(2,1)}, bf16[256,1024]{1,0:T(8,128)(2,1)}, u32[]{:S(2)}, u32[]{:S(2)}) collective-permute-start(bf16[256,1024]{1,0:T(8,128)(2,1)} %add_convert_fusion.2), channel_id=1, source_target_pairs={{0,4},{4,12},{8,0},{12,20},{16,8},{20,28},{24,16},{28,24},{1,5},{5... | collective-permute-start | bytes 1572872 | tf_op jit(solution)/shard_map/ppermute | solution.py:260
  620.3 76.8 %all-to-all-start.3 = ((bf16[8,1,256,256]{3,2,1,0:T(8,128)(2,1)}), bf16[8,1,256,256]{3,2,1,0:T(8,128)(2,1)S(1)}, u32[]{:S(2)}, u32[]{:S(2)}) async-start(bf16[8,1,256,256]{3,2,1,0:T(8,128)(2,1)} %bitcast.326), calls=%async_computation.3 | async-start | bytes 2097152 | tf_op jit(solution)/shard_map/all_to_all | solution.py:442
  629.9 64.5 %collective-permute-start.72 = (bf16[256,1024]{1,0:T(8,128)(2,1)S(1)}, bf16[256,1024]{1,0:T(8,128)(2,1)S(1)}, u32[]{:S(2)}, u32[]{:S(2)}) collective-permute-start(bf16[256,1024]{1,0:T(8,128)(2,1)S(1)} %add_convert_fusion.7), channel_id=1, source_target_pairs={{0,8},{4,0},{8,16},{12,4},{16,24},{20,12},{24,28},{28,20},{1,9},{5... | collective-permute-start | bytes 1572872 | tf_op jit(solution)/shard_map/ppermute | solution.py:260
  643.5 48.2 %collective-permute-start.58 = (bf16[256,1024]{1,0:T(8,128)(2,1)S(1)}, bf16[256,1024]{1,0:T(8,128)(2,1)S(1)}, u32[]{:S(2)}, u32[]{:S(2)}) collective-permute-start(bf16[256,1024]{1,0:T(8,128)(2,1)S(1)} %add_convert_fusion.21), channel_id=1, source_target_pairs={{0,8},{4,0},{8,16},{12,4},{16,24},{20,12},{24,28},{28,20},{1,9},{5... | collective-permute-start | bytes 1572872 | tf_op jit(solution)/shard_map/ppermute | solution.py:260
  658.4 112.1 %collective-permute-start.79 = (bf16[256,1024]{1,0:T(8,128)(2,1)}, bf16[256,1024]{1,0:T(8,128)(2,1)}, u32[]{:S(2)}, u32[]{:S(2)}) collective-permute-start(bf16[256,1024]{1,0:T(8,128)(2,1)} %add_convert_fusion.1), channel_id=1, source_target_pairs={{0,4},{4,12},{8,0},{12,20},{16,8},{20,28},{24,16},{28,24},{1,5},{5... | collective-permute-start | bytes 1572872 | tf_op jit(solution)/shard_map/ppermute | solution.py:260
  697.1 112.8 %all-to-all-start.5 = ((bf16[4,64,2048]{2,1,0:T(8,128)(2,1)}), bf16[4,64,2048]{2,1,0:T(8,128)(2,1)}, u32[]{:S(2)}, u32[]{:S(2)}) async-start(bf16[4,64,2048]{2,1,0:T(8,128)(2,1)} %pad_maximum_fusion.10), calls=%async_computation.6 | async-start | bytes 2097152 | tf_op jit(solution)/shard_map/all_to_all | solution.py:332
  827.1 61.9 %all-to-all-start.4 = ((bf16[8,64,768]{2,1,0:T(8,128)(2,1)}), bf16[8,64,768]{2,1,0:T(8,128)(2,1)}, u32[]{:S(2)}, u32[]{:S(2)}) async-start(bf16[8,64,768]{2,1,0:T(8,128)(2,1)} %fusion.24), calls=%async_computation.4 | async-start | bytes 1572864 | tf_op jit(solution)/shard_map/all_to_all | solution.py:461
  (110 other events, 2494.9 us)
Sparse Core Ops, SparseCore 0:
  10.9 105.6 all-gather.1
  554.4 152.6 reduce-scatter.1

commit v2 on v1

--- a/solution.py
+++ b/solution.py
@@ -224,13 +224,16 @@
         self.size = size
         self.order = list(range(0, size, 2)) + list(range(1, size, 2))[::-1]
         place = {w: p for p, w in enumerate(self.order)}
+        self.table = [[self.order[(place[w] + k) % size] for k in range(size)] for w in range(size)]
+        self.near = None
         self.right = [(w, self.order[(place[w] + 1) % size]) for w in range(size)]
         self.left = [(w, self.order[(place[w] - 1) % size]) for w in range(size)]
-        self.places = [place[w] for w in range(size)]
 
     def at(self, shift):
-        here = jnp.array(self.places, jnp.int32)[lax.axis_index(self.axis)]
-        return jnp.array(self.order, jnp.int32)[(here + shift) % self.size]
+        if self.near is None:
+            row = lax.dynamic_slice_in_dim(jnp.array(self.table, jnp.int32), lax.axis_index(self.axis), 1, 0)
+            self.near = [row[0, k] for k in range(self.size)]
+        return self.near[shift % self.size]
 
     def gather(self, part):
         found = [(self.at(0), part)]
@@ -246,11 +249,10 @@
         found.append((self.at(half), jnp.concatenate([first, second], axis=0)))
         return found
 
-    def gather_rows(self, part):
-        rows = part.shape[0]
-        whole = jnp.zeros((self.size * rows,) + part.shape[1:], part.dtype)
+    def gather_whole(self, part):
+        whole = jnp.zeros((self.size,) + part.shape, part.dtype)
         for owner, piece in self.gather(part):
-            whole = lax.dynamic_update_slice_in_dim(whole, piece, owner * rows, 0)
+            whole = lax.dynamic_update_slice_in_dim(whole, piece[None], owner, 0)
         return whole
 
     def scatter(self, term):
@@ -260,6 +262,447 @@
                 come = lax.ppermute(sums[side].astype(bf16), self.axis, perm)
                 sums[side] = come.astype(f32) + term(self.at(sign * step), side)
         return sums
+
+
+def join(*arrays):
+    return lax.optimization_barrier(arrays)
+
+
+def after(array, *others):
+    return lax.optimization_barrier((array,) + others)[0]
+
+
+def place_kernel(count, targets, *refs):
+    pieces, whole, held, in_sems, out_sems = refs[:-4], refs[-4], refs[-3], refs[-2], refs[-1]
+    spots = [(i, k) for i in range(len(pieces)) for k in range(count)]
+    loads = [
+        pltpu.make_async_copy(pieces[i].at[k], held.at[at], in_sems.at[at]) for at, (i, k) in enumerate(spots)
+    ]
+    stores = [
+        pltpu.make_async_copy(held.at[at], whole.at[targets(i, k)], out_sems.at[at])
+        for at, (i, k) in enumerate(spots)
+    ]
+    for load in loads:
+        load.start()
+    for load, store in zip(loads, stores):
+        load.wait()
+        store.start()
+    for store in stores:
+        store.wait()
+
+
+def place(pieces, total, targets):
+    count = pieces[0].shape[0]
+    anywhere = pl.BlockSpec(memory_space=pl.ANY)
+    shape = (total,) + pieces[0].shape[1:]
+    size = 2 * 2 * total * pieces[0][0].size
+    return pl.pallas_call(
+        functools.partial(place_kernel, count, targets),
+        in_specs=[anywhere] * len(pieces),
+        out_specs=anywhere,
+        out_shape=jax.ShapeDtypeStruct(shape, pieces[0].dtype),
+        scratch_shapes=[
+            pltpu.VMEM((len(pieces) * count,) + pieces[0].shape[1:], pieces[0].dtype),
+            pltpu.SemaphoreType.DMA((len(pieces) * count,)),
+            pltpu.SemaphoreType.DMA((len(pieces) * count,)),
+        ],
+        compiler_params=pltpu.CompilerParams(vmem_limit_bytes=40 * 2**20),
+        cost_estimate=pl.CostEstimate(flops=0, bytes_accessed=size, transcendentals=0),
+    )(*pieces)
+
+
+def up_sum_kernel(narrow, act_ref, dpre_ref, out_ref):
+    shard = out_ref.shape[-2]
+    total = dot(act_ref[...], dpre_ref[...], ((0,), (0,))).astype(bf16)
+    for y in range(2):
+        for core in range(2):
+            at = (2 * y + core) * shard
+            out_ref[core, 0, 0, y] = total[at : at + shard]
+
+
+def up_sums(act, dpre, wide, narrow, shard):
+    tokens, cols = dpre.shape
+    upper = wide // 4
+    if (narrow * shard) % 128:
+        total = dot(act, dpre, ((0,), (0,))).astype(bf16)
+        total = total.reshape(upper, 2, 2, 2, 2, shard, cols).transpose(4, 2, 0, 1, 3, 5, 6)
+        return total.reshape(2, 2, upper, 4, shard, cols)
+    return pl.pallas_call(
+        functools.partial(up_sum_kernel, narrow),
+        grid=(wide,),
+        in_specs=[
+            pl.BlockSpec((tokens, narrow * shard), lambda w: (0, w)),
+            pl.BlockSpec((tokens, cols), lambda w: (0, 0)),
+        ],
+        out_specs=pl.BlockSpec((2, 1, 1, 2, shard, cols), lambda w: (0, w % 2, w // 4, (w // 2) % 2, 0, 0)),
+        out_shape=jax.ShapeDtypeStruct((2, 2, upper, 4, shard, cols), bf16),
+        compiler_params=pltpu.CompilerParams(vmem_limit_bytes=40 * 2**20),
+        cost_estimate=pl.CostEstimate(
+            flops=2 * tokens * cols * act.shape[1], bytes_accessed=2**24, transcendentals=0
+        ),
+    )(act, dpre)
+
+
+MESH = pl.DeviceIdType.MESH
+TILE = 512
+Y, Z, CORE, X, FAR = range(5)
+
+
+def each(count, body):
+    def step(i, carry):
+        body(i)
+        return carry
+
+    lax.fori_loop(0, count, step, 0)
+
+
+def feed_kernel(
+    act_ref,
+    top_zero,
+    top_one,
+    top_two,
+    top_three,
+    chosen_ref,
+    width_ref,
+    need_ref,
+    up_zero,
+    up_far,
+    up_next,
+    up_both,
+    down_zero,
+    down_far,
+    down_next,
+    down_both,
+    mixed_own,
+    mixed_come,
+    dact_own,
+    dact_come,
+    down_own,
+    down_come,
+    up_own,
+    up_come,
+    down_core,
+    up_core,
+    up,
+    down,
+    act,
+    dmix,
+    scale,
+    hid,
+    dpre,
+    relu,
+    mixed,
+    dact,
+    mixed_low,
+    dact_low,
+    down_near,
+    up_near,
+    down_held,
+    up_held,
+    load_sem,
+    send_sem,
+    recv_sem,
+):
+    w = lax.axis_index("wide")
+    n = lax.axis_index("narrow")
+    core, x, far = n % 2, w % 2, w // 4
+    peers = {
+        Y: {"narrow": (n + 2) % 4},
+        Z: {"wide": w + 2 - 4 * ((w // 2) % 2)},
+        CORE: {"narrow": n + 1 - 2 * core},
+        X: {"wide": w + 1 - 2 * x},
+        FAR: {"wide": (w + 4) % 8},
+    }
+    rows = act_ref.shape[0]
+    dim = act_ref.shape[1]
+    started = []
+
+    def send(source, target, peer):
+        at = len(started)
+        copy = pltpu.make_async_remote_copy(
+            src_ref=source,
+            dst_ref=target,
+            send_sem=send_sem.at[at],
+            recv_sem=recv_sem.at[at],
+            device_id=peers[peer],
+            device_id_type=MESH,
+        )
+        copy.start()
+        started.append(copy)
+        return copy
+
+    def load(source, target, at):
+        copy = pltpu.make_async_copy(source, target, load_sem.at[at])
+        copy.start()
+        return copy
+
+    def slot(k):
+        return pl.ds(k * rows, rows)
+
+    barrier = pltpu.get_barrier_semaphore()
+    for peer in peers.values():
+        pl.semaphore_signal(barrier, inc=1, device_id=peer, device_id_type=MESH)
+    pl.semaphore_wait(barrier, len(peers))
+
+    to_y = send(act_ref, act.at[slot(1)], Y)
+    to_z = send(act_ref, act.at[slot(2)], Z)
+    scale_y = send(chosen_ref, scale.at[slot(1)], Y)
+    scale_z = send(chosen_ref, scale.at[slot(2)], Z)
+    loads = [load(act_ref, act.at[slot(0)], 0)]
+    for k, top in enumerate((top_zero, top_one, top_two, top_three)):
+        loads.append(load(top, dmix.at[slot(k)], 1 + k))
+    weights = []
+    for k, (up_part, down_part) in enumerate(
+        ((up_zero, down_zero), (up_far, down_far), (up_next, down_next), (up_both, down_both))
+    ):
+        its_far = far + (1 - 2 * far) * (k % 2)
+        its_x = x + (1 - 2 * x) * (k // 2)
+        up_slot = up.at[its_far, :, its_x, :, core]
+        down_slot = down.at[core, its_x, its_far]
+        weights += [send(up_part, up_slot, CORE), send(down_part, down_slot, CORE)]
+        loads += [load(up_part, up_slot, 5 + 2 * k), load(down_part, down_slot, 6 + 2 * k)]
+    scale[slot(0), :] = chosen_ref[...]
+    for copy in loads:
+        copy.wait()
+    for copy in weights:
+        copy.wait_recv()
+    half = rows // 2
+    to_y.wait_recv()
+    to_z.wait_recv()
+    scale_y.wait_recv()
+    scale_z.wait_recv()
+    both_y = send(act.at[pl.ds(2 * rows, half)], act.at[pl.ds(3 * rows, half)], Y)
+    both_z = send(act.at[pl.ds(rows + half, half)], act.at[pl.ds(3 * rows + half, half)], Z)
+    scale_both = send(scale.at[slot(2)], scale.at[slot(3)], Y)
+
+    def columns(t):
+        return pl.ds(pl.multiple_of(t * TILE, TILE), TILE)
+
+    def forward(pair):
+        group = pl.ds(pair * 2 * rows, 2 * rows)
+        width = width_ref[group, :]
+
+        def scaled(i):
+            at = pl.ds(pl.multiple_of(pair * 2 * rows + i * 32, 32), 32)
+            dmix[at, :] = (dmix[at, :].astype(f32) * scale[at, :][:, :1]).astype(bf16)
+
+        each(2 * rows // 32, scaled)
+
+        def first(t, carry):
+            at = columns(t)
+            weight = up[:, :, :, :, :, :, at].reshape(dim, TILE)
+            pre = jnp.maximum(dot(act[group, :], weight, ((1,), (0,))), 0.0)
+            pre = jnp.where(need_ref[:, at] <= width, pre, 0.0)
+            relu[:, at] = pre.astype(bf16)
+            hid[group, at] = (pre * pre).astype(bf16)
+            return carry
+
+        def second(t, carry):
+            at = columns(t)
+            weight = down[:, :, :, :, at].reshape(dim, TILE)
+            value = dot(hid[group, :], weight, ((1,), (0,)))
+            mixed[group, at] = value.astype(bf16)
+            return carry
+
+        def third(t, carry):
+            at = columns(t)
+            weight = down[t // 2, t % 2].reshape(TILE, dim)
+            value = dot(dmix[group, :], weight, ((1,), (1,)))
+            dpre[group, at] = (value * 2.0 * relu[:, at].astype(f32)).astype(bf16)
+            return carry
+
+        def fourth(t, carry):
+            at = columns(t)
+            weight = up[t // 2, t % 2].reshape(TILE, dim)
+            value = dot(dpre[group, :], weight, ((1,), (1,)))
+            dact[group, at] = value.astype(bf16)
+            return carry
+
+        lax.fori_loop(0, dim // TILE, first, 0)
+        lax.fori_loop(0, dim // TILE, second, 0)
+        lax.fori_loop(0, dim // TILE, third, 0)
+        lax.fori_loop(0, dim // TILE, fourth, 0)
+
+    forward(0)
+    mixed_one = send(mixed.at[slot(1)], mixed_low.at[0], Y)
+    both_y.wait_recv()
+    both_z.wait_recv()
+    scale_both.wait_recv()
+    forward(1)
+    mixed_three = send(mixed.at[slot(3)], mixed_low.at[1], Y)
+    dact_two = send(dact.at[slot(2)], dact_low.at[0], Z)
+    dact_three = send(dact.at[slot(3)], dact_low.at[1], Z)
+
+    cut = dim // 2
+
+    def down_terms(side):
+        at = pl.ds(side * cut, cut)
+
+        def block(k, carry):
+            rows_of = hid[:, pl.ds(pl.multiple_of(k * TILE, TILE), TILE)]
+            value = dot(rows_of, dmix[:, at], ((0,), (0,))).astype(bf16)
+            down[k // 2, k % 2, :, :, at] = value.reshape(2, TILE // 2, cut)
+            return carry
+
+        lax.fori_loop(0, dim // TILE, block, 0)
+
+    def up_terms(side):
+        at = pl.ds(side * cut, cut)
+
+        def block(k, carry):
+            rows_of = act[:, pl.ds(pl.multiple_of(k * TILE, TILE), TILE)]
+            value = dot(rows_of, dpre[:, at], ((0,), (0,))).astype(bf16)
+            up[k // 2, k % 2, :, :, :, :, at] = value.reshape(2, 2, 2, TILE // 8, cut)
+            return carry
+
+        lax.fori_loop(0, dim // TILE, block, 0)
+
+    cores = []
+    for side in range(2):
+        at = pl.ds(side * cut, cut)
+        down_terms(side)
+        cores.append(send(down.at[1 - core, :, :, :, at], down_core.at[side], CORE))
+    for side in range(2):
+        at = pl.ds(side * cut, cut)
+        up_terms(side)
+        cores.append(send(up.at[:, :, :, :, 1 - core, :, at], up_core.at[side], CORE))
+
+    def core_sum(k):
+        side = k % 2
+        at = pl.ds(side * cut, cut)
+        cores[k].wait_recv()
+        source = (down_core if k < 2 else up_core).at[side]
+        copy = load(source, down_held if k < 2 else up_held, 13 + k)
+        copy.wait()
+        if k < 2:
+
+            def add_down(i):
+                a, b, part = i // 16, (i // 8) % 2, pl.ds(pl.multiple_of((i % 8) * 32, 32), 32)
+                here = down[core, a, b, part, at].astype(f32)
+                down[core, a, b, part, at] = (here + down_held[a, b, part, :].astype(f32)).astype(bf16)
+
+            each(32, add_down)
+            return send(down.at[core, 1 - x, :, :, at], down_near.at[:, :, at], X)
+
+        def add_up(i):
+            a, b, c, d = i // 8, (i // 4) % 2, (i // 2) % 2, i % 2
+            here = up[a, b, c, d, core, :, at].astype(f32)
+            up[a, b, c, d, core, :, at] = (here + up_held[a, b, c, d].astype(f32)).astype(bf16)
+
+        each(16, add_up)
+        return send(up.at[:, :, 1 - x, :, core, :, at], up_near.at[:, :, :, :, at], X)
+
+    nears = [core_sum(k) for k in range(4)]
+
+    mixed_one.wait_recv()
+    mixed_three.wait_recv()
+
+    def add_low(total, k, low, side):
+        def step(i):
+            at = pl.ds(pl.multiple_of(k * rows + i * 32, 32), 32)
+            come = low[side, pl.ds(pl.multiple_of(i * 32, 32), 32), :].astype(f32)
+            total[at, :] = (total[at, :].astype(f32) + come).astype(bf16)
+
+        each(rows // 32, step)
+
+    add_low(mixed, 2, mixed_low, 1)
+    mixed_last = send(mixed.at[slot(2)], mixed_come, Z)
+    add_low(mixed, 0, mixed_low, 0)
+    keep = [load(mixed.at[slot(0)], mixed_own, 17)]
+    dact_two.wait_recv()
+    dact_three.wait_recv()
+    add_low(dact, 1, dact_low, 1)
+    dact_last = send(dact.at[slot(1)], dact_come, Y)
+    add_low(dact, 0, dact_low, 0)
+    keep.append(load(dact.at[slot(0)], dact_own, 18))
+
+    fars = []
+    for k in range(4):
+        at = pl.ds((k % 2) * cut, cut)
+        nears[k].wait_recv()
+        if k < 2:
+
+            def add_down(i, at=at):
+                b, part = i // 8, pl.ds(pl.multiple_of((i % 8) * 32, 32), 32)
+                here = down[core, x, b, part, at].astype(f32)
+                down[core, x, b, part, at] = (here + down_near[b, part, at].astype(f32)).astype(bf16)
+
+            each(16, add_down)
+            fars.append(send(down.at[core, x, 1 - far, :, at], down_come.at[:, at], FAR))
+            keep.append(load(down.at[core, x, far, :, at], down_own.at[:, at], 19 + k))
+        else:
+
+            def add_up(i, at=at):
+                a, b, d = i // 4, (i // 2) % 2, i % 2
+                here = up[a, b, x, d, core, :, at].astype(f32)
+                up[a, b, x, d, core, :, at] = (here + up_near[a, b, d, :, at].astype(f32)).astype(bf16)
+
+            each(8, add_up)
+            fars.append(send(up.at[1 - far, :, x, :, core, :, at], up_come.at[:, :, :, at], FAR))
+            keep.append(load(up.at[far, :, x, :, core, :, at], up_own.at[:, :, :, at], 19 + k))
+    for copy in keep:
+        copy.wait()
+    for copy in [mixed_last, dact_last] + fars:
+        copy.wait_recv()
+    for copy in started:
+        copy.wait_send()
+
+
+def feed_forward(act, tops, chosen, width_all, need, ups, downs):
+    rows, dim = act.shape
+    any_space = pl.BlockSpec(memory_space=pl.ANY)
+    in_vmem = pl.BlockSpec(memory_space=pltpu.VMEM)
+    tokens = 4 * rows
+    cut = dim // 2
+    shard = dim // 32
+
+    def shape(*dims):
+        return jax.ShapeDtypeStruct(dims, bf16)
+
+    return pl.pallas_call(
+        feed_kernel,
+        in_specs=[any_space] * 5 + [in_vmem] * 3 + [any_space] * 8,
+        out_specs=[any_space] * 10,
+        out_shape=[
+            shape(rows, dim),
+            shape(rows, dim),
+            shape(rows, dim),
+            shape(rows, dim),
+            shape(dim // 8, dim),
+            shape(dim // 8, dim),
+            shape(2, 2, shard, dim),
+            shape(2, 2, shard, dim),
+            shape(2, 2, 2, dim // 8, cut),
+            shape(2, 2, 2, 2, 2, shard, cut),
+        ],
+        scratch_shapes=[
+            pltpu.VMEM((2, 2, 2, 2, 2, shard, dim), bf16),
+            pltpu.VMEM((2, 2, 2, dim // 8, dim), bf16),
+            pltpu.VMEM((tokens, dim), bf16),
+            pltpu.VMEM((tokens, dim), bf16),
+            pltpu.VMEM((tokens, 128), f32),
+            pltpu.VMEM((tokens, dim), bf16),
+            pltpu.VMEM((tokens, dim), bf16),
+            pltpu.VMEM((2 * rows, dim), bf16),
+            pltpu.VMEM((tokens, dim), bf16),
+            pltpu.VMEM((tokens, dim), bf16),
+            pltpu.VMEM((2, rows, dim), bf16),
+            pltpu.VMEM((2, rows, dim), bf16),
+            pltpu.VMEM((2, dim // 8, dim), bf16),
+            pltpu.VMEM((2, 2, 2, shard, dim), bf16),
+            pltpu.VMEM((2, 2, dim // 8, cut), bf16),
+            pltpu.VMEM((2, 2, 2, 2, shard, cut), bf16),
+            pltpu.SemaphoreType.DMA((23,)),
+            pltpu.SemaphoreType.DMA((36,)),
+            pltpu.SemaphoreType.DMA((36,)),
+        ],
+        compiler_params=pltpu.CompilerParams(
+            collective_id=0, has_side_effects=True, vmem_limit_bytes=62 * 2**20
+        ),
+        cost_estimate=pl.CostEstimate(
+            flops=12 * tokens * dim * dim, bytes_accessed=2**25, transcendentals=0
+        ),
+    )(act, *tops, chosen, width_all, need, *ups, *downs)
 
 
 def swap(array, axis, size, bits):
@@ -298,7 +741,6 @@
     head_at = w_at % head_groups
     row_at = (w_at // head_groups) * my_rows
     ring = Ring("wide", wide)
-    slots = (0, 2, 1, 3)
 
     def pick_rows(array):
         return lax.dynamic_slice_in_dim(array, row_at, my_rows, 0) if row_groups > 1 else array
@@ -310,26 +752,61 @@
         return lax.dynamic_update_slice_in_dim(whole, array, row_at, 0)
 
     def narrow_gather(part):
-        other = swap(part, "narrow", narrow, 2)
-        both = jnp.stack([part, other])
-        return jnp.concatenate([both, swap(both, "narrow", narrow, 1)])
-
-    def narrow_scatter(terms):
-        come = swap(terms[2:].astype(bf16), "narrow", narrow, 1)
-        pair = terms[:2] + come.astype(f32)
-        return pair[0] + swap(pair[1].astype(bf16), "narrow", narrow, 2).astype(f32)
-
-    def in_order(parts):
-        whole = jnp.zeros(parts.shape, parts.dtype)
-        for place, slot in enumerate(slots):
-            whole = lax.dynamic_update_slice_in_dim(whole, parts[place : place + 1], n_at ^ slot, 0)
-        return whole
-
-    def out_of_order(whole):
-        return jnp.concatenate([lax.dynamic_slice_in_dim(whole, n_at ^ slot, 1, 0) for slot in slots])
-
-    def narrow_all_to_all(blocks):
-        return lax.all_to_all(blocks, "narrow", 0, 0, tiled=True)
+        found = part[None]
+        for bits in [2**k for k in range(narrow.bit_length() - 1)]:
+            other = swap(found, "narrow", narrow, bits)
+            mine = (n_at & bits) == 0
+            found = jnp.concatenate([jnp.where(mine, found, other), jnp.where(mine, other, found)])
+        return found
+
+    def narrow_scatter(array):
+        for bits in [2**k for k in range(narrow.bit_length() - 1)]:
+            array = array.reshape((-1, 2) + array.shape[1:])
+            at = (n_at // bits) & 1
+            others = lax.dynamic_index_in_dim(array, 1 - at, 1, keepdims=False)
+            array = lax.dynamic_index_in_dim(array, at, 1, keepdims=False)
+            come = swap(others.astype(bf16), "narrow", narrow, bits)
+            array = array + come.astype(f32)
+        return array[0]
+
+    shares = wide
+    upper = wide // 4
+    upper_bits = [2**k for k in range(2, wide.bit_length() - 1)][::-1]
+
+    def share_of(w, n):
+        return ((n & 1) * 2 + (w & 1)) * upper + (w >> 2)
+
+    def wide_of(share, team):
+        return (share % upper) * 4 + ((team >> 1) << 1) + ((share // upper) & 1)
+
+    def narrow_of(share, team):
+        return ((team & 1) << 1) + share // (2 * upper)
+
+    def team_of(w, n):
+        return ((w >> 1) & 1) * 2 + (n >> 1)
+
+    def beside(part):
+        return swap(part, "narrow", narrow, 2)
+
+    def across(part):
+        return swap(part, "wide", wide, 2)
+
+    def team_swap(blocks):
+        team = team_of(w_at, n_at)
+        mine = [lax.dynamic_index_in_dim(blocks, team ^ k, 0, keepdims=False) for k in range(4)]
+        both = [(i, i ^ (2 * narrow + 2)) for i in range(wide * narrow)]
+        come = jnp.stack(
+            [
+                mine[0],
+                beside(mine[1]),
+                across(mine[2]),
+                lax.ppermute(mine[3], ("wide", "narrow"), both),
+            ]
+        )
+        return jnp.stack([lax.dynamic_index_in_dim(come, team ^ k, 0, keepdims=False) for k in range(4)])
+
+    def pick(array, at):
+        return lax.dynamic_index_in_dim(array, at, 0, keepdims=False)
 
     exponent = jnp.arange(HEAD_DIM // 2, dtype=f32) * (2.0 / HEAD_DIM)
     angles = jnp.arange(length, dtype=f32)[:, None] * jnp.power(rope_base, -exponent)[None, :]
@@ -350,76 +827,150 @@
     blocks = w_qkv.reshape(shard, 3, head_groups, cols).transpose(2, 0, 1, 3)
     blocks = jnp.tile(blocks.reshape(head_groups, shard, 3 * cols), (row_groups, 1, 1))
     blocks = lax.all_to_all(blocks, "wide", 0, 0, tiled=True)
-    my_qkv = in_order(narrow_gather(blocks)).transpose(1, 0, 2, 3).reshape(dim, 3 * cols)
-
-    act_all = jnp.zeros((my_rows, length, dim), bf16)
-    for owner, piece in ring.gather(act_one.transpose(1, 0, 2)):
-        piece = pick_rows(piece.transpose(1, 0, 2))
-        act_all = lax.dynamic_update_slice_in_dim(act_all, piece, owner * part_len, 1)
+    my_qkv = narrow_gather(blocks).transpose(1, 0, 2, 3).reshape(dim, 3 * cols)
+    out_parts = narrow_gather(lax.all_gather(w_out, "wide", axis=0, tiled=False))
+    out_full = out_parts.transpose(1, 0, 2, 3).reshape(dim, dim)
+
+    piece_rows = w_down.shape[0]
+    up_blocks = w_up.reshape(shard, upper, 2, 2, 2, 2, piece_rows).transpose(2, 4, 0, 5, 3, 1, 6)
+    up_part = team_swap(up_blocks.reshape(4, shard, shares * piece_rows))
+    top = out_grad.reshape(count, dim)
+    top_beside = beside(top)
+    width_flat = width_choice.reshape(count)
+    width_across = across(width_flat)
+    width_all = jnp.concatenate([width_flat, beside(width_flat), width_across, beside(width_across)])
+
+    act_all = jnp.zeros((my_rows, wide, part_len, dim), bf16)
+    for owner, piece in ring.gather(act_one.reshape(count, dim)):
+        piece = pick_rows(piece.reshape(rows, part_len, dim))
+        act_all = lax.dynamic_update_slice(act_all, piece[:, None], (0, owner, 0, 0))
     act_flat = act_all.reshape(my_rows * length, dim)
+    act_flat, my_qkv, up_part, top_beside, width_all, down_part, top = join(
+        act_flat, my_qkv, up_part, top_beside, width_all, w_down, top
+    )
+
+    up_found = [((0, 0), up_part)]
+    down_found = [((0, 0), down_part)]
+
+    def spread(found, bit):
+        return found + [((w ^ bit, n), swap(piece, "wide", wide, bit)) for (w, n), piece in found]
+
+    for bit in upper_bits:
+        up_found = spread(up_found, bit)
+    up_near = ((1, 0), swap(up_part, "wide", wide, 1))
+    down_near = ((1, 0), swap(down_part, "wide", wide, 1))
     proj = dot(act_flat, my_qkv, ((1,), (0,))).reshape(my_rows, length, 3 * cols)
     qkv, att, att_part, lse = attend(proj, split, limits, cos2, sin2, my_heads)
-
     sends = att_part.reshape(my_rows, wide, part_len, cols).transpose(1, 0, 2, 3)
+    joined = join(sends, up_near[1], down_near[1], *[piece for _, piece in up_found])
+    sends = joined[0]
+    up_near, down_near = (up_near[0], joined[1]), (down_near[0], joined[2])
+    up_found = [(at, piece) for (at, _), piece in zip(up_found, joined[3:])]
+
     come = lax.all_to_all(sends, "wide", 0, 0, tiled=True)
+    up_far = [((w ^ 1, n), swap(piece, "wide", wide, 1)) for (w, n), piece in up_found[1:]]
+    top_across = across(top)
+    joined = join(come, top_across, down_part, *[piece for _, piece in up_far])
+    come, top_across, down_part = joined[:3]
+    up_found = up_found + [up_near] + [(at, piece) for (at, _), piece in zip(up_far, joined[3:])]
     come = come.reshape(row_groups, head_groups, my_rows, part_len, cols)
     att_low = come.transpose(0, 2, 3, 1, 4).reshape(count, dim)
-    out_full = lax.all_gather(w_out, ("wide", "narrow"), axis=0, tiled=True)
+
+    down_found = [((0, 0), down_part)]
+    for bit in upper_bits:
+        down_found = spread(down_found, bit)
+    down_far = [((w ^ 1, n), swap(piece, "wide", wide, 1)) for (w, n), piece in down_found[1:]]
+    down_found = down_found + [down_near] + down_far
+    top_both = beside(top_across)
     x_one = inputs.reshape(count, dim) + dot(att_low, out_full, ((1,), (0,)))
 
     center = x_one - jnp.mean(x_one, axis=-1, keepdims=True)
     inv_two = lax.rsqrt(jnp.mean(center * center, axis=-1, keepdims=True) + norm_eps)
     normed_two = center * inv_two
     ln_out = normed_two * gain_two + bias_two
-    width_flat = width_choice.reshape(count)
+    act_two = ln_out.astype(bf16)
     onehot = (width_flat[:, None] == jnp.arange(WIDTHS, dtype=jnp.int32)[None, :]).astype(f32)
     router_prob = jax.nn.softmax(jnp.dot(ln_out, router, precision=highest), axis=-1)
     chosen = jnp.sum(router_prob * onehot, axis=-1)
-    act_two = ln_out.astype(bf16)
-    grad_top = out_grad.reshape(count, dim).astype(f32)
-
-    piece_rows = w_down.shape[0]
-    up_blocks = w_up.reshape(shard, wide, narrow, piece_rows).transpose(2, 0, 1, 3)
-    up_part = narrow_all_to_all(up_blocks.reshape(narrow, shard, wide * piece_rows))
-    up_mine = ring.gather_rows(up_part.reshape(narrow * shard, wide * piece_rows))
-    down_mine = ring.gather_rows(w_down)
-    top_all = narrow_gather(out_grad.reshape(count, dim)).reshape(narrow * count, dim)
-    facts = narrow_gather(jnp.stack([chosen, width_flat.astype(f32)]))
-    chosen_all = facts[:, 0].reshape(narrow * count, 1)
-    width_all = facts[:, 1].reshape(narrow * count, 1)
-    act_many = narrow_gather(act_two).reshape(narrow * count, dim)
-    units = (jnp.arange(wide, dtype=jnp.int32)[:, None] * narrow + n_at) * piece_rows
-    units = (units + jnp.arange(piece_rows, dtype=jnp.int32)[None, :]).reshape(-1)
-    need = (units // (hidden // WIDTHS)).astype(f32)
-    mask = need[None, :] <= width_all
-
-    pre = jnp.maximum(dot(act_many, up_mine, ((1,), (0,))), 0.0)
-    pre = jnp.where(mask, pre, 0.0)
-    hid = (pre * pre).astype(bf16)
-    dmix = (top_all.astype(f32) * chosen_all).astype(bf16)
-    mixed = dot(hid, down_mine, ((1,), (0,)))
-    dhid = dot(dmix, down_mine, ((1,), (1,)))
-    dpre = (dhid * 2.0 * pre).astype(bf16)
-    dact = dot(dpre, up_mine, ((1,), (1,)))
-    mixed = narrow_scatter(mixed.reshape(narrow, count, dim))
-    grad_act_two = narrow_scatter(dact.reshape(narrow, count, dim))
-
-    half = dim // 2
-
-    def up_term(owner, side):
-        rows_of = lax.dynamic_slice_in_dim(act_many, owner * (narrow * shard), narrow * shard, 1)
-        wide_half = dpre.shape[1] // 2
-        return dot(rows_of, dpre[:, side * wide_half : (side + 1) * wide_half], ((0,), (0,)))
-
-    def down_term(owner, side):
-        rows_of = lax.dynamic_slice_in_dim(hid, owner * piece_rows, piece_rows, 1)
-        return dot(rows_of, dmix[:, side * half : (side + 1) * half], ((0,), (0,)))
-
-    down_grad = jnp.concatenate(ring.scatter(down_term), axis=1)
-    up_sum = jnp.concatenate(ring.scatter(up_term), axis=1).astype(bf16)
-    up_sum = narrow_all_to_all(up_sum.reshape(narrow, shard, wide * piece_rows))
-    up_grad = up_sum.reshape(narrow, shard, wide, piece_rows).transpose(1, 2, 0, 3)
-    up_grad = up_grad.reshape(shard, hidden).astype(f32)
+    grad_top = top.astype(f32)
+    share = jnp.arange(shares, dtype=jnp.int32)[:, None]
+    team = team_of(w_at, n_at)
+    units = (wide_of(share, team) * narrow + narrow_of(share, team)) * piece_rows
+    units = (units + jnp.arange(piece_rows, dtype=jnp.int32)[None, :]).reshape(1, -1)
+    need = units // (hidden // WIDTHS)
+
+    def share_core(array):
+        return pick(array, n_at & 1) + swap(pick(array, 1 - (n_at & 1)), "narrow", narrow, 1)
+
+    def share_near(array):
+        return pick(array, w_at & 1) + swap(pick(array, 1 - (w_at & 1)), "wide", wide, 1)
+
+    def share_far(array):
+        for bit in upper_bits:
+            array = array.reshape((2, -1) + array.shape[1:])
+            at = (w_at // bit) & 1
+            array = pick(array, at) + swap(pick(array, 1 - at), "wide", wide, bit)
+        return array[0]
+
+    tops = (top, top_beside, top_across, top_both)
+    if wide == 8 and narrow == 4:
+        mixed, mixed_come, grad_act_two, dact_come, down_grad, down_come, up_sum, up_come, _, _ = feed_forward(
+            act_two,
+            tops,
+            jnp.broadcast_to(chosen[:, None], (count, 128)),
+            width_all[:, None].astype(f32),
+            need.astype(f32),
+            [piece.reshape(2, 2, shard, shares * piece_rows) for _, piece in up_found],
+            [piece for _, piece in down_found],
+        )
+        mixed = mixed.astype(f32) + mixed_come.astype(f32)
+        grad_act_two = grad_act_two.astype(f32) + dact_come.astype(f32)
+        down_grad = down_grad.astype(f32) + down_come.astype(f32)
+        up_sum = up_sum + up_come
+        up_sum = up_sum.reshape(4, shard, shares * piece_rows)
+    else:
+        up_found = up_found + [((w, n ^ 1), swap(piece, "narrow", narrow, 1)) for (w, n), piece in up_found]
+        down_found = down_found + [((w, n ^ 1), swap(p, "narrow", narrow, 1)) for (w, n), p in down_found]
+
+        def up_target(i, k):
+            w, n = lax.axis_index("wide"), lax.axis_index("narrow")
+            dw, dn = up_found[i][0]
+            return ((w ^ dw) & ~2 | (k & 2)) * narrow + ((n ^ dn) & 1 | ((k & 1) * 2))
+
+        def down_target(i, k):
+            dw, dn = down_found[i][0]
+            return share_of(lax.axis_index("wide") ^ dw, lax.axis_index("narrow") ^ dn)
+
+        up_mine = place([piece for _, piece in up_found], wide * narrow, up_target)
+        up_mine = up_mine.reshape(dim, shares * piece_rows)
+        down_mine = place([piece[None] for _, piece in down_found], shares, down_target)
+        down_mine = down_mine.reshape(shares * piece_rows, dim)
+
+        def team_gather(part):
+            far = across(part)
+            return jnp.concatenate([part, beside(part), far, beside(far)])
+
+        def team_scatter(terms):
+            low = beside(jnp.stack([terms[1], terms[3]])).astype(f32)
+            near, far = terms[0] + low[0], terms[2] + low[1]
+            return near + across(far.astype(bf16)).astype(f32)
+
+        act_many = team_gather(act_two)
+        mask = need <= width_all[:, None]
+        pre = jnp.maximum(dot(act_many, up_mine, ((1,), (0,))), 0.0)
+        pre = jnp.where(mask, pre, 0.0).astype(bf16).astype(f32)
+        hid = (pre * pre).astype(bf16)
+        dmix = (jnp.concatenate(tops).astype(f32) * team_gather(chosen)[:, None]).astype(bf16)
+        mixed = dot(hid, down_mine, ((1,), (0,))).astype(bf16)
+        dhid = dot(dmix, down_mine, ((1,), (1,)))
+        dpre = (dhid * 2.0 * pre).astype(bf16)
+        dact = dot(dpre, up_mine, ((1,), (1,))).astype(bf16)
+        mixed = team_scatter(mixed.reshape(4, count, dim))
+        grad_act_two = team_scatter(dact.reshape(4, count, dim))
+        down_sum = dot(hid, dmix, ((0,), (0,))).astype(bf16).reshape(2, 2, upper, piece_rows, dim)
+        down_grad = share_far(share_near(share_core(down_sum))).astype(f32)
+        up_sum = up_sums(act_many, dpre, wide, narrow, shard)
+        up_sum = share_far(share_near(share_core(up_sum)))
 
     block_out = (x_one + mixed * chosen[:, None]).astype(bf16)
     grad_prob = jnp.sum(grad_top * mixed, axis=-1)
@@ -442,10 +993,15 @@
     come = lax.all_to_all(sends, "wide", 0, 0, tiled=True)
     dat = come.transpose(1, 0, 2, 3).reshape(my_rows, length, cols)
     dproj = attend_back(qkv, att, lse, dat, split, limits, cos2, sin2, my_heads)
-    grad_out = dot(att_low, grad_branch, ((0,), (0,))).astype(bf16)
-    out_proj_grad = lax.psum_scatter(
-        grad_out, ("wide", "narrow"), scatter_dimension=0, tiled=True
-    ).astype(f32)
+    grad_out = dot(att_low, grad_branch, ((0,), (0,)))
+    grad_out = grad_out.reshape(wide, narrow, shard, dim).transpose(1, 0, 2, 3)
+    grad_out = narrow_scatter(grad_out).astype(bf16).reshape(wide * shard, dim)
+    dproj, act_flat, grad_out = join(dproj, act_flat, grad_out)
+    out_proj_grad = lax.psum_scatter(grad_out, "wide", scatter_dimension=0, tiled=True).astype(f32)
+    up_sum = team_swap(up_sum)
+    up_grad = up_sum.reshape(2, 2, shard, 2, 2, upper, piece_rows).transpose(2, 5, 0, 4, 1, 3, 6)
+    up_grad = up_grad.reshape(shard, hidden).astype(f32)
+    half = dim // 2
 
     def one_term(owner, side):
         rows_of = lax.dynamic_slice_in_dim(dproj, owner * part_len, part_len, 1)
@@ -456,22 +1012,28 @@
     grad_act_one = jnp.concatenate(ring.scatter(one_term), axis=1)
 
     grad_qkv = dot(act_flat, dproj.reshape(my_rows * length, 3 * cols), ((0,), (0,)))
+    gain_one_part = jnp.sum(grad_qkv * my_qkv.astype(f32), axis=1) / gain_one
     grad_qkv = grad_qkv.reshape(wide, narrow, shard, 3 * cols).transpose(1, 0, 2, 3)
-    grad_qkv = narrow_scatter(out_of_order(grad_qkv)).astype(bf16)
+    grad_qkv = narrow_scatter(grad_qkv).astype(bf16)
     grad_qkv = lax.all_to_all(grad_qkv, "wide", 0, 0, tiled=True).astype(f32)
     grad_qkv = jnp.sum(grad_qkv.reshape(row_groups, head_groups, shard, 3, cols), axis=0)
     qkv_grad = grad_qkv.transpose(1, 2, 0, 3).reshape(shard, 3 * dim)
 
     normed_flat = normed_one.reshape(count, dim)
-    grad_gain_one = jnp.sum(grad_act_one * normed_flat, axis=0)
     grad_scaled = grad_act_one * gain_one
     input_grad = grad_x_one + inv_one.reshape(count, 1) * (
         grad_scaled - normed_flat * jnp.mean(grad_scaled * normed_flat, axis=-1, keepdims=True)
     )
-    router_grad, gain_one_grad, gain_two_grad, bias_two_grad, counts_all = lax.psum(
-        (grad_router, grad_gain_one, grad_gain_two, grad_bias_two, jnp.sum(onehot, axis=0)),
-        ("wide", "narrow"),
+    small = jnp.concatenate(
+        [gain_one_part, grad_gain_two, grad_bias_two, grad_router.T.reshape(-1), jnp.sum(onehot, axis=0)]
     )
+    for bits in (1, 2):
+        small = small + swap(small, "narrow", narrow, bits)
+    for bits in [2**k for k in range(wide.bit_length() - 1)]:
+        small = small + swap(small, "wide", wide, bits)
+    gain_one_grad, gain_two_grad, bias_two_grad = (small[k * dim : (k + 1) * dim] for k in range(3))
+    router_grad = small[3 * dim : (3 + WIDTHS) * dim].reshape(WIDTHS, dim).T
+    counts_all = small[(3 + WIDTHS) * dim :]
     return (
         block_out.reshape(rows, part_len, dim),
         input_grad.reshape(rows, part_len, dim),

time: 917 us -> 831 us (0.906)
  Pallas kernels: 61.3 us -> 281 us
  matrix products: 168 us -> 66.9 us
  waiting for transfers between devices: 301 us -> 209 us
  local copies, waits for them, and re-layouts: 121 us -> 72.7 us
  blocking collectives: 44 us -> 0 us
  starting transfers between devices: 122 us -> 84.3 us
  other arithmetic: 46.9 us -> 71 us
    pallas_call x0 -> x1, Pallas kernels: none -> 220 us  [feed_forward(): pl.pallas_call(feed_kernel, in_specs=[any_space] * 5 + [in_vmem] * 3 + [a...]
    dot_general x57 -> x21, matrix products: 161 us -> 59.2 us  [dot(): lax.dot_general(a, b, (contract, ((), ())), preferred_element_type=f32)]
    ppermute x42 -> x14, waiting for transfers between devices: 141 us -> 39.4 us  [scatter(): come = lax.ppermute(sums[side].astype(bf16), self.axis, perm)]
    ppermute x14 -> x29, waiting for transfers between devices: 44.6 us -> 115 us  [swap(): return lax.ppermute(array, axis, [(i, i ^ bits) for i in range(size)])]
    dynamic_update_slice x26 -> x6, local copies, waits for them, and re-layouts: 62.7 us -> 13.9 us  [on_device(): lax.dynamic_update_slice(act_all, piece[:, None], (0, owner, 0, 0))]
    psum x1 -> x0, blocking collectives: 44 us -> none  [on_device(): lax.psum((grad_router, grad_gain_one, grad_gain_two, grad_bias_two, jnp.s...]
    ppermute x42 -> x14, starting transfers between devices: 55.1 us -> 16 us  [scatter(): come = lax.ppermute(sums[side].astype(bf16), self.axis, perm)]
    ppermute x9 -> x3, waiting for transfers between devices: 50.3 us -> 14.9 us  [gather(): back = lax.ppermute(back, self.axis, self.left)]
  transfers between devices with their start and end apart: 88 -> 59, of which waited for: 35 -> 23; matrix products, arithmetic and copies ran while one was open for 30% -> 21% of each run, Pallas kernels for 7% -> 7%
where the time goes in v2:
time: 831 us; the launch traced here: 821 us
  Pallas kernels  281 us (34%)
  waiting for transfers between devices  209 us (25%)
  starting transfers between devices  84.3 us (10%)
  local copies, waits for them, and re-layouts  72.7 us (9%)
  other arithmetic  71 us (9%)
  matrix products  66.9 us (8%)
  between operations  36 us (4%)
    pallas_call x1, Pallas kernels, feed_forward(): pl.pallas_call(feed_kernel, in_specs=[any_space] * 5 + [in_vmem] * 3 + [a...  220 us
    ppermute x29, waiting for transfers between devices, swap(): return lax.ppermute(array, axis, [(i, i ^ bits) for i in range(size)])  115 us
    dot_general x21, matrix products, dot(): lax.dot_general(a, b, (contract, ((), ())), preferred_element_type=f32)  59.2 us
    ppermute x14, waiting for transfers between devices, scatter(): come = lax.ppermute(sums[side].astype(bf16), self.axis, perm)  39.4 us
    pallas_call x1, Pallas kernels, attend_back(): pl.pallas_call(functools.partial(attend_back_kernel, heads, length), grid...  33.4 us
    ppermute x29, starting transfers between devices, swap(): return lax.ppermute(array, axis, [(i, i ^ bits) for i in range(size)])  31.2 us
    pallas_call x1, Pallas kernels, attend(): pl.pallas_call(functools.partial(attend_kernel, heads, length), grid=(row...  27.7 us
    ppermute x3, waiting for transfers between devices, gather(): onward = lax.ppermute(onward, self.axis, self.right)  19.7 us
  transfers between devices with their start and end apart: 59, of which 23 were waited for; matrix products, arithmetic and copies ran while one was open for 21% of the time, Pallas kernels for 7%

profile of v2, /device:TPU:8, one launch (start us, length us, event | category | flops | bytes accessed | tf_op | source)
XLA Modules:
  0.0 821.2 jit_solution(14259656735488944164)
XLA Ops:
  17.6 6.4 all-to-all-start
  27.7 4.7 fusion.33
  39.2 4.3 broadcast_in_dim.11
  65.9 11.9 %collective-permute-done.11 = bf16[64,2048]{1,0:T(8,128)(2,1)} collective-permute-done((bf16[64,2048]{1,0:T(8,128)(2,1)}, bf16[64,2048]{1,0:T(8,128)(2,1)}, u32[]{:S(2)}, u32[]{:S(2)}) %collective-permute-start.11) | collective-permute-done | bytes 262176 | tf_op jit(solution)/shard_map/ppermute | solution.py:709
  88.5 19.7 %collective-permute-done.2 = bf16[256,2048]{1,0:T(8,128)(2,1)} collective-permute-done((bf16[256,2048]{1,0:T(8,128)(2,1)}, bf16[256,2048]{1,0:T(8,128)(2,1)}, u32[]{:S(2)}, u32[]{:S(2)}) %collective-permute-start.2) | collective-permute-done | bytes 1048608 | tf_op jit(solution)/shard_map/ppermute | solution.py:243
  118.9 14.8 %collective-permute-done.5 = bf16[256,2048]{1,0:T(8,128)(2,1)} collective-permute-done((bf16[256,2048]{1,0:T(8,128)(2,1)}, bf16[256,2048]{1,0:T(8,128)(2,1)}, u32[]{:S(2)}, u32[]{:S(2)}) %collective-permute-start.5) | collective-permute-done | bytes 1048608 | tf_op jit(solution)/shard_map/ppermute | solution.py:244
  162.5 10.8 %convolution_bitcast_fusion.proj_ref = f32[1,2048,768]{2,1,0:T(8,128)} fusion(bf16[2048,2048]{1,0:T(8,128)(2,1)} %bitcast.19, bf16[2048,768]{1,0:T(8,128)(2,1)S(1)} %bitcast.244), kind=kOutput, calls=%fused_computation.10 | convolution fusion | flops 6442450944 | bytes 17825792 | tf_op jit(solution)/shard_map/dot_general | solution.py:23
  173.3 27.7 %shard_map.221 = (bf16[1,2048,768]{2,1,0:T(8,128)(2,1)}, f32[1,2048,256]{2,1,0:T(8,128)}, bf16[1,2048,256]{2,1,0:T(8,128)(2,1)}, f32[1,2048,256]{2,1,0:T(8,128)}) custom-call(s32[1]{0:T(128)S(6)} %copy.78.split_ref, s32[1,3]{1,0:T(1,128)} %pad_add_fusion.1.limit_ref, f32[1,2048,768]{2,1,0:T(8,128)} %convolution_bitcast_fusion.proj_ref, ...), custom_call_target="tpu_custom_call" | custom-call | flops 4294967296 | bytes 16777216 | tf_op jit(solution)/shard_map/pallas_call | solution.py:111
  205.2 4.7 all-to-all-start.1
  211.9 37.5 %collective-permute-done.20.top_two = bf16[256,2048]{1,0:T(8,128)(2,1)} collective-permute-done((bf16[256,2048]{1,0:T(8,128)(2,1)}, bf16[256,2048]{1,0:T(8,128)(2,1)}, u32[]{:S(2)}, u32[]{:S(2)}) %collective-permute-start.20) | collective-permute-done | bytes 1048608 | tf_op jit(solution)/shard_map/ppermute | solution.py:709
  255.2 41.7 %collective-permute-done.25.down_far = bf16[256,2048]{1,0:T(8,128)(2,1)} collective-permute-done((bf16[256,2048]{1,0:T(8,128)(2,1)}, bf16[256,2048]{1,0:T(8,128)(2,1)}, u32[]{:S(2)}, u32[]{:S(2)}) %collective-permute-start.25) | collective-permute-done | bytes 1048608 | tf_op jit(solution)/shard_map/ppermute | solution.py:709
  297.5 5.4 broadcast_select_fusion.1
  302.9 7.5 pad_maximum_fusion
  310.4 6.1 fusion.165
  322.9 220.2 %shard_map.222 = (bf16[256,2048]{1,0:T(8,128)(2,1)}, bf16[256,2048]{1,0:T(8,128)(2,1)}, bf16[256,2048]{1,0:T(8,128)(2,1)}, bf16[256,2048]{1,0:T(8,128)(2,1)}, bf...) custom-call(bf16[256,2048]{1,0:T(8,128)(2,1)} %fusion.17.act_ref, ...), custom_call_target="tpu_custom_call" | custom-call | flops 51539607552 | bytes 33554432 | tf_op jit(solution)/shard_map/pallas_call | solution.py:662
  545.9 4.2 multiply_reduce_fusion.1
  557.2 5.8 copy-done.5
  565.6 5.7 convolution_convert_fusion
  572.8 9.0 %all-to-all-start.2 = ((bf16[8,1,256,256]{3,2,1,0:T(8,128)(2,1)}), bf16[8,1,256,256]{3,2,1,0:T(8,128)(2,1)}, u32[]{:S(2)}, u32[]{:S(2)}) async-start(bf16[8,1,256,256]{3,2,1,0:T(8,128)(2,1)} %bitcast.269), calls=%async_computation.2 | async-start | bytes 2097152 | tf_op jit(solution)/shard_map/all_to_all | solution.py:993
  582.0 5.9 bitcast_add_fusion
  606.2 33.4 %shard_map.223 = bf16[1,2048,768]{2,1,0:T(8,128)(2,1)} custom-call(s32[1]{0:T(128)S(6)} %copy.78.split_ref, s32[1,3]{1,0:T(1,128)} %pad_add_fusion.1.limit_ref, bf16[1,2048,768]{2,1,0:T(8,128)(2,1)} %get-tuple-element.63.qkv_ref, f32[1,2048,256]{2,1,0:T(8,128)} %get-tuple-element.64.att_ref, f32[1,2048,256]{2,1,0:T(8,128)} %get-tuple-element.65.lse_ref, ...), custom_call_target="tpu_custom_call" | custom-call | flops 10737418240 | bytes 16777216 | tf_op jit(solution)/shard_map/pallas_call | solution.py:205
  639.6 7.1 collective-permute-done.28
  646.6 4.8 add_convert_fusion
  658.3 10.8 %multiply_reduce_fusion = (f32[2048]{0:T(1024)S(1)}, f32[2048,768]{1,0:T(8,128)S(1)}) fusion(bf16[2048,768]{1,0:T(8,128)(2,1)S(1)} %bitcast.249, bf16[2048,2048]{1,0:T(8,128)(2,1)} %bitcast.19, bf16[1,2048,768]{2,1,0:T(8,128)(2,1)} %shard_map.223), kind=kOutput, calls=%fused_computation.3 | convolution fusion | flops 6447167488 | bytes 20979712 | tf_op jit(solution)/shard_map/dot_general | solution.py:23
  682.8 4.7 collective-permute-done.37
  694.3 8.9 %collective-permute-done.51 = f32[14340]{0:T(1024)S(1)} collective-permute-done((f32[14340]{0:T(1024)S(1)}, f32[14340]{0:T(1024)S(1)}, u32[]{:S(2)}, u32[]{:S(2)}) %collective-permute-start.51) | collective-permute-done | bytes 57392 | tf_op jit(solution)/shard_map/ppermute | solution.py:709
  716.3 4.1 copy.63
  735.0 17.7 %collective-permute-done.40 = bf16[256,1024]{1,0:T(8,128)(2,1)S(1)} collective-permute-done((bf16[256,1024]{1,0:T(8,128)(2,1)S(1)}, bf16[256,1024]{1,0:T(8,128)(2,1)S(1)}, u32[]{:S(2)}, u32[]{:S(2)}) %collective-permute-start.40) | collective-permute-done | bytes 524320 | tf_op jit(solution)/shard_map/ppermute | solution.py:262
  758.7 8.4 %collective-permute-done.41 = bf16[256,1024]{1,0:T(8,128)(2,1)S(1)} collective-permute-done((bf16[256,1024]{1,0:T(8,128)(2,1)S(1)}, bf16[256,1024]{1,0:T(8,128)(2,1)S(1)}, u32[]{:S(2)}, u32[]{:S(2)}) %collective-permute-start.41) | collective-permute-done | bytes 524320 | tf_op jit(solution)/shard_map/ppermute | solution.py:262
  773.2 5.4 all-to-all-start.3
  781.3 8.2 collective-permute-done.35
  793.8 13.2 %all-to-all-done.3 = bf16[8,64,768]{2,1,0:T(8,128)(2,1)} async-done(((bf16[8,64,768]{2,1,0:T(8,128)(2,1)}), bf16[8,64,768]{2,1,0:T(8,128)(2,1)}, u32[]{:S(2)}, u32[]{:S(2)}) %all-to-all-start.3) | async-done | bytes 786464 | tf_op jit(solution)/shard_map/all_to_all | solution.py:1018
  (292 shorter events, 204.5 us)
Async XLA Ops:
  11.3 67.8 %collective-permute-start = (bf16[256,2048]{1,0:T(8,128)(2,1)}, bf16[256,2048]{1,0:T(8,128)(2,1)}, u32[]{:S(2)}, u32[]{:S(2)}) collective-permute-start(bf16[256,2048]{1,0:T(8,128)(2,1)} %fusion.108), channel_id=1, source_target_pairs={{0,8},{4,0},{8,16},{12,4},{16,24},{20,12},{24,28},{28,20},{1,9},{5... | collective-permute-start | bytes 3145736 | tf_op jit(solution)/shard_map/ppermute | solution.py:243
  12.9 67.0 %collective-permute-start.1 = (bf16[256,2048]{1,0:T(8,128)(2,1)}, bf16[256,2048]{1,0:T(8,128)(2,1)}, u32[]{:S(2)}, u32[]{:S(2)}) collective-permute-start(bf16[256,2048]{1,0:T(8,128)(2,1)} %fusion.108), channel_id=1, source_target_pairs={{0,4},{4,12},{8,0},{12,20},{16,8},{20,28},{24,16},{28,24},{1,5},{5... | collective-permute-start | bytes 3145736 | tf_op jit(solution)/shard_map/ppermute | solution.py:244
  13.4 31.5 %collective-permute-start.14 = (s32[256]{0:T(256)S(1)}, s32[256]{0:T(256)S(1)}, u32[]{:S(2)}, u32[]{:S(2)}) collective-permute-start(s32[256]{0:T(256)S(1)} %bitcast.286), channel_id=1, source_target_pairs={{0,2},{1,3},{2,0},{3,1},{4,6},{5,7},{6,4},{7,5},{8,10},{9,11},{10,... | collective-permute-start | bytes 3080 | tf_op jit(solution)/shard_map/ppermute | solution.py:709
  17.6 68.6 %all-to-all-start = ((bf16[8,64,768]{2,1,0:T(8,128)(2,1)}), bf16[8,64,768]{2,1,0:T(8,128)(2,1)}, u32[]{:S(2)}, u32[]{:S(2)}) async-start(bf16[8,64,768]{2,1,0:T(8,128)(2,1)} %tile_reshape.3), calls=%async_computation | async-start | bytes 1572864 | tf_op jit(solution)/shard_map/all_to_all | solution.py:829
  24.0 92.6 %all-gather.3.cloned.1.call-start = ((), (), s32[]{:S(2)}) async-start(), calls=%async_computation.6 | async-start | bytes 2359296 | tf_op jit(solution)/shard_map/all_gather | solution.py:831
  27.6 37.7 %collective-permute-start.12 = (bf16[64,2048]{1,0:T(8,128)(2,1)}, bf16[64,2048]{1,0:T(8,128)(2,1)}, u32[]{:S(2)}, u32[]{:S(2)}) collective-permute-start(bf16[64,2048]{1,0:T(8,128)(2,1)} %get-tuple-element.103), channel_id=1, source_target_pairs={{0,10},{1,11},{2,8},{3,9},{4,14},{5,15},{6,12},{7,13},{8,2},{9,3},... | collective-permute-start | bytes 786440 | tf_op jit(solution)/shard_map/ppermute | solution.py:803
  44.9 32.8 %collective-permute-start.11 = (bf16[64,2048]{1,0:T(8,128)(2,1)}, bf16[64,2048]{1,0:T(8,128)(2,1)}, u32[]{:S(2)}, u32[]{:S(2)}) collective-permute-start(bf16[64,2048]{1,0:T(8,128)(2,1)} %get-tuple-element.104), channel_id=1, source_target_pairs={{0,8},{4,12},{8,0},{12,4},{16,24},{20,28},{24,16},{28,20},{1,9},{5... | collective-permute-start | bytes 786440 | tf_op jit(solution)/shard_map/ppermute | solution.py:709
  46.9 30.8 %collective-permute-start.10 = (bf16[64,2048]{1,0:T(8,128)(2,1)}, bf16[64,2048]{1,0:T(8,128)(2,1)}, u32[]{:S(2)}, u32[]{:S(2)}) collective-permute-start(bf16[64,2048]{1,0:T(8,128)(2,1)} %get-tuple-element.105), channel_id=1, source_target_pairs={{0,2},{1,3},{2,0},{3,1},{4,6},{5,7},{6,4},{7,5},{8,10},{9,11},{10,... | collective-permute-start | bytes 786440 | tf_op jit(solution)/shard_map/ppermute | solution.py:709
  65.4 86.5 %collective-permute-start.13 = (bf16[256,2048]{1,0:T(8,128)(2,1)}, bf16[256,2048]{1,0:T(8,128)(2,1)}, u32[]{:S(2)}, u32[]{:S(2)}) collective-permute-start(bf16[256,2048]{1,0:T(8,128)(2,1)} %bitcast.31.top_zero), channel_id=1, source_target_pairs={{0,2},{1,3},{2,0},{3,1},{4,6},{5,7},{6,4},{7,5},{8,10},{9,11},{10,... | collective-permute-start | bytes 3145736 | tf_op jit(solution)/shard_map/ppermute | solution.py:709
  79.1 29.1 %collective-permute-start.2 = (bf16[256,2048]{1,0:T(8,128)(2,1)}, bf16[256,2048]{1,0:T(8,128)(2,1)}, u32[]{:S(2)}, u32[]{:S(2)}) collective-permute-start(bf16[256,2048]{1,0:T(8,128)(2,1)} %collective-permute-done), channel_id=1, source_target_pairs={{0,8},{4,0},{8,16},{12,4},{16,24},{20,12},{24,28},{28,20},{1,9},{5... | collective-permute-start | bytes 3145736 | tf_op jit(solution)/shard_map/ppermute | solution.py:243
  79.9 29.2 %collective-permute-start.3 = (bf16[256,2048]{1,0:T(8,128)(2,1)}, bf16[256,2048]{1,0:T(8,128)(2,1)}, u32[]{:S(2)}, u32[]{:S(2)}) collective-permute-start(bf16[256,2048]{1,0:T(8,128)(2,1)} %collective-permute-done.1), channel_id=1, source_target_pairs={{0,4},{4,12},{8,0},{12,20},{16,8},{20,28},{24,16},{28,24},{1,5},{5... | collective-permute-start | bytes 3145736 | tf_op jit(solution)/shard_map/ppermute | solution.py:244
  86.2 26.4 %collective-permute-start.8 = (bf16[1,8,64,768]{3,2,1,0:T(8,128)(2,1)}, bf16[1,8,64,768]{3,2,1,0:T(8,128)(2,1)S(1)}, u32[]{:S(2)}, u32[]{:S(2)}) collective-permute-start(bf16[1,8,64,768]{3,2,1,0:T(8,128)(2,1)} %bitcast.21), channel_id=1, source_target_pairs={{0,1},{1,0},{2,3},{3,2},{4,5},{5,4},{6,7},{7,6},{8,9},{9,8},{10,11... | collective-permute-start | bytes 2359304 | tf_op jit(solution)/shard_map/ppermute | solution.py:709
  108.2 26.9 %collective-permute-start.4 = (bf16[256,2048]{1,0:T(8,128)(2,1)}, bf16[256,2048]{1,0:T(8,128)(2,1)}, u32[]{:S(2)}, u32[]{:S(2)}) collective-permute-start(bf16[256,2048]{1,0:T(8,128)(2,1)} %collective-permute-done.2), channel_id=1, source_target_pairs={{0,8},{4,0},{8,16},{12,4},{16,24},{20,12},{24,28},{28,20},{1,9},{5... | collective-permute-start | bytes 3145736 | tf_op jit(solution)/shard_map/ppermute | solution.py:243
  115.1 34.7 %collective-permute-start.9 = (bf16[2,8,64,768]{3,2,1,0:T(8,128)(2,1)}, bf16[2,8,64,768]{3,2,1,0:T(8,128)(2,1)}, u32[]{:S(2)}, u32[]{:S(2)}) collective-permute-start(bf16[2,8,64,768]{3,2,1,0:T(8,128)(2,1)} %pad_maximum_fusion.2), channel_id=1, source_target_pairs={{0,2},{1,3},{2,0},{3,1},{4,6},{5,7},{6,4},{7,5},{8,10},{9,11},{10,... | collective-permute-start | bytes 4718600 | tf_op jit(solution)/shard_map/ppermute | solution.py:709
  116.6 41.4 %collective-permute-start.22 = (bf16[1,8,64,2048]{3,2,0,1:T(8,128)(2,1)}, bf16[1,8,64,2048]{3,2,0,1:T(8,128)(2,1)S(1)}, u32[]{:S(2)}, u32[]{:S(2)}) collective-permute-start(bf16[1,8,64,2048]{3,2,0,1:T(8,128)(2,1)} %bitcast.273), channel_id=1, source_target_pairs={{0,1},{1,0},{2,3},{3,2},{4,5},{5,4},{6,7},{7,6},{8,9},{9,8},{10,11... | collective-permute-start | bytes 6291464 | tf_op jit(solution)/shard_map/ppermute | solution.py:709
  153.0 48.0 %collective-permute-start.17 = (bf16[4,64,2048]{2,1,0:T(8,128)(2,1)S(1)}, bf16[4,64,2048]{2,1,0:T(8,128)(2,1)S(1)}, u32[]{:S(2)}, u32[]{:S(2)}) collective-permute-start(bf16[4,64,2048]{2,1,0:T(8,128)(2,1)S(1)} %copy-done.19), channel_id=1, source_target_pairs={{0,4},{4,0},{8,12},{12,8},{16,20},{20,16},{24,28},{28,24},{1,5},{5... | collective-permute-start | bytes 3145736 | tf_op jit(solution)/shard_map/ppermute | solution.py:709
  153.7 47.2 %collective-permute-start.19 = (bf16[4,64,2048]{2,1,0:T(8,128)(2,1)S(1)}, bf16[4,64,2048]{2,1,0:T(8,128)(2,1)S(1)}, u32[]{:S(2)}, u32[]{:S(2)}) collective-permute-start(bf16[4,64,2048]{2,1,0:T(8,128)(2,1)S(1)} %copy-done.19), channel_id=1, source_target_pairs={{0,16},{4,20},{8,24},{12,28},{16,0},{20,4},{24,8},{28,12},{1,17},{... | collective-permute-start | bytes 3145736 | tf_op jit(solution)/shard_map/ppermute | solution.py:709
  156.2 44.8 %collective-permute-start.18 = (bf16[256,2048]{1,0:T(8,128)(2,1)S(1)}, bf16[256,2048]{1,0:T(8,128)(2,1)}, u32[]{:S(2)}, u32[]{:S(2)}) collective-permute-start(bf16[256,2048]{1,0:T(8,128)(2,1)S(1)} %copy-done.33), channel_id=1, source_target_pairs={{0,4},{4,0},{8,12},{12,8},{16,20},{20,16},{24,28},{28,24},{1,5},{5... | collective-permute-start | bytes 3145736 | tf_op jit(solution)/shard_map/ppermute | solution.py:709
  161.0 136.6 %collective-permute-start.23 = (bf16[2,8,64,2048]{3,2,0,1:T(8,128)(2,1)}, bf16[2,8,64,2048]{3,2,0,1:T(8,128)(2,1)}, u32[]{:S(2)}, u32[]{:S(2)}) collective-permute-start(bf16[2,8,64,2048]{3,2,0,1:T(8,128)(2,1)} %pad_maximum_fusion.1), channel_id=1, source_target_pairs={{0,2},{1,3},{2,0},{3,1},{4,6},{5,7},{6,4},{7,5},{8,10},{9,11},{10,... | collective-permute-start | bytes 12582920 | tf_op jit(solution)/shard_map/ppermute | solution.py:709
  205.2 44.3 %all-to-all-start.1 = ((bf16[8,1,256,256]{2,3,1,0:T(8,128)(2,1)}), bf16[8,1,256,256]{2,3,1,0:T(8,128)(2,1)}, u32[]{:S(2)}, u32[]{:S(2)}) async-start(bf16[8,1,256,256]{2,3,1,0:T(8,128)(2,1)} %copy.48), calls=%async_computation.1 | async-start | bytes 2097152 | tf_op jit(solution)/shard_map/all_to_all | solution.py:870
  209.8 39.6 %collective-permute-start.20 = (bf16[256,2048]{1,0:T(8,128)(2,1)}, bf16[256,2048]{1,0:T(8,128)(2,1)}, u32[]{:S(2)}, u32[]{:S(2)}) collective-permute-start(bf16[256,2048]{1,0:T(8,128)(2,1)} %bitcast.31.top_zero), channel_id=1, source_target_pairs={{0,8},{4,12},{8,0},{12,4},{16,24},{20,28},{24,16},{28,20},{1,9},{5... | collective-permute-start | bytes 3145736 | tf_op jit(solution)/shard_map/ppermute | solution.py:709
  210.0 39.5 %collective-permute-start.21 = (bf16[4,64,2048]{2,1,0:T(8,128)(2,1)}, bf16[4,64,2048]{2,1,0:T(8,128)(2,1)}, u32[]{:S(2)}, u32[]{:S(2)}) collective-permute-start(bf16[4,64,2048]{2,1,0:T(8,128)(2,1)} %copy-done.35), channel_id=1, source_target_pairs={{0,4},{4,0},{8,12},{12,8},{16,20},{20,16},{24,28},{28,24},{1,5},{5... | collective-permute-start | bytes 3145736 | tf_op jit(solution)/shard_map/ppermute | solution.py:709
  249.5 47.4 %collective-permute-start.25 = (bf16[256,2048]{1,0:T(8,128)(2,1)}, bf16[256,2048]{1,0:T(8,128)(2,1)}, u32[]{:S(2)}, u32[]{:S(2)}) collective-permute-start(bf16[256,2048]{1,0:T(8,128)(2,1)} %down_zero), channel_id=1, source_target_pairs={{0,16},{4,20},{8,24},{12,28},{16,0},{20,4},{24,8},{28,12},{1,17},{... | collective-permute-start | bytes 3145736 | tf_op jit(solution)/shard_map/ppermute | solution.py:709
  253.6 67.3 %collective-permute-start.24 = (bf16[256,2048]{1,0:T(8,128)(2,1)}, bf16[256,2048]{1,0:T(8,128)(2,1)}, u32[]{:S(2)}, u32[]{:S(2)}) collective-permute-start(bf16[256,2048]{1,0:T(8,128)(2,1)} %collective-permute-done.20.top_two), channel_id=1, source_target_pairs={{0,2},{1,3},{2,0},{3,1},{4,6},{5,7},{6,4},{7,5},{8,10},{9,11},{10,... | collective-permute-start | bytes 3145736 | tf_op jit(solution)/shard_map/ppermute | solution.py:709
  296.9 25.3 %collective-permute-start.26 = (bf16[256,2048]{1,0:T(8,128)(2,1)}, bf16[256,2048]{1,0:T(8,128)(2,1)}, u32[]{:S(2)}, u32[]{:S(2)}) collective-permute-start(bf16[256,2048]{1,0:T(8,128)(2,1)} %collective-permute-done.25.down_far), channel_id=1, source_target_pairs={{0,4},{4,0},{8,12},{12,8},{16,20},{20,16},{24,28},{28,24},{1,5},{5... | collective-permute-start | bytes 3145736 | tf_op jit(solution)/shard_map/ppermute | solution.py:709
  572.8 33.3 %all-to-all-start.2 = ((bf16[8,1,256,256]{3,2,1,0:T(8,128)(2,1)}), bf16[8,1,256,256]{3,2,1,0:T(8,128)(2,1)}, u32[]{:S(2)}, u32[]{:S(2)}) async-start(bf16[8,1,256,256]{3,2,1,0:T(8,128)(2,1)} %bitcast.269), calls=%async_computation.2 | async-start | bytes 2097152 | tf_op jit(solution)/shard_map/all_to_all | solution.py:993
  581.8 230.3 %reduce-scatter.2.cloned.1.call-start = ((), (), s32[]{:S(2)}) async-start(), calls=%async_computation.5 | async-start | bytes 2359296 | tf_op jit(solution)/shard_map/reduce_scatter | solution.py:1000
  592.9 53.7 %collective-permute-start.28 = (bf16[1,8,64,2048]{3,2,0,1:T(8,128)(2,1)}, bf16[1,8,64,2048]{3,2,0,1:T(8,128)(2,1)}, u32[]{:S(2)}, u32[]{:S(2)}) collective-permute-start(bf16[1,8,64,2048]{3,2,0,1:T(8,128)(2,1)} %dynamic-slice_convert_fusion.1), channel_id=1, source_target_pairs={{0,2},{1,3},{2,0},{3,1},{4,6},{5,7},{6,4},{7,5},{8,10},{9,11},{10,... | collective-permute-start | bytes 6291464 | tf_op jit(solution)/shard_map/ppermute | solution.py:709
  601.0 73.9 %collective-permute-start.47 = (bf16[64,2048]{1,0:T(8,128)(2,1)}, bf16[64,2048]{1,0:T(8,128)(2,1)}, u32[]{:S(2)}, u32[]{:S(2)}) collective-permute-start(bf16[64,2048]{1,0:T(8,128)(2,1)} %get-tuple-element.95), channel_id=1, source_target_pairs={{0,10},{1,11},{2,8},{3,9},{4,14},{5,15},{6,12},{7,13},{8,2},{9,3},... | collective-permute-start | bytes 786440 | tf_op jit(solution)/shard_map/ppermute | solution.py:803
  602.6 73.9 %collective-permute-start.46 = (bf16[64,2048]{1,0:T(8,128)(2,1)}, bf16[64,2048]{1,0:T(8,128)(2,1)}, u32[]{:S(2)}, u32[]{:S(2)}) collective-permute-start(bf16[64,2048]{1,0:T(8,128)(2,1)} %get-tuple-element.96), channel_id=1, source_target_pairs={{0,8},{4,12},{8,0},{12,4},{16,24},{20,28},{24,16},{28,20},{1,9},{5... | collective-permute-start | bytes 786440 | tf_op jit(solution)/shard_map/ppermute | solution.py:709
  694.3 37.8 %collective-permute-start.43 = (bf16[2,8,64,768]{3,2,1,0:T(8,128)(2,1)}, bf16[2,8,64,768]{3,2,1,0:T(8,128)(2,1)}, u32[]{:S(2)}, u32[]{:S(2)}) collective-permute-start(bf16[2,8,64,768]{3,2,1,0:T(8,128)(2,1)} %fusion.18), channel_id=1, source_target_pairs={{0,1},{1,0},{2,3},{3,2},{4,5},{5,4},{6,7},{7,6},{8,9},{9,8},{10,11... | collective-permute-start | bytes 4718600 | tf_op jit(solution)/shard_map/ppermute | solution.py:709
  773.2 33.9 %all-to-all-start.3 = ((bf16[8,64,768]{2,1,0:T(8,128)(2,1)}), bf16[8,64,768]{2,1,0:T(8,128)(2,1)}, u32[]{:S(2)}, u32[]{:S(2)}) async-start(bf16[8,64,768]{2,1,0:T(8,128)(2,1)} %fusion.30), calls=%async_computation.3 | async-start | bytes 1572864 | tf_op jit(solution)/shard_map/all_to_all | solution.py:1018
  (65 other events, 986.3 us)
Sparse Core Ops, SparseCore 0:
  27.8 64.8 all-gather.2
  724.5 80.6 reduce-scatter.1

commit v3 on v2

--- a/solution.py
+++ b/solution.py
@@ -15,6 +15,7 @@
 norm_eps = 1e-05
 rope_base = 10000.0
 masked_score = -1e30
+LOG2E = 1.4426950408889634
 f32 = jnp.float32
 bf16 = jnp.bfloat16
 
@@ -34,7 +35,7 @@
 def attend_kernel(heads, length, split_ref, limit_ref, proj_ref, cos_ref, sin_ref, qkv_ref, att_ref, low_ref, lse_ref):
     row = pl.program_id(0)
     split = split_ref[row]
-    scale = HEAD_DIM ** (-0.5)
+    scale = HEAD_DIM ** (-0.5) * LOG2E
     block = min(BLOCK, length)
     blocks = length // block
     width = heads * HEAD_DIM
@@ -70,8 +71,8 @@
                 ok = (kat <= at) & (kat >= low)
                 s = jnp.where(ok, s, masked_score)
                 new_top = jnp.maximum(top, jnp.max(s, axis=1, keepdims=True))
-                p = jnp.where(ok, jnp.exp(s - new_top), 0.0)
-                fade = jnp.exp(top - new_top)
+                p = jnp.exp2(s - new_top)
+                fade = jnp.exp2(top - new_top)
                 total = total * fade + jnp.sum(p, axis=1, keepdims=True)
                 acc = acc * fade + dot(p.astype(bf16), qkv_ref[keys, vcol], ((1,), (0,)))
                 return new_top, total, acc
@@ -92,7 +93,7 @@
             active = (limit_ref[row, 2] + h < limit).astype(f32)
             att_ref[rows, qcol] = att
             low_ref[rows, qcol] = (att * active).astype(bf16)
-            lse_ref[rows, qcol] = jnp.broadcast_to(top + jnp.log(total), (block, HEAD_DIM))
+            lse_ref[rows, qcol] = jnp.broadcast_to(top + jnp.log2(total), (block, HEAD_DIM))
             return carry
 
         lax.fori_loop(0, blocks, query_block, 0)
@@ -164,9 +165,9 @@
                 at = i * block + lax.broadcasted_iota(jnp.int32, (block, 1), 0)
                 low = first_key(split, at)
                 ok = (kat <= at) & (kat >= low)
-                s = dot(q, k, ((1,), (1,))) * scale
+                s = dot(q, k, ((1,), (1,))) * (scale * LOG2E)
                 lse = lse_ref[rows, qcol][:, :1]
-                p = jnp.where(ok, jnp.exp(s - lse), 0.0)
+                p = jnp.exp2(jnp.where(ok, s - lse, masked_score))
                 dp = dot(datt, v, ((1,), (1,)))
                 ds = (p * (dp - delta_ref[rows, :][:, :1])).astype(bf16)
                 dv = dv + dot(p.astype(bf16), datt, ((0,), (0,)))
@@ -370,9 +371,7 @@
     up_next,
     up_both,
     down_zero,
-    down_far,
     down_next,
-    down_both,
     mixed_own,
     mixed_come,
     dact_own,
@@ -390,15 +389,14 @@
     scale,
     hid,
     dpre,
-    relu,
     mixed,
     dact,
     mixed_low,
     dact_low,
     down_near,
     up_near,
-    down_held,
-    up_held,
+    held,
+    down_sum,
     load_sem,
     send_sem,
     recv_sem,
@@ -451,16 +449,18 @@
     loads = [load(act_ref, act.at[slot(0)], 0)]
     for k, top in enumerate((top_zero, top_one, top_two, top_three)):
         loads.append(load(top, dmix.at[slot(k)], 1 + k))
+    down_to_far = send(down_zero, down.at[core, x, far], FAR)
     weights = []
-    for k, (up_part, down_part) in enumerate(
-        ((up_zero, down_zero), (up_far, down_far), (up_next, down_next), (up_both, down_both))
-    ):
+    for k, up_part in enumerate((up_zero, up_far, up_next, up_both)):
         its_far = far + (1 - 2 * far) * (k % 2)
         its_x = x + (1 - 2 * x) * (k // 2)
         up_slot = up.at[its_far, :, its_x, :, core]
-        down_slot = down.at[core, its_x, its_far]
-        weights += [send(up_part, up_slot, CORE), send(down_part, down_slot, CORE)]
-        loads += [load(up_part, up_slot, 5 + 2 * k), load(down_part, down_slot, 6 + 2 * k)]
+        weights.append(send(up_part, up_slot, CORE))
+        loads.append(load(up_part, up_slot, 5 + k))
+    for k, down_part in enumerate((down_zero, down_next)):
+        down_slot = down.at[core, x + (1 - 2 * x) * k, far]
+        weights.append(send(down_part, down_slot, CORE))
+        loads.append(load(down_part, down_slot, 9 + k))
     scale[slot(0), :] = chosen_ref[...]
     for copy in loads:
         copy.wait()
@@ -478,124 +478,129 @@
     def columns(t):
         return pl.ds(pl.multiple_of(t * TILE, TILE), TILE)
 
-    def forward(pair):
-        group = pl.ds(pair * 2 * rows, 2 * rows)
+    def group_of(pair):
+        return pl.ds(pair * 2 * rows, 2 * rows)
+
+    def hidden_of(pair):
+        group = group_of(pair)
         width = width_ref[group, :]
 
         def scaled(i):
             at = pl.ds(pl.multiple_of(pair * 2 * rows + i * 32, 32), 32)
             dmix[at, :] = (dmix[at, :].astype(f32) * scale[at, :][:, :1]).astype(bf16)
 
-        each(2 * rows // 32, scaled)
-
-        def first(t, carry):
+        def first(t):
             at = columns(t)
             weight = up[:, :, :, :, :, :, at].reshape(dim, TILE)
             pre = jnp.maximum(dot(act[group, :], weight, ((1,), (0,))), 0.0)
             pre = jnp.where(need_ref[:, at] <= width, pre, 0.0)
-            relu[:, at] = pre.astype(bf16)
+            dpre[group, at] = pre.astype(bf16)
             hid[group, at] = (pre * pre).astype(bf16)
-            return carry
-
-        def second(t, carry):
+
+        each(2 * rows // 32, scaled)
+        each(dim // TILE, first)
+
+    def mixed_of(pair):
+        group = group_of(pair)
+
+        def second(t):
             at = columns(t)
             weight = down[:, :, :, :, at].reshape(dim, TILE)
-            value = dot(hid[group, :], weight, ((1,), (0,)))
-            mixed[group, at] = value.astype(bf16)
-            return carry
-
-        def third(t, carry):
+            mixed[group, at] = dot(hid[group, :], weight, ((1,), (0,))).astype(bf16)
+
+        each(dim // TILE, second)
+
+    def dact_of(pair):
+        group = group_of(pair)
+
+        def third(t):
             at = columns(t)
             weight = down[t // 2, t % 2].reshape(TILE, dim)
             value = dot(dmix[group, :], weight, ((1,), (1,)))
-            dpre[group, at] = (value * 2.0 * relu[:, at].astype(f32)).astype(bf16)
-            return carry
-
-        def fourth(t, carry):
+            dpre[group, at] = (value * 2.0 * dpre[group, at].astype(f32)).astype(bf16)
+
+        def fourth(t):
             at = columns(t)
             weight = up[t // 2, t % 2].reshape(TILE, dim)
-            value = dot(dpre[group, :], weight, ((1,), (1,)))
-            dact[group, at] = value.astype(bf16)
-            return carry
-
-        lax.fori_loop(0, dim // TILE, first, 0)
-        lax.fori_loop(0, dim // TILE, second, 0)
-        lax.fori_loop(0, dim // TILE, third, 0)
-        lax.fori_loop(0, dim // TILE, fourth, 0)
-
-    forward(0)
-    mixed_one = send(mixed.at[slot(1)], mixed_low.at[0], Y)
-    both_y.wait_recv()
-    both_z.wait_recv()
-    scale_both.wait_recv()
-    forward(1)
-    mixed_three = send(mixed.at[slot(3)], mixed_low.at[1], Y)
-    dact_two = send(dact.at[slot(2)], dact_low.at[0], Z)
-    dact_three = send(dact.at[slot(3)], dact_low.at[1], Z)
+            dact[group, at] = dot(dpre[group, :], weight, ((1,), (1,))).astype(bf16)
+
+        each(dim // TILE, third)
+        each(dim // TILE, fourth)
 
     cut = dim // 2
 
-    def down_terms(side):
-        at = pl.ds(side * cut, cut)
-
-        def block(k, carry):
-            rows_of = hid[:, pl.ds(pl.multiple_of(k * TILE, TILE), TILE)]
-            value = dot(rows_of, dmix[:, at], ((0,), (0,))).astype(bf16)
-            down[k // 2, k % 2, :, :, at] = value.reshape(2, TILE // 2, cut)
-            return carry
-
-        lax.fori_loop(0, dim // TILE, block, 0)
-
-    def up_terms(side):
-        at = pl.ds(side * cut, cut)
-
-        def block(k, carry):
-            rows_of = act[:, pl.ds(pl.multiple_of(k * TILE, TILE), TILE)]
-            value = dot(rows_of, dpre[:, at], ((0,), (0,))).astype(bf16)
-            up[k // 2, k % 2, :, :, :, :, at] = value.reshape(2, 2, 2, TILE // 8, cut)
-            return carry
-
-        lax.fori_loop(0, dim // TILE, block, 0)
-
-    cores = []
-    for side in range(2):
-        at = pl.ds(side * cut, cut)
-        down_terms(side)
-        cores.append(send(down.at[1 - core, :, :, :, at], down_core.at[side], CORE))
-    for side in range(2):
-        at = pl.ds(side * cut, cut)
-        up_terms(side)
-        cores.append(send(up.at[:, :, :, :, 1 - core, :, at], up_core.at[side], CORE))
+    def side_of(k):
+        return pl.ds((k % 2) * cut, cut)
+
+    def down_terms(k):
+        def block(i):
+            rows_of = hid[:, columns(i)]
+            value = dot(rows_of, dmix[:, side_of(k)], ((0,), (0,))).astype(bf16)
+            down_sum[i // 2, i % 2, :, :, :, :, side_of(k)] = value.reshape(2, 2, 2, TILE // 8, cut)
+
+        each(dim // TILE, block)
+        return send(down_sum.at[1 - core, :, :, :, :, :, side_of(k)], down_core.at[k], CORE)
+
+    def up_terms(k):
+        def block(i):
+            rows_of = act[:, columns(i)]
+            value = dot(rows_of, dpre[:, side_of(k)], ((0,), (0,))).astype(bf16)
+            up[i // 2, i % 2, :, :, :, :, side_of(k)] = value.reshape(2, 2, 2, TILE // 8, cut)
+
+        each(dim // TILE, block)
+        return send(up.at[:, :, :, :, 1 - core, :, side_of(k)], up_core.at[k % 2], CORE)
 
     def core_sum(k):
-        side = k % 2
-        at = pl.ds(side * cut, cut)
         cores[k].wait_recv()
-        source = (down_core if k < 2 else up_core).at[side]
-        copy = load(source, down_held if k < 2 else up_held, 13 + k)
-        copy.wait()
+        load((down_core if k < 2 else up_core).at[k % 2], held, 13 + k).wait()
+
+        def add(i):
+            a, b, c, d = i // 8, (i // 4) % 2, (i // 2) % 2, i % 2
+            come = held[a, b, c, d].astype(f32)
+            if k < 2:
+                here = down_sum[core, a, b, c, d, :, side_of(k)].astype(f32)
+                down_sum[core, a, b, c, d, :, side_of(k)] = (here + come).astype(bf16)
+            else:
+                here = up[a, b, c, d, core, :, side_of(k)].astype(f32)
+                up[a, b, c, d, core, :, side_of(k)] = (here + come).astype(bf16)
+
+        each(16, add)
         if k < 2:
-
-            def add_down(i):
-                a, b, part = i // 16, (i // 8) % 2, pl.ds(pl.multiple_of((i % 8) * 32, 32), 32)
-                here = down[core, a, b, part, at].astype(f32)
-                down[core, a, b, part, at] = (here + down_held[a, b, part, :].astype(f32)).astype(bf16)
-
-            each(32, add_down)
-            return send(down.at[core, 1 - x, :, :, at], down_near.at[:, :, at], X)
-
-        def add_up(i):
-            a, b, c, d = i // 8, (i // 4) % 2, (i // 2) % 2, i % 2
-            here = up[a, b, c, d, core, :, at].astype(f32)
-            up[a, b, c, d, core, :, at] = (here + up_held[a, b, c, d].astype(f32)).astype(bf16)
-
-        each(16, add_up)
-        return send(up.at[:, :, 1 - x, :, core, :, at], up_near.at[:, :, :, :, at], X)
-
-    nears = [core_sum(k) for k in range(4)]
-
-    mixed_one.wait_recv()
-    mixed_three.wait_recv()
+            source = down_sum.at[core, 1 - x, :, :, :, :, side_of(k)]
+            return send(source, down_near.at[:, :, :, :, side_of(k)], X)
+        source = up.at[:, :, 1 - x, :, core, :, side_of(k)]
+        return send(source, up_near.at[:, :, :, :, side_of(k)], X)
+
+    def near_sum(k):
+        nears[k].wait_recv()
+
+        def add(i):
+            a, b, c = i // 4, (i // 2) % 2, i % 2
+            if k < 2:
+                here = down_sum[core, x, a, b, c, :, side_of(k)].astype(f32)
+                come = down_near[a, b, c, :, side_of(k)].astype(f32)
+                down_sum[core, x, a, b, c, :, side_of(k)] = (here + come).astype(bf16)
+            else:
+                here = up[a, b, x, c, core, :, side_of(k)].astype(f32)
+                come = up_near[a, b, c, :, side_of(k)].astype(f32)
+                up[a, b, x, c, core, :, side_of(k)] = (here + come).astype(bf16)
+
+        each(8, add)
+        if k < 2:
+            fars.append(
+                send(
+                    down_sum.at[core, x, 1 - far, :, :, :, side_of(k)],
+                    down_come.at[:, :, :, side_of(k)],
+                    FAR,
+                )
+            )
+            source = down_sum.at[core, x, far, :, :, :, side_of(k)]
+            keep.append(load(source, down_own.at[:, :, :, side_of(k)], 19 + k))
+        else:
+            source = up.at[1 - far, :, x, :, core, :, side_of(k)]
+            fars.append(send(source, up_come.at[:, :, :, side_of(k)], FAR))
+            source = up.at[far, :, x, :, core, :, side_of(k)]
+            keep.append(load(source, up_own.at[:, :, :, side_of(k)], 19 + k))
 
     def add_low(total, k, low, side):
         def step(i):
@@ -605,41 +610,54 @@
 
         each(rows // 32, step)
 
+    cores, nears, fars, keep = [], [], [], []
+    hidden_of(0)
+    both_y.wait_recv()
+    both_z.wait_recv()
+    scale_both.wait_recv()
+    hidden_of(1)
+    down_to_far.wait_recv()
+    down_slot = down.at[core, x, 1 - far]
+    down_to_x = send(down_slot, down_slot, X)
+    down_to_core = send(down_slot, down_slot, CORE)
+    cores.append(down_terms(0))
+    cores.append(down_terms(1))
+    down_to_x.wait_recv()
+    down_slot = down.at[core, 1 - x, 1 - far]
+    down_last = send(down_slot, down_slot, CORE)
+    down_to_core.wait_recv()
+    down_last.wait_recv()
+    mixed_of(0)
+    mixed_one = send(mixed.at[slot(1)], mixed_low.at[0], Y)
+    nears.append(core_sum(0))
+    mixed_of(1)
+    mixed_three = send(mixed.at[slot(3)], mixed_low.at[1], Y)
+    nears.append(core_sum(1))
+    dact_of(1)
+    dact_two = send(dact.at[slot(2)], dact_low.at[0], Z)
+    dact_three = send(dact.at[slot(3)], dact_low.at[1], Z)
+    dact_of(0)
+    near_sum(0)
+    cores.append(up_terms(2))
+    cores.append(up_terms(3))
+    nears.append(core_sum(2))
+    nears.append(core_sum(3))
+
+    mixed_one.wait_recv()
+    mixed_three.wait_recv()
     add_low(mixed, 2, mixed_low, 1)
     mixed_last = send(mixed.at[slot(2)], mixed_come, Z)
+    near_sum(1)
     add_low(mixed, 0, mixed_low, 0)
-    keep = [load(mixed.at[slot(0)], mixed_own, 17)]
+    keep.append(load(mixed.at[slot(0)], mixed_own, 17))
     dact_two.wait_recv()
     dact_three.wait_recv()
     add_low(dact, 1, dact_low, 1)
     dact_last = send(dact.at[slot(1)], dact_come, Y)
     add_low(dact, 0, dact_low, 0)
     keep.append(load(dact.at[slot(0)], dact_own, 18))
-
-    fars = []
-    for k in range(4):
-        at = pl.ds((k % 2) * cut, cut)
-        nears[k].wait_recv()
-        if k < 2:
-
-            def add_down(i, at=at):
-                b, part = i // 8, pl.ds(pl.multiple_of((i % 8) * 32, 32), 32)
-                here = down[core, x, b, part, at].astype(f32)
-                down[core, x, b, part, at] = (here + down_near[b, part, at].astype(f32)).astype(bf16)
-
-            each(16, add_down)
-            fars.append(send(down.at[core, x, 1 - far, :, at], down_come.at[:, at], FAR))
-            keep.append(load(down.at[core, x, far, :, at], down_own.at[:, at], 19 + k))
-        else:
-
-            def add_up(i, at=at):
-                a, b, d = i // 4, (i // 2) % 2, i % 2
-                here = up[a, b, x, d, core, :, at].astype(f32)
-                up[a, b, x, d, core, :, at] = (here + up_near[a, b, d, :, at].astype(f32)).astype(bf16)
-
-            each(8, add_up)
-            fars.append(send(up.at[1 - far, :, x, :, core, :, at], up_come.at[:, :, :, at], FAR))
-            keep.append(load(up.at[far, :, x, :, core, :, at], up_own.at[:, :, :, at], 19 + k))
+    near_sum(2)
+    near_sum(3)
     for copy in keep:
         copy.wait()
     for copy in [mixed_last, dact_last] + fars:
@@ -661,18 +679,18 @@
 
     return pl.pallas_call(
         feed_kernel,
-        in_specs=[any_space] * 5 + [in_vmem] * 3 + [any_space] * 8,
+        in_specs=[any_space] * 5 + [in_vmem] * 3 + [any_space] * 6,
         out_specs=[any_space] * 10,
         out_shape=[
             shape(rows, dim),
             shape(rows, dim),
             shape(rows, dim),
             shape(rows, dim),
-            shape(dim // 8, dim),
-            shape(dim // 8, dim),
             shape(2, 2, shard, dim),
             shape(2, 2, shard, dim),
-            shape(2, 2, 2, dim // 8, cut),
+            shape(2, 2, shard, dim),
+            shape(2, 2, shard, dim),
+            shape(2, 2, 2, 2, 2, shard, cut),
             shape(2, 2, 2, 2, 2, shard, cut),
         ],
         scratch_shapes=[
@@ -683,15 +701,14 @@
             pltpu.VMEM((tokens, 128), f32),
             pltpu.VMEM((tokens, dim), bf16),
             pltpu.VMEM((tokens, dim), bf16),
-            pltpu.VMEM((2 * rows, dim), bf16),
             pltpu.VMEM((tokens, dim), bf16),
             pltpu.VMEM((tokens, dim), bf16),
             pltpu.VMEM((2, rows, dim), bf16),
             pltpu.VMEM((2, rows, dim), bf16),
-            pltpu.VMEM((2, dim // 8, dim), bf16),
             pltpu.VMEM((2, 2, 2, shard, dim), bf16),
-            pltpu.VMEM((2, 2, dim // 8, cut), bf16),
+            pltpu.VMEM((2, 2, 2, shard, dim), bf16),
             pltpu.VMEM((2, 2, 2, 2, shard, cut), bf16),
+            pltpu.VMEM((2, 2, 2, 2, 2, shard, dim), bf16),
             pltpu.SemaphoreType.DMA((23,)),
             pltpu.SemaphoreType.DMA((36,)),
             pltpu.SemaphoreType.DMA((36,)),
@@ -703,6 +720,639 @@
             flops=12 * tokens * dim * dim, bytes_accessed=2**25, transcendentals=0
         ),
     )(act, *tops, chosen, width_all, need, *ups, *downs)
+
+
+def ring_index(place):
+    place = place % 8
+    upper = place // 4
+    return (1 - upper) * 2 * place + upper * (2 * (7 - place) + 1)
+
+
+def first_kernel(
+    split_ref,
+    limit_ref,
+    tokens_ref,
+    gain_ref,
+    cos_ref,
+    sin_ref,
+    qkv_part,
+    out_part,
+    up_blocks,
+    down_part,
+    top_zero,
+    qkv,
+    att,
+    lse,
+    act_out,
+    weight_out,
+    low_out,
+    out_full,
+    up_zero,
+    up_far,
+    up_next,
+    up_both,
+    down_next,
+    top_one,
+    top_two,
+    top_three,
+    act,
+    weight,
+    low,
+    local_sem,
+    send_sem,
+    recv_sem,
+    qkv_send_sem,
+    qkv_recv_sem,
+    low_send_sem,
+    low_recv_sem,
+):
+    w = lax.axis_index("wide")
+    n = lax.axis_index("narrow")
+    core, y, far, z = n % 2, n // 2, w // 4, (w // 2) % 2
+    odd = w % 2
+    place = w // 2 + odd * (7 - 2 * (w // 2))
+    rows, dim = tokens_ref.shape
+    cols = weight.shape[3] // 3
+    heads = cols // HEAD_DIM
+    right, left = {"wide": ring_index(place + 1)}, {"wide": ring_index(place + 7)}
+    to_y, to_core = {"narrow": (n + 2) % 4}, {"narrow": n + 1 - 2 * core}
+    to_z, to_x = {"wide": w + 2 - 4 * z}, {"wide": w + 1 - 2 * odd}
+    to_far = {"wide": (w + 4) % 8}
+    to_both = {"wide": w + 2 - 4 * z, "narrow": (n + 2) % 4}
+    barrier = pltpu.get_barrier_semaphore()
+    peers = [{"wide": (w + k) % 8} for k in range(1, 8)] + [to_y, to_core, to_both]
+    for peer in peers:
+        pl.semaphore_signal(barrier, inc=1, device_id=peer, device_id_type=MESH)
+    pl.semaphore_wait(barrier, len(peers))
+    started, kept = [], []
+
+    def send(source, target, peer):
+        at = len(started)
+        copy = pltpu.make_async_remote_copy(
+            src_ref=source,
+            dst_ref=target,
+            send_sem=send_sem.at[at],
+            recv_sem=recv_sem.at[at],
+            device_id=peer,
+            device_id_type=MESH,
+        )
+        copy.start()
+        started.append(copy)
+        return copy
+
+    def keep(source, target):
+        copy = pltpu.make_async_copy(source, target, local_sem.at[len(kept)])
+        copy.start()
+        kept.append(copy)
+        return copy
+
+    def norm(i):
+        at = pl.ds(pl.multiple_of(i * 32, 32), 32)
+        value = tokens_ref[at, :].astype(f32)
+        inv = lax.rsqrt(jnp.mean(value * value, axis=-1, keepdims=True) + norm_eps)
+        act[w, at, :] = (value * inv * gain_ref[...]).astype(bf16)
+
+    each(rows // 32, norm)
+
+    first, second = pl.ds(0, rows // 2), pl.ds(rows // 2, rows // 2)
+    shard = out_part.shape[0]
+    out_first, out_second = pl.ds(0, shard // 2), pl.ds(shard // 2, shard // 2)
+    onward = send(act.at[w], act.at[w], right)
+    back = send(act.at[w], act.at[w], left)
+    exchanges = []
+    for k in range(1, 8):
+        target = (w + k) % 8
+        for part in range(3):
+            source = qkv_part.at[:, pl.ds(pl.multiple_of(part * dim + target * cols, cols), cols)]
+            copy = pltpu.make_async_remote_copy(
+                src_ref=source,
+                dst_ref=weight.at[w, n, :, pl.ds(part * cols, cols)],
+                send_sem=qkv_send_sem.at[k - 1, part],
+                recv_sem=qkv_recv_sem.at[k - 1, part],
+                device_id={"wide": target},
+                device_id_type=MESH,
+            )
+            copy.start()
+            exchanges.append(copy)
+    for part in range(3):
+        source = qkv_part.at[:, pl.ds(pl.multiple_of(part * dim + w * cols, cols), cols)]
+        keep(source, weight.at[w, n, :, pl.ds(part * cols, cols)])
+    out_onward = send(out_part, out_full.at[w, n], right)
+    out_back = send(out_part, out_full.at[w, n], left)
+    out_own = keep(out_part, out_full.at[w, n])
+    team = z * 2 + y
+    swaps = [
+        send(up_blocks.at[z * 2 + 1 - y], up_zero.at[team], to_y),
+        send(up_blocks.at[(1 - z) * 2 + y], up_zero.at[team], to_z),
+        send(up_blocks.at[(1 - z) * 2 + 1 - y], up_zero.at[team], to_both),
+    ]
+    up_own = keep(up_blocks.at[team], up_zero.at[team])
+
+    def ring_hop(step):
+        nonlocal onward, back, out_onward, out_back
+        behind, ahead = ring_index(place + 8 - step), ring_index(place + step)
+        onward.wait_recv()
+        back.wait_recv()
+        if step < 3:
+            onward = send(act.at[behind], act.at[behind], right)
+            back = send(act.at[ahead], act.at[ahead], left)
+        else:
+            onward = send(act.at[behind, first], act.at[behind, first], right)
+            back = send(act.at[ahead, second], act.at[ahead, second], left)
+        out_onward.wait_recv()
+        out_back.wait_recv()
+        if step < 3:
+            out_onward = send(out_full.at[behind, n], out_full.at[behind, n], right)
+            out_back = send(out_full.at[ahead, n], out_full.at[ahead, n], left)
+        else:
+            out_onward = send(out_full.at[behind, n, out_first], out_full.at[behind, n, out_first], right)
+            out_back = send(out_full.at[ahead, n, out_second], out_full.at[ahead, n, out_second], left)
+
+    def project(owner):
+        at = pl.ds(pl.multiple_of(owner * rows, rows), rows)
+        for part in range(3):
+            its = weight[:, :, :, pl.ds(part * cols, cols)].reshape(dim, cols)
+            value = dot(act[owner], its, ((1,), (0,)))
+            for h in range(heads):
+                piece = value[:, h * HEAD_DIM : (h + 1) * HEAD_DIM]
+                if part < 2:
+                    piece = turn(piece, cos_ref[at, :], sin_ref[at, :])
+                qkv[at, pl.ds(part * cols + h * HEAD_DIM, HEAD_DIM)] = piece.astype(bf16)
+
+    def project_pair(step):
+        each(2, lambda i: project(ring_index(place + 8 - step + 2 * step * i)))
+
+    for copy in kept[:3]:
+        copy.wait()
+    for copy in exchanges:
+        copy.wait_recv()
+    weight_y = send(weight.at[:, n], weight.at[:, n], to_y)
+    ring_hop(1)
+    weight_y.wait_recv()
+    weight_core = [
+        send(weight.at[:, n], weight.at[:, n], to_core),
+        send(weight.at[:, (n + 2) % 4], weight.at[:, (n + 2) % 4], to_core),
+    ]
+    beside = send(top_zero, top_one, to_y)
+    for copy in weight_core:
+        copy.wait_recv()
+    each(1, lambda i: project(w + i))
+    project_pair(1)
+    ring_hop(2)
+    project_pair(2)
+    ring_hop(3)
+    for copy in swaps:
+        copy.wait_recv()
+    up_own.wait()
+    up_to_far = send(up_zero, up_far, to_far)
+    up_to_x = send(up_zero, up_next, to_x)
+    down_to_x = send(down_part, down_next, to_x)
+    project_pair(3)
+    onward.wait_recv()
+    back.wait_recv()
+    project(ring_index(place + 4))
+    out_onward.wait_recv()
+    out_back.wait_recv()
+    out_own.wait()
+    out_y = send(out_full.at[:, n], out_full.at[:, n], to_y)
+    across = send(top_zero, top_two, to_z)
+    keep(act, act_out)
+    keep(weight, weight_out)
+
+    split = split_ref[0]
+    factor = HEAD_DIM ** (-0.5) * LOG2E
+    block = 2 * rows
+    limit_one, limit_two, head_first = limit_ref[0, 0], limit_ref[0, 1], limit_ref[0, 2]
+
+    def low_send(target):
+        return pltpu.make_async_remote_copy(
+            src_ref=low.at[pl.ds(target * rows, rows)],
+            dst_ref=low_out.at[:, pl.ds(pl.multiple_of(w * cols, cols), cols)],
+            send_sem=low_send_sem.at[target],
+            recv_sem=low_recv_sem.at[w],
+            device_id={"wide": target},
+            device_id_type=MESH,
+        )
+
+    def low_come(source):
+        return pltpu.make_async_remote_copy(
+            src_ref=low.at[pl.ds(source * rows, rows)],
+            dst_ref=low_out.at[:, pl.ds(source * cols, cols)],
+            send_sem=low_send_sem.at[source],
+            recv_sem=low_recv_sem.at[source],
+            device_id={"wide": source},
+            device_id_type=MESH,
+        )
+
+    def low_keep(target):
+        return pltpu.make_async_copy(
+            low.at[pl.ds(target * rows, rows)],
+            low_out.at[:, pl.ds(target * cols, cols)],
+            low_send_sem.at[target],
+        )
+
+    for i in range(4):
+        at_rows = pl.ds(i * block, block)
+        at = i * block + lax.broadcasted_iota(jnp.int32, (block, 1), 0)
+        lowest = jnp.where(at >= split, split, 0)
+
+        def keys_of(j, state, diagonal):
+            keys = pl.ds(pl.multiple_of(j * block, block), block)
+            kat = j * block + lax.broadcasted_iota(jnp.int32, (block, block), 1)
+            ok = kat >= lowest
+            if diagonal:
+                ok = ok & (kat <= at)
+            found = []
+            for h in range(heads):
+                top, total, acc = state[h]
+                q = qkv[at_rows, pl.ds(h * HEAD_DIM, HEAD_DIM)]
+                k = qkv[keys, pl.ds(cols + h * HEAD_DIM, HEAD_DIM)]
+                v = qkv[keys, pl.ds(2 * cols + h * HEAD_DIM, HEAD_DIM)]
+                s = jnp.where(ok, dot(q, k, ((1,), (1,))) * factor, masked_score)
+                new_top = jnp.maximum(top, jnp.max(s, axis=1, keepdims=True))
+                p = jnp.exp2(s - new_top)
+                fade = jnp.exp2(top - new_top)
+                total = total * fade + jnp.sum(p, axis=1, keepdims=True)
+                acc = acc * fade + dot(p.astype(bf16), v, ((1,), (0,)))
+                found.append((new_top, total, acc))
+            return tuple(found)
+
+        start = (
+            jnp.full((block, 1), masked_score, f32),
+            jnp.zeros((block, 1), f32),
+            jnp.zeros((block, HEAD_DIM), f32),
+        )
+        state = (start,) * heads
+        if i:
+            state = lax.fori_loop(0, i, functools.partial(keys_of, diagonal=False), state)
+        state = keys_of(i, state, True)
+        limit = jnp.where(at < split, limit_one, limit_two)
+        for h in range(heads):
+            top, total, acc = state[h]
+            value = acc / total
+            head = pl.ds(h * HEAD_DIM, HEAD_DIM)
+            active = (head_first + h < limit).astype(f32)
+            att[at_rows, head] = value
+            low[at_rows, head] = (value * active).astype(bf16)
+            lse[at_rows, head] = jnp.broadcast_to(top + jnp.log2(total), (block, HEAD_DIM))
+        for target in (2 * i, 2 * i + 1):
+
+            @pl.when(w != target)
+            def _():
+                low_send(target).start()
+
+            @pl.when(w == target)
+            def _():
+                low_keep(target).start()
+
+        if i == 2:
+            out_y.wait_recv()
+            out_core = [
+                send(out_full.at[:, n], out_full.at[:, n], to_core),
+                send(out_full.at[:, (n + 2) % 4], out_full.at[:, (n + 2) % 4], to_core),
+            ]
+    across.wait_recv()
+    both = send(top_two, top_three, to_y)
+    up_to_far.wait_recv()
+    up_to_both = send(up_far, up_both, to_x)
+    for copy in out_core + [beside, both, up_to_x, up_to_both, down_to_x]:
+        copy.wait_recv()
+    for target in range(8):
+
+        @pl.when(w != target)
+        def _():
+            low_send(target).wait_send()
+            low_come(target).wait_recv()
+
+        @pl.when(w == target)
+        def _():
+            low_keep(target).wait()
+
+    for copy in kept[3:]:
+        if copy is not up_own and copy is not out_own:
+            copy.wait()
+    for copy in started + exchanges:
+        copy.wait_send()
+
+
+def first_sums(split, limits, tokens, gain, cos2, sin2, w_qkv, w_out, up_blocks, w_down, top):
+    rows, dim = tokens.shape
+    length = 8 * rows
+    shard, wide_cols = w_qkv.shape
+    cols = wide_cols // 24
+    any_space = pl.BlockSpec(memory_space=pl.ANY)
+    in_vmem = pl.BlockSpec(memory_space=pltpu.VMEM)
+    smem = pl.BlockSpec(memory_space=pltpu.SMEM)
+    dma = pltpu.SemaphoreType.DMA
+
+    def shape(*dims):
+        return jax.ShapeDtypeStruct(dims, bf16)
+
+    flops = 6 * length * dim * cols + 4 * length * length * cols
+    return pl.pallas_call(
+        first_kernel,
+        in_specs=[smem] * 2 + [in_vmem] * 4 + [any_space] * 5,
+        out_specs=[in_vmem] * 3 + [any_space] * 12,
+        out_shape=[
+            shape(length, 3 * cols),
+            jax.ShapeDtypeStruct((length, cols), f32),
+            jax.ShapeDtypeStruct((length, cols), f32),
+            shape(8, rows, dim),
+            shape(8, 4, shard, 3 * cols),
+            shape(rows, dim),
+            shape(8, 4, shard, dim),
+            shape(4, shard, dim),
+            shape(4, shard, dim),
+            shape(4, shard, dim),
+            shape(4, shard, dim),
+            shape(*w_down.shape),
+            shape(rows, dim),
+            shape(rows, dim),
+            shape(rows, dim),
+        ],
+        scratch_shapes=[
+            pltpu.VMEM((8, rows, dim), bf16),
+            pltpu.VMEM((8, 4, shard, 3 * cols), bf16),
+            pltpu.VMEM((length, cols), bf16),
+            dma((8,)),
+            dma((32,)),
+            dma((32,)),
+            dma((7, 3)),
+            dma((7, 3)),
+            dma((8,)),
+            dma((8,)),
+        ],
+        compiler_params=pltpu.CompilerParams(
+            collective_id=2, has_side_effects=True, vmem_limit_bytes=56 * 2**20
+        ),
+        cost_estimate=pl.CostEstimate(flops=flops, bytes_accessed=2**25, transcendentals=2**22),
+    )(split, limits, tokens, gain, cos2, sin2, w_qkv, w_out, up_blocks, w_down, top)
+
+
+STRIP = 128
+
+
+def last_kernel(
+    dproj,
+    weight,
+    act_ref,
+    out_terms,
+    small_ref,
+    base_ref,
+    tokens_ref,
+    inv_ref,
+    gain_ref,
+    input_grad,
+    out_grad,
+    qkv_grad,
+    small_out,
+    act_grad,
+    qkv_come,
+    act,
+    terms,
+    core_come,
+    side_come,
+    act_send,
+    act_recv,
+    out_send,
+    out_recv,
+    small_sum,
+    small_recv,
+    load_sem,
+    ring_send_sem,
+    ring_recv_sem,
+    send_sem,
+    recv_sem,
+):
+    w = lax.axis_index("wide")
+    n = lax.axis_index("narrow")
+    core, y = n % 2, n // 2
+    odd = w % 2
+    place = w // 2 + odd * (7 - 2 * (w // 2))
+    dim = weight.shape[0]
+    half = dim // 2
+    rows = act_grad.shape[0]
+    shard = out_grad.shape[0]
+    aims = ({"wide": ring_index(place + 1)}, {"wide": ring_index(place + 7)})
+    other_core = {"narrow": n + 1 - 2 * core}
+    other_y = {"narrow": (n + 2) % 4}
+    others = [{"wide": (w + k) % 8} for k in range(1, 8)]
+    barrier = pltpu.get_barrier_semaphore()
+    for peer in others + [other_core, other_y]:
+        pl.semaphore_signal(barrier, inc=1, device_id=peer, device_id_type=MESH)
+    pl.semaphore_wait(barrier, len(others) + 2)
+    load = pltpu.make_async_copy(act_ref, act, load_sem)
+    load.start()
+    started = []
+
+    def send(source, target, peer):
+        at = len(started)
+        copy = pltpu.make_async_remote_copy(
+            src_ref=source,
+            dst_ref=target,
+            send_sem=send_sem.at[at],
+            recv_sem=recv_sem.at[at],
+            device_id=peer,
+            device_id_type=MESH,
+        )
+        copy.start()
+        started.append(copy)
+        return copy
+
+    def hop(step, stream):
+        if stream < 4:
+            source, target, side = act_send.at[step, stream], act_recv.at[step, stream], stream // 2
+        else:
+            source, target, side = out_send.at[step, stream - 4], out_recv.at[step, stream - 4], stream - 4
+        return pltpu.make_async_remote_copy(
+            src_ref=source,
+            dst_ref=target,
+            send_sem=ring_send_sem.at[step, stream],
+            recv_sem=ring_recv_sem.at[step, stream],
+            device_id=aims[side],
+            device_id_type=MESH,
+        )
+
+    def owner_of(step, side):
+        return ring_index(place + 7 - step) if side == 0 else ring_index(place + 1 + step)
+
+    def ring_step(step):
+        for stream in range(4):
+            side, strip = stream // 2, stream % 2
+            owner = owner_of(step, side)
+            at = pl.ds(pl.multiple_of(owner * rows + strip * STRIP, STRIP), STRIP)
+            for part in range(2):
+                cols = pl.ds(part * 512, 512)
+                wide_cols = pl.ds(side * half + part * 512, 512)
+                value = dot(dproj[at, :], weight[wide_cols, :], ((1,), (1,)))
+                if step == 0:
+                    act_send[0, stream, :, cols] = value.astype(bf16)
+                elif step < 7:
+                    act_send[step, stream, :, cols] = value.astype(bf16)
+                else:
+                    act_grad[pl.ds(strip * STRIP, STRIP), wide_cols] = value
+            if step > 0:
+                hop(step - 1, stream).wait_recv()
+
+                def add(i):
+                    part = pl.ds(pl.multiple_of(i * 32, 32), 32)
+                    come = act_recv[step - 1, stream, part, :].astype(f32)
+                    if step < 7:
+                        act_send[step, stream, part, :] = (
+                            act_send[step, stream, part, :].astype(f32) + come
+                        ).astype(bf16)
+                    else:
+                        row = pl.ds(pl.multiple_of(strip * STRIP + i * 32, 32), 32)
+                        act_grad[row, pl.ds(side * half, half)] += come
+
+                each(STRIP // 32, add)
+            if step < 7:
+                hop(step, stream).start()
+        for stream in (4, 5):
+            side = stream - 4
+            value = out_terms[owner_of(step, side), :, pl.ds(side * half, half)]
+            if step > 0:
+                hop(step - 1, stream).wait_recv()
+                value = value.astype(f32) + out_recv[step - 1, side].astype(f32)
+            if step < 7:
+                out_send[step, side] = value.astype(bf16)
+                hop(step, stream).start()
+            else:
+                out_grad[:, pl.ds(side * half, half)] = value
+
+    ring_step(0)
+    load.wait()
+    small_sum[0] = small_ref[...]
+
+    def weight_terms(k):
+        at = pl.ds(pl.multiple_of(k * rows, rows), rows)
+        value = dot(act[:, at], dproj[...], ((0,), (0,)))
+        product = value * weight[at, :].astype(f32)
+        ones = jnp.ones((8, product.shape[1]), f32)
+        sums = lax.dot_general(
+            ones, product, (((1,), (1,)), ((), ())), precision=highest, preferred_element_type=f32
+        )
+        small_sum[0, 0:1, at] = small_sum[0, 0:1, at] + sums[0:1]
+        terms[k] = value.astype(bf16).reshape(2, 2, shard, value.shape[1])
+
+    each(8, weight_terms)
+    to_core = send(terms.at[:, :, 1 - core], core_come, other_core)
+
+    small_peers = [other_core, other_y] + [{"wide": w + b - 2 * b * ((w // b) % 2)} for b in (1, 2, 4)]
+
+    def small_step(k):
+        if k:
+            pending.pop().wait_recv()
+            small_sum[k] = small_sum[k - 1] + small_recv[k - 1]
+        if k < 5:
+            pending.append(send(small_sum.at[k], small_recv.at[k], small_peers[k]))
+        else:
+            small_out[...] = small_sum[k]
+
+    pending = []
+    small_step(0)
+    ring_step(1)
+    to_core.wait_recv()
+
+    def add_core(i):
+        a, b = i // 2, i % 2
+        here = terms[a, b, core].astype(f32)
+        terms[a, b, core] = (here + core_come[a, b].astype(f32)).astype(bf16)
+
+    each(16, add_core)
+    to_side = send(terms.at[:, 1 - y, core], side_come, other_y)
+    small_step(1)
+    ring_step(2)
+    small_step(2)
+    ring_step(3)
+    to_side.wait_recv()
+
+    def add_side(i):
+        here = terms[i, y, core].astype(f32)
+        terms[i, y, core] = (here + side_come[i].astype(f32)).astype(bf16)
+
+    each(8, add_side)
+    own = pltpu.make_async_copy(terms.at[w, y, core], qkv_come.at[w], load_sem)
+    own.start()
+    blocks = []
+    for k, peer in enumerate(others):
+        target = (w + 1 + k) % 8
+        blocks.append(send(terms.at[target, y, core], qkv_come.at[w], peer))
+    small_step(3)
+    ring_step(4)
+    small_step(4)
+    ring_step(5)
+    small_step(5)
+    ring_step(6)
+    ring_step(7)
+
+    def finish(i):
+        at = pl.ds(pl.multiple_of(i * 32, 32), 32)
+        inv = inv_ref[at, :]
+        normed = tokens_ref[at, :].astype(f32) * inv
+        scaled = act_grad[at, :] * gain_ref[...]
+        mean = jnp.mean(scaled * normed, axis=-1, keepdims=True)
+        input_grad[at, :] = base_ref[at, :] + inv * (scaled - normed * mean)
+
+    each(rows // 32, finish)
+    own.wait()
+    for copy in blocks:
+        copy.wait_recv()
+    cols = weight.shape[1] // 3
+    for k in range(8):
+        for part in range(3):
+            value = qkv_come[k, :, pl.ds(part * cols, cols)].astype(f32)
+            qkv_grad[:, pl.ds(part * dim + k * cols, cols)] = value
+    for copy in started:
+        copy.wait_send()
+    for step in range(7):
+        for stream in range(6):
+            hop(step, stream).wait_send()
+
+
+def last_sums(dproj, weight, act, out_terms, small, base, tokens_in, inv, gain):
+    tokens, cols = dproj.shape
+    dim = weight.shape[0]
+    rows, shard, half = tokens // 8, dim // 32, dim // 2
+    any_space = pl.BlockSpec(memory_space=pl.ANY)
+    in_vmem = pl.BlockSpec(memory_space=pltpu.VMEM)
+    dma = pltpu.SemaphoreType.DMA
+    return pl.pallas_call(
+        last_kernel,
+        in_specs=[in_vmem, in_vmem, any_space] + [in_vmem] * 6,
+        out_specs=[in_vmem] * 4,
+        out_shape=[
+            jax.ShapeDtypeStruct((rows, dim), f32),
+            jax.ShapeDtypeStruct((shard, dim), f32),
+            jax.ShapeDtypeStruct((shard, 3 * dim), f32),
+            jax.ShapeDtypeStruct((8, dim), f32),
+        ],
+        scratch_shapes=[
+            pltpu.VMEM((rows, dim), f32),
+            pltpu.VMEM((8, shard, cols), bf16),
+            pltpu.VMEM((tokens, dim), bf16),
+            pltpu.VMEM((8, 2, 2, shard, cols), bf16),
+            pltpu.VMEM((8, 2, shard, cols), bf16),
+            pltpu.VMEM((8, shard, cols), bf16),
+            pltpu.VMEM((7, 4, STRIP, half), bf16),
+            pltpu.VMEM((7, 4, STRIP, half), bf16),
+            pltpu.VMEM((7, 2, shard, half), bf16),
+            pltpu.VMEM((7, 2, shard, half), bf16),
+            pltpu.VMEM((6, 8, dim), f32),
+            pltpu.VMEM((5, 8, dim), f32),
+            dma,
+            dma((7, 6)),
+            dma((7, 6)),
+            dma((16,)),
+            dma((16,)),
+        ],
+        compiler_params=pltpu.CompilerParams(
+            collective_id=1, has_side_effects=True, vmem_limit_bytes=60 * 2**20
+        ),
+        cost_estimate=pl.CostEstimate(
+            flops=4 * tokens * cols * dim, bytes_accessed=2**24, transcendentals=0
+        ),
+    )(dproj, weight, act, out_terms, small, base, tokens_in, inv, gain)
 
 
 def swap(array, axis, size, bits):
@@ -761,13 +1411,12 @@
 
     def narrow_scatter(array):
         for bits in [2**k for k in range(narrow.bit_length() - 1)]:
-            array = array.reshape((-1, 2) + array.shape[1:])
+            array = array.reshape((wide, -1, 2) + array.shape[2:])
             at = (n_at // bits) & 1
-            others = lax.dynamic_index_in_dim(array, 1 - at, 1, keepdims=False)
-            array = lax.dynamic_index_in_dim(array, at, 1, keepdims=False)
-            come = swap(others.astype(bf16), "narrow", narrow, bits)
-            array = array + come.astype(f32)
-        return array[0]
+            others = lax.dynamic_index_in_dim(array, 1 - at, 2, keepdims=False)
+            array = lax.dynamic_index_in_dim(array, at, 2, keepdims=False)
+            array = array + swap(others, "narrow", narrow, bits)
+        return array[:, 0]
 
     shares = wide
     upper = wide // 4
@@ -824,64 +1473,83 @@
     act_one = (normed_one * gain_one).astype(bf16)
 
     shard = w_qkv.shape[0]
-    blocks = w_qkv.reshape(shard, 3, head_groups, cols).transpose(2, 0, 1, 3)
-    blocks = jnp.tile(blocks.reshape(head_groups, shard, 3 * cols), (row_groups, 1, 1))
-    blocks = lax.all_to_all(blocks, "wide", 0, 0, tiled=True)
-    my_qkv = narrow_gather(blocks).transpose(1, 0, 2, 3).reshape(dim, 3 * cols)
-    out_parts = narrow_gather(lax.all_gather(w_out, "wide", axis=0, tiled=False))
-    out_full = out_parts.transpose(1, 0, 2, 3).reshape(dim, dim)
-
     piece_rows = w_down.shape[0]
     up_blocks = w_up.reshape(shard, upper, 2, 2, 2, 2, piece_rows).transpose(2, 4, 0, 5, 3, 1, 6)
-    up_part = team_swap(up_blocks.reshape(4, shard, shares * piece_rows))
+    up_blocks = up_blocks.reshape(4, shard, shares * piece_rows)
     top = out_grad.reshape(count, dim)
-    top_beside = beside(top)
     width_flat = width_choice.reshape(count)
     width_across = across(width_flat)
     width_all = jnp.concatenate([width_flat, beside(width_flat), width_across, beside(width_across)])
 
-    act_all = jnp.zeros((my_rows, wide, part_len, dim), bf16)
-    for owner, piece in ring.gather(act_one.reshape(count, dim)):
-        piece = pick_rows(piece.reshape(rows, part_len, dim))
-        act_all = lax.dynamic_update_slice(act_all, piece[:, None], (0, owner, 0, 0))
-    act_flat = act_all.reshape(my_rows * length, dim)
-    act_flat, my_qkv, up_part, top_beside, width_all, down_part, top = join(
-        act_flat, my_qkv, up_part, top_beside, width_all, w_down, top
-    )
-
-    up_found = [((0, 0), up_part)]
-    down_found = [((0, 0), down_part)]
-
-    def spread(found, bit):
-        return found + [((w ^ bit, n), swap(piece, "wide", wide, bit)) for (w, n), piece in found]
-
-    for bit in upper_bits:
-        up_found = spread(up_found, bit)
-    up_near = ((1, 0), swap(up_part, "wide", wide, 1))
-    down_near = ((1, 0), swap(down_part, "wide", wide, 1))
-    proj = dot(act_flat, my_qkv, ((1,), (0,))).reshape(my_rows, length, 3 * cols)
-    qkv, att, att_part, lse = attend(proj, split, limits, cos2, sin2, my_heads)
-    sends = att_part.reshape(my_rows, wide, part_len, cols).transpose(1, 0, 2, 3)
-    joined = join(sends, up_near[1], down_near[1], *[piece for _, piece in up_found])
-    sends = joined[0]
-    up_near, down_near = (up_near[0], joined[1]), (down_near[0], joined[2])
-    up_found = [(at, piece) for (at, _), piece in zip(up_found, joined[3:])]
-
-    come = lax.all_to_all(sends, "wide", 0, 0, tiled=True)
-    up_far = [((w ^ 1, n), swap(piece, "wide", wide, 1)) for (w, n), piece in up_found[1:]]
-    top_across = across(top)
-    joined = join(come, top_across, down_part, *[piece for _, piece in up_far])
-    come, top_across, down_part = joined[:3]
-    up_found = up_found + [up_near] + [(at, piece) for (at, _), piece in zip(up_far, joined[3:])]
-    come = come.reshape(row_groups, head_groups, my_rows, part_len, cols)
-    att_low = come.transpose(0, 2, 3, 1, 4).reshape(count, dim)
-
-    down_found = [((0, 0), down_part)]
-    for bit in upper_bits:
-        down_found = spread(down_found, bit)
-    down_far = [((w ^ 1, n), swap(piece, "wide", wide, 1)) for (w, n), piece in down_found[1:]]
-    down_found = down_found + [down_near] + down_far
-    top_both = beside(top_across)
+    kernels = wide == 8 and narrow == 4 and rows == 1
+    if kernels:
+        qkv, att, lse, act_flat, my_qkv, att_low, out_full, *found = first_sums(
+            split,
+            limits,
+            tokens.reshape(count, dim),
+            gain_one[None],
+            cos2,
+            sin2,
+            w_qkv,
+            w_out,
+            up_blocks,
+            w_down,
+            top,
+        )
+        qkv, att, lse = qkv[None], att[None], lse[None]
+        act_flat = act_flat.reshape(length, dim)
+        my_qkv = my_qkv.reshape(dim, 3 * cols)
+        out_full = out_full.reshape(dim, dim)
+        ups, downs = found[:4], [w_down, found[4]]
+        tops = (top, *found[5:])
+    else:
+        blocks = w_qkv.reshape(shard, 3, head_groups, cols).transpose(2, 0, 1, 3)
+        blocks = jnp.tile(blocks.reshape(head_groups, shard, 3 * cols), (row_groups, 1, 1))
+        blocks = lax.all_to_all(blocks, "wide", 0, 0, tiled=True)
+        my_qkv = narrow_gather(blocks).transpose(1, 0, 2, 3).reshape(dim, 3 * cols)
+        out_parts = narrow_gather(lax.all_gather(w_out, "wide", axis=0, tiled=False))
+        out_full = out_parts.transpose(1, 0, 2, 3).reshape(dim, dim)
+
+        up_part = team_swap(up_blocks)
+        top_beside = beside(top)
+        act_all = jnp.zeros((my_rows, wide, part_len, dim), bf16)
+        for owner, piece in ring.gather(act_one.reshape(count, dim)):
+            piece = pick_rows(piece.reshape(rows, part_len, dim))
+            act_all = lax.dynamic_update_slice(act_all, piece[:, None], (0, owner, 0, 0))
+        act_flat = act_all.reshape(my_rows * length, dim)
+        act_flat, my_qkv, up_part, top_beside, down_part, top = join(
+            act_flat, my_qkv, up_part, top_beside, w_down, top
+        )
+
+        up_found = [((0, 0), up_part)]
+
+        def spread(found, bit):
+            return found + [((w ^ bit, n), swap(piece, "wide", wide, bit)) for (w, n), piece in found]
+
+        for bit in upper_bits:
+            up_found = spread(up_found, bit)
+        up_near = ((1, 0), swap(up_part, "wide", wide, 1))
+        down_near = ((1, 0), swap(down_part, "wide", wide, 1))
+        proj = dot(act_flat, my_qkv, ((1,), (0,))).reshape(my_rows, length, 3 * cols)
+        qkv, att, att_part, lse = attend(proj, split, limits, cos2, sin2, my_heads)
+        sends = att_part.reshape(my_rows, wide, part_len, cols).transpose(1, 0, 2, 3)
+        sends, down_part = join(sends, down_part)
+
+        come = lax.all_to_all(sends, "wide", 0, 0, tiled=True)
+        down_found = [((0, 0), down_part)]
+        for bit in upper_bits:
+            down_found = spread(down_found, bit)
+        come, out_full = join(come, out_full)
+        up_far = [((w ^ 1, n), swap(piece, "wide", wide, 1)) for (w, n), piece in up_found[1:]]
+        up_found = up_found + [up_near] + up_far
+        top_across = across(top)
+        come = come.reshape(row_groups, head_groups, my_rows, part_len, cols)
+        att_low = come.transpose(0, 2, 3, 1, 4).reshape(count, dim)
+
+        down_far = [((w ^ 1, n), swap(piece, "wide", wide, 1)) for (w, n), piece in down_found[1:]]
+        down_found = down_found + [down_near] + down_far
+        top_both = beside(top_across)
+        tops = (top, top_beside, top_across, top_both)
     x_one = inputs.reshape(count, dim) + dot(att_low, out_full, ((1,), (0,)))
 
     center = x_one - jnp.mean(x_one, axis=-1, keepdims=True)
@@ -912,20 +1580,19 @@
             array = pick(array, at) + swap(pick(array, 1 - at), "wide", wide, bit)
         return array[0]
 
-    tops = (top, top_beside, top_across, top_both)
-    if wide == 8 and narrow == 4:
+    if kernels:
         mixed, mixed_come, grad_act_two, dact_come, down_grad, down_come, up_sum, up_come, _, _ = feed_forward(
             act_two,
             tops,
             jnp.broadcast_to(chosen[:, None], (count, 128)),
             width_all[:, None].astype(f32),
             need.astype(f32),
-            [piece.reshape(2, 2, shard, shares * piece_rows) for _, piece in up_found],
-            [piece for _, piece in down_found],
+            [piece.reshape(2, 2, shard, shares * piece_rows) for piece in ups],
+            downs,
         )
         mixed = mixed.astype(f32) + mixed_come.astype(f32)
         grad_act_two = grad_act_two.astype(f32) + dact_come.astype(f32)
-        down_grad = down_grad.astype(f32) + down_come.astype(f32)
+        down_grad = (down_grad.astype(f32) + down_come.astype(f32)).reshape(piece_rows, dim)
         up_sum = up_sum + up_come
         up_sum = up_sum.reshape(4, shard, shares * piece_rows)
     else:
@@ -993,47 +1660,61 @@
     come = lax.all_to_all(sends, "wide", 0, 0, tiled=True)
     dat = come.transpose(1, 0, 2, 3).reshape(my_rows, length, cols)
     dproj = attend_back(qkv, att, lse, dat, split, limits, cos2, sin2, my_heads)
-    grad_out = dot(att_low, grad_branch, ((0,), (0,)))
-    grad_out = grad_out.reshape(wide, narrow, shard, dim).transpose(1, 0, 2, 3)
-    grad_out = narrow_scatter(grad_out).astype(bf16).reshape(wide * shard, dim)
+    grad_out = dot(att_low, grad_branch, ((0,), (0,))).astype(bf16)
+    grad_out = narrow_scatter(grad_out.reshape(wide, narrow, shard, dim))
     dproj, act_flat, grad_out = join(dproj, act_flat, grad_out)
-    out_proj_grad = lax.psum_scatter(grad_out, "wide", scatter_dimension=0, tiled=True).astype(f32)
     up_sum = team_swap(up_sum)
     up_grad = up_sum.reshape(2, 2, shard, 2, 2, upper, piece_rows).transpose(2, 5, 0, 4, 1, 3, 6)
     up_grad = up_grad.reshape(shard, hidden).astype(f32)
-    half = dim // 2
-
-    def one_term(owner, side):
-        rows_of = lax.dynamic_slice_in_dim(dproj, owner * part_len, part_len, 1)
-        rows_of = rows_of.reshape(my_rows * part_len, 3 * cols)
-        term = dot(rows_of, my_qkv[side * half : (side + 1) * half], ((1,), (1,)))
-        return put_rows(term.reshape(my_rows, part_len, half)).reshape(count, half)
-
-    grad_act_one = jnp.concatenate(ring.scatter(one_term), axis=1)
-
-    grad_qkv = dot(act_flat, dproj.reshape(my_rows * length, 3 * cols), ((0,), (0,)))
-    gain_one_part = jnp.sum(grad_qkv * my_qkv.astype(f32), axis=1) / gain_one
-    grad_qkv = grad_qkv.reshape(wide, narrow, shard, 3 * cols).transpose(1, 0, 2, 3)
-    grad_qkv = narrow_scatter(grad_qkv).astype(bf16)
-    grad_qkv = lax.all_to_all(grad_qkv, "wide", 0, 0, tiled=True).astype(f32)
-    grad_qkv = jnp.sum(grad_qkv.reshape(row_groups, head_groups, shard, 3, cols), axis=0)
-    qkv_grad = grad_qkv.transpose(1, 2, 0, 3).reshape(shard, 3 * dim)
-
     normed_flat = normed_one.reshape(count, dim)
-    grad_scaled = grad_act_one * gain_one
-    input_grad = grad_x_one + inv_one.reshape(count, 1) * (
-        grad_scaled - normed_flat * jnp.mean(grad_scaled * normed_flat, axis=-1, keepdims=True)
-    )
-    small = jnp.concatenate(
-        [gain_one_part, grad_gain_two, grad_bias_two, grad_router.T.reshape(-1), jnp.sum(onehot, axis=0)]
-    )
-    for bits in (1, 2):
-        small = small + swap(small, "narrow", narrow, bits)
-    for bits in [2**k for k in range(wide.bit_length() - 1)]:
-        small = small + swap(small, "wide", wide, bits)
-    gain_one_grad, gain_two_grad, bias_two_grad = (small[k * dim : (k + 1) * dim] for k in range(3))
-    router_grad = small[3 * dim : (3 + WIDTHS) * dim].reshape(WIDTHS, dim).T
-    counts_all = small[(3 + WIDTHS) * dim :]
+    counts = jnp.pad(jnp.sum(onehot, axis=0), (0, dim - WIDTHS))[None]
+    small = [grad_gain_two[None], grad_bias_two[None], grad_router.T, counts]
+
+    if kernels:
+        small = jnp.concatenate([jnp.zeros((1, dim), f32)] + small)
+        input_grad, out_proj_grad, qkv_grad, small = last_sums(
+            dproj[0],
+            my_qkv,
+            act_flat,
+            grad_out,
+            small,
+            grad_x_one,
+            tokens.reshape(count, dim),
+            inv_one.reshape(count, 1),
+            gain_one[None],
+        )
+    else:
+        half = dim // 2
+
+        def one_term(owner, side):
+            rows_of = lax.dynamic_slice_in_dim(dproj, owner * part_len, part_len, 1)
+            rows_of = rows_of.reshape(my_rows * part_len, 3 * cols)
+            term = dot(rows_of, my_qkv[side * half : (side + 1) * half], ((1,), (1,)))
+            return put_rows(term.reshape(my_rows, part_len, half)).reshape(count, half)
+
+        out_proj_grad = lax.psum_scatter(
+            grad_out.reshape(wide * shard, dim), "wide", scatter_dimension=0, tiled=True
+        ).astype(f32)
+        grad_act_one = jnp.concatenate(ring.scatter(one_term), axis=1)
+        grad_qkv = dot(act_flat, dproj.reshape(my_rows * length, 3 * cols), ((0,), (0,)))
+        gain_one_part = jnp.sum(grad_qkv * my_qkv.astype(f32), axis=1)
+        small = jnp.concatenate([gain_one_part[None]] + small)
+        grad_qkv = narrow_scatter(grad_qkv.astype(bf16).reshape(wide, narrow, shard, 3 * cols))
+        grad_qkv = lax.all_to_all(grad_qkv, "wide", 0, 0, tiled=True).astype(f32)
+        for bits in (1, 2):
+            small = small + swap(small, "narrow", narrow, bits)
+        for bits in [2**k for k in range(wide.bit_length() - 1)]:
+            small = small + swap(small, "wide", wide, bits)
+        grad_qkv = jnp.sum(grad_qkv.reshape(row_groups, head_groups, shard, 3, cols), axis=0)
+        qkv_grad = grad_qkv.transpose(1, 2, 0, 3).reshape(shard, 3 * dim)
+        grad_scaled = grad_act_one * gain_one
+        input_grad = grad_x_one + inv_one.reshape(count, 1) * (
+            grad_scaled - normed_flat * jnp.mean(grad_scaled * normed_flat, axis=-1, keepdims=True)
+        )
+    gain_one_grad = small[0] / gain_one
+    gain_two_grad, bias_two_grad = small[1], small[2]
+    router_grad = small[3 : 3 + WIDTHS].T
+    counts_all = small[3 + WIDTHS, :WIDTHS]
     return (
         block_out.reshape(rows, part_len, dim),
         input_grad.reshape(rows, part_len, dim),

time: 831 us -> 750 us (0.903)
  Pallas kernels: 281 us -> 632 us
  waiting for transfers between devices: 209 us -> 4.44 us
  starting transfers between devices: 84.3 us -> 16 us
  matrix products: 66.9 us -> 21.9 us
  other arithmetic: 71 us -> 27.6 us
  between operations: 36 us -> 2.1 us
  local copies, waits for them, and re-layouts: 72.7 us -> 41 us
    pallas_call x1 -> x2, Pallas kernels: 27.7 us -> 350 us  [the longest x1 211 us: first_sums(): pl.pallas_call(first_kernel, in_specs=[smem] * 2 + [in_vmem] * 4 + [any_s...]
    ppermute x29 -> x7, waiting for transfers between devices: 115 us -> 2.44 us  [swap(): return lax.ppermute(array, axis, [(i, i ^ bits) for i in range(size)])]
    ppermute x22 -> x0, waiting for transfers between devices: 79.2 us -> none  [the longest x14 39.4 us: scatter(): come = lax.ppermute(sums[side].astype(bf16), self.axis, perm)]
    dot_general x21 -> x3, matrix products: 59.2 us -> 14.3 us  [dot(): lax.dot_general(a, b, (contract, ((), ())), preferred_element_type=f32)]
    pallas_call x1, Pallas kernels: 220 us -> 248 us  [feed_forward(): pl.pallas_call(feed_kernel, in_specs=[any_space] * 5 + [in_vmem] * 3 + [a...]
    ppermute x22 -> x0, starting transfers between devices: 25.9 us -> none  [the longest x14 16 us: scatter(): come = lax.ppermute(sums[side].astype(bf16), self.axis, perm)]
    ppermute x29 -> x7, starting transfers between devices: 31.2 us -> 10.7 us  [swap(): return lax.ppermute(array, axis, [(i, i ^ bits) for i in range(size)])]
    dynamic_update_slice x6 -> x0, local copies, waits for them, and re-layouts: 13.9 us -> none  [on_device(): lax.dynamic_update_slice(act_all, piece[:, None], (0, owner, 0, 0))]
  transfers between devices with their start and end apart: 59 -> 9, of which waited for: 23 -> 2; matrix products, arithmetic and copies ran while one was open for 21% -> 7% of each run, Pallas kernels for 7% -> 33%
where the time goes in v3:
time: 750 us; the launch traced here: 745 us
  Pallas kernels  632 us (84%)
  local copies, waits for them, and re-layouts  41 us (5%)
  other arithmetic  27.6 us (4%)
  matrix products  21.9 us (3%)
  starting transfers between devices  16 us (2%)
    pallas_call x1, Pallas kernels, feed_forward(): pl.pallas_call(feed_kernel, in_specs=[any_space] * 5 + [in_vmem] * 3 + [a...  248 us
    pallas_call x1, Pallas kernels, first_sums(): pl.pallas_call(first_kernel, in_specs=[smem] * 2 + [in_vmem] * 4 + [any_s...  211 us
    pallas_call x1, Pallas kernels, last_sums(): pl.pallas_call(last_kernel, in_specs=[in_vmem, in_vmem, any_space] + [in_...  140 us
    pallas_call x1, Pallas kernels, attend_back(): pl.pallas_call(functools.partial(attend_back_kernel, heads, length), grid...  33.4 us
  transfers between devices with their start and end apart: 9, of which 2 were waited for; matrix products, arithmetic and copies ran while one was open for 7% of the time, Pallas kernels for 33%

profile of v3, /device:TPU:8, one launch (start us, length us, event | category | flops | bytes accessed | tf_op | source)
XLA Modules:
  0.0 745.1 jit_solution(6086595395119687494)
XLA Ops:
  0.7 2.0 collective-permute-start
  2.7 3.9 fusion.15
  7.3 2.8 reshape.429
  10.1 3.3 copy.67
  13.4 2.6 reshape.430.up_blocks
  16.6 2.0 pad_maximum_fusion
  18.5 210.5 %shard_map.212 = (bf16[2048,768]{1,0:T(8,128)(2,1)}, f32[2048,256]{1,0:T(8,128)}, f32[2048,256]{1,0:T(8,128)}, bf16[8,256,2048]{2,1,0:T(8,128)(2,1)}, bf16[8,4,6...) custom-call(s32[1]{0:T(128)S(6)} %copy.71.split_ref, ...), custom_call_target="tpu_custom_call" | custom-call | flops 10737418240 | bytes 33554432 | tf_op jit(solution)/shard_map/pallas_call | solution.py:1052
  229.1 6.1 fusion.36
  237.4 2.0 fusion.37
  241.4 2.4 collective-permute-done.2
  245.6 248.4 %shard_map.213 = (bf16[256,2048]{1,0:T(8,128)(2,1)}, bf16[256,2048]{1,0:T(8,128)(2,1)}, bf16[256,2048]{1,0:T(8,128)(2,1)}, bf16[256,2048]{1,0:T(8,128)(2,1)}, bf...) custom-call(bf16[256,2048]{1,0:T(8,128)(2,1)} %fusion.5.act_ref, ...), custom_call_target="tpu_custom_call" | custom-call | flops 51539607552 | bytes 33554432 | tf_op jit(solution)/shard_map/pallas_call | solution.py:680
  494.1 2.2 fusion.2
  496.5 4.2 multiply_reduce_fusion
  500.8 2.2 convert_add_fusion
  503.0 2.4 convolution_convert_fusion
  505.4 3.2 constant_dynamic-slice_fusion.7
  508.6 2.3 copy.64
  513.9 1.8 add.244
  515.8 1.8 collective-permute-start.5
  517.6 3.2 collective-permute-start.6
  520.8 5.7 convolution_convert_fusion.1
  528.2 5.2 all-to-all-start
  533.4 3.9 fusion
  540.1 1.9 collective-permute-start.4
  546.9 2.8 reshape.446
  549.6 2.7 copy.65
  552.4 2.7 reshape.445
  555.1 2.0 all-to-all-done
  558.1 33.4 %shard_map.214 = bf16[1,2048,768]{2,1,0:T(8,128)(2,1)} custom-call(s32[1]{0:T(128)S(6)} %copy.71.split_ref, s32[1,3]{1,0:T(1,128)} %pad_add_fusion.limit_ref, bf16[1,2048,768]{2,1,0:T(8,128)(2,1)} %bitcast.125, f32[1,2048,256]{2,1,0:T(8,128)} %bitcast.127, f32[1,2048,256]{2,1,0:T(8,128)} %bitcast.128, bf16[1,2048,256]{2,1,0:T(8,128)(2,1)} %bitcast.97, ...), custom_call_target="tpu_custom_call" | custom-call | flops 10737418240 | bytes 16777216 | tf_op jit(solution)/shard_map/pallas_call | solution.py:206
  591.4 3.2 add_bitcast_fusion.out_terms
  594.6 139.7 %shard_map.215 = (f32[256,2048]{1,0:T(8,128)}, f32[64,2048]{1,0:T(8,128)}, f32[64,6144]{1,0:T(8,128)}, f32[8,2048]{1,0:T(8,128)}) custom-call(bf16[2048,768]{1,0:T(8,128)(2,1)} %bitcast.126, bf16[2048,768]{1,0:T(8,128)(2,1)} %bitcast.124, bf16[2048,2048]{1,0:T(8,128)(2,1)} %bitcast.121, bf16[8,64,2048]{2,1,0:T(8,128)(2,1)} %add_bitcast_fusion.out_terms, ...), custom_call_target="tpu_custom_call" | custom-call | flops 12884901888 | bytes 16777216 | tf_op jit(solution)/shard_map/pallas_call | solution.py:1320
  739.2 3.3 copy.72
  (102 shorter events, 27.1 us)
Async XLA Ops:
  0.6 236.8 %copy-start = (f32[2048,4]{0,1:T(4,128)S(1)}, f32[2048,4]{0,1:T(4,128)}, u32[]{:S(2)}) copy-start(f32[2048,4]{0,1:T(4,128)} %param.19) | copy-start | bytes 98308
  0.7 239.5 %collective-permute-start.1 = (s32[256]{0:T(256)}, s32[256]{0:T(256)S(1)}, u32[]{:S(2)}, u32[]{:S(2)}) collective-permute-start(s32[256]{0:T(256)} %bitcast.105), channel_id=1, source_target_pairs={{0,8},{4,12},{8,0},{12,4},{16,24},{20,28},{24,16},{28,20},{1,9},{5... | collective-permute-start | bytes 3080 | tf_op jit(solution)/shard_map/ppermute | solution.py:1359
  0.7 240.7 %collective-permute-start = (s32[256]{0:T(256)}, s32[256]{0:T(256)S(1)}, u32[]{:S(2)}, u32[]{:S(2)}) collective-permute-start(s32[256]{0:T(256)} %bitcast.106), channel_id=1, source_target_pairs={{0,2},{1,3},{2,0},{3,1},{4,6},{5,7},{6,4},{7,5},{8,10},{9,11},{10,... | collective-permute-start | bytes 3080 | tf_op jit(solution)/shard_map/ppermute | solution.py:1359
  10.1 5.9 copy-start.24
  18.5 210.5 %copy-start.15 = (bf16[1,256,2048]{2,1,0:T(8,128)(2,1)S(1)}, bf16[1,256,2048]{2,1,0:T(8,128)(2,1)}, u32[]{:S(2)}) copy-start(bf16[1,256,2048]{2,1,0:T(8,128)(2,1)} %param.13) | copy-start | bytes 3145732
  235.2 2.2 copy-start.2
  236.0 5.3 copy-start.22
  240.2 3.6 collective-permute-start.2
  245.6 248.4 %copy-start.9 = (bf16[1,256,2048]{2,1,0:T(8,128)(2,1)S(1)}, bf16[1,256,2048]{2,1,0:T(8,128)(2,1)}, u32[]{:S(2)}) copy-start(bf16[1,256,2048]{2,1,0:T(8,128)(2,1)} %param.25) | copy-start | bytes 3145732
  494.0 2.2 copy-start.3
  494.0 2.5 copy-start.25
  496.5 4.3 copy-start.10
  496.5 4.3 copy-start.11
  500.8 2.2 copy-start.12
  503.0 2.4 copy-start.7
  508.6 5.3 copy-start.14
  510.9 22.5 %collective-permute-start.3 = (bf16[8,2,64,2048]{3,2,0,1:T(8,128)(2,1)}, bf16[8,2,64,2048]{3,2,0,1:T(8,128)(2,1)}, u32[]{:S(2)}, u32[]{:S(2)}) collective-permute-start(bf16[8,2,64,2048]{3,2,0,1:T(8,128)(2,1)} %bitcast.82), channel_id=1, source_target_pairs={{0,1},{1,0},{2,3},{3,2},{4,5},{5,4},{6,7},{7,6},{8,9},{9,8},{10,11... | collective-permute-start | bytes 12582920 | tf_op jit(solution)/shard_map/ppermute | solution.py:1359
  513.9 6.9 copy-start.8
  515.8 30.6 %collective-permute-start.5 = (bf16[64,2048]{1,0:T(8,128)(2,1)S(1)}, bf16[64,2048]{1,0:T(8,128)(2,1)S(1)}, u32[]{:S(2)}, u32[]{:S(2)}) collective-permute-start(bf16[64,2048]{1,0:T(8,128)(2,1)S(1)} %get-tuple-element.89), channel_id=1, source_target_pairs={{0,2},{1,3},{2,0},{3,1},{4,6},{5,7},{6,4},{7,5},{8,10},{9,11},{10,... | collective-permute-start | bytes 786440 | tf_op jit(solution)/shard_map/ppermute | solution.py:1359
  517.6 28.8 %collective-permute-start.6 = (bf16[64,2048]{1,0:T(8,128)(2,1)S(1)}, bf16[64,2048]{1,0:T(8,128)(2,1)S(1)}, u32[]{:S(2)}, u32[]{:S(2)}) collective-permute-start(bf16[64,2048]{1,0:T(8,128)(2,1)S(1)} %get-tuple-element.88), channel_id=1, source_target_pairs={{0,8},{4,12},{8,0},{12,4},{16,24},{20,28},{24,16},{28,20},{1,9},{5... | collective-permute-start | bytes 786440 | tf_op jit(solution)/shard_map/ppermute | solution.py:1359
  520.8 25.6 %collective-permute-start.7 = (bf16[64,2048]{1,0:T(8,128)(2,1)S(1)}, bf16[64,2048]{1,0:T(8,128)(2,1)S(1)}, u32[]{:S(2)}, u32[]{:S(2)}) collective-permute-start(bf16[64,2048]{1,0:T(8,128)(2,1)S(1)} %get-tuple-element.87), channel_id=1, source_target_pairs={{0,10},{1,11},{2,8},{3,9},{4,14},{5,15},{6,12},{7,13},{8,2},{9,3},... | collective-permute-start | bytes 786440 | tf_op jit(solution)/shard_map/ppermute | solution.py:1452
  528.2 28.9 %all-to-all-start = ((bf16[8,1,256,256]{3,2,1,0:T(8,128)(2,1)}), bf16[8,1,256,256]{3,2,1,0:T(8,128)(2,1)S(1)}, u32[]{:S(2)}, u32[]{:S(2)}) async-start(bf16[8,1,256,256]{3,2,1,0:T(8,128)(2,1)} %bitcast.84), calls=%async_computation | async-start | bytes 2097152 | tf_op jit(solution)/shard_map/all_to_all | solution.py:1660
  537.3 2.8 copy-start.5
  537.3 4.7 copy-start.17
  537.3 4.7 copy-start.18
  540.1 51.3 %collective-permute-start.4 = (bf16[8,1,64,2048]{3,2,0,1:T(8,128)(2,1)}, bf16[8,1,64,2048]{3,2,0,1:T(8,128)(2,1)}, u32[]{:S(2)}, u32[]{:S(2)}) collective-permute-start(bf16[8,1,64,2048]{3,2,0,1:T(8,128)(2,1)} %constant_dynamic-slice_fusion.5), channel_id=1, source_target_pairs={{0,2},{1,3},{2,0},{3,1},{4,6},{5,7},{6,4},{7,5},{8,10},{9,11},{10,... | collective-permute-start | bytes 6291464 | tf_op jit(solution)/shard_map/ppermute | solution.py:1359
  542.1 2.2 copy-start.4
  558.1 33.4 %copy-start.6 = (bf16[8,2,64,2048]{3,2,0,1:T(8,128)(2,1)S(1)}, bf16[8,2,64,2048]{3,2,0,1:T(8,128)(2,1)}, u32[]{:S(2)}) copy-start(bf16[8,2,64,2048]{3,2,0,1:T(8,128)(2,1)} %copy-done.5) | copy-start | bytes 12582916
  594.6 144.0 %copy-start.23 = (f32[2048]{0:T(1024)S(1)}, f32[2048]{0:T(1024)}, u32[]{:S(2)}) copy-start(f32[2048]{0:T(1024)} %param.14) | copy-start | bytes 24580
  739.2 3.3 copy-start.13
  739.2 5.5 copy-start.1
  742.4 1.4 copy-start.19
  (3 other events, 2.5 us)

commit v4 on v3

--- a/solution.py
+++ b/solution.py
@@ -2,6 +2,7 @@
 
 import jax
 import jax.numpy as jnp
+import numpy as np
 from jax import lax
 from jax.experimental import pallas as pl
 from jax.experimental.pallas import tpu as pltpu
@@ -358,24 +359,28 @@
 
 
 def feed_kernel(
-    act_ref,
+    act_many,
     top_zero,
     top_one,
     top_two,
     top_three,
-    chosen_ref,
-    width_ref,
-    need_ref,
-    up_zero,
-    up_far,
-    up_next,
-    up_both,
+    scale,
+    ups,
+    downs,
     down_zero,
-    down_next,
-    mixed_own,
-    mixed_come,
-    dact_own,
-    dact_come,
+    x_ref,
+    low_ref,
+    out_ref,
+    coef_ref,
+    router_ref,
+    small,
+    block_out,
+    grad_x,
+    branch,
+    dat_out,
+    out_own,
+    out_come,
+    out_other,
     down_own,
     down_come,
     up_own,
@@ -386,7 +391,6 @@
     down,
     act,
     dmix,
-    scale,
     hid,
     dpre,
     mixed,
@@ -397,9 +401,18 @@
     up_near,
     held,
     down_sum,
+    mixed_come,
+    dact_come,
+    x_one,
     load_sem,
     send_sem,
     recv_sem,
+    dat_send_sem,
+    dat_recv_sem,
+    out_send_sem,
+    out_recv_sem,
+    side_send_sem,
+    side_recv_sem,
 ):
     w = lax.axis_index("wide")
     n = lax.axis_index("narrow")
@@ -411,8 +424,7 @@
         X: {"wide": w + 1 - 2 * x},
         FAR: {"wide": (w + 4) % 8},
     }
-    rows = act_ref.shape[0]
-    dim = act_ref.shape[1]
+    rows, dim = x_ref.shape
     started = []
 
     def send(source, target, peer):
@@ -438,42 +450,25 @@
         return pl.ds(k * rows, rows)
 
     barrier = pltpu.get_barrier_semaphore()
-    for peer in peers.values():
+    others = [{"wide": (w + k) % 8} for k in range(1, 8)]
+    for peer in others + [peers[Y], peers[CORE]]:
         pl.semaphore_signal(barrier, inc=1, device_id=peer, device_id_type=MESH)
-    pl.semaphore_wait(barrier, len(peers))
-
-    to_y = send(act_ref, act.at[slot(1)], Y)
-    to_z = send(act_ref, act.at[slot(2)], Z)
-    scale_y = send(chosen_ref, scale.at[slot(1)], Y)
-    scale_z = send(chosen_ref, scale.at[slot(2)], Z)
-    loads = [load(act_ref, act.at[slot(0)], 0)]
+    pl.semaphore_wait(barrier, len(others) + 2)
+
+    loads = [load(act_many, act, 0)]
     for k, top in enumerate((top_zero, top_one, top_two, top_three)):
         loads.append(load(top, dmix.at[slot(k)], 1 + k))
-    down_to_far = send(down_zero, down.at[core, x, far], FAR)
-    weights = []
-    for k, up_part in enumerate((up_zero, up_far, up_next, up_both)):
-        its_far = far + (1 - 2 * far) * (k % 2)
-        its_x = x + (1 - 2 * x) * (k // 2)
-        up_slot = up.at[its_far, :, its_x, :, core]
-        weights.append(send(up_part, up_slot, CORE))
-        loads.append(load(up_part, up_slot, 5 + k))
-    for k, down_part in enumerate((down_zero, down_next)):
-        down_slot = down.at[core, x + (1 - 2 * x) * k, far]
-        weights.append(send(down_part, down_slot, CORE))
-        loads.append(load(down_part, down_slot, 9 + k))
-    scale[slot(0), :] = chosen_ref[...]
-    for copy in loads:
+    up_loads, down_loads = [], []
+    for its in range(2):
+        its_core = core + (1 - 2 * core) * its
+        for k in range(4):
+            its_far = far + (1 - 2 * far) * (k % 2)
+            its_x = x + (1 - 2 * x) * (k // 2)
+            source = downs.at[its, k] if its or k else down_zero
+            up_loads.append(load(ups.at[its, k], up.at[its_far, :, its_x, :, its_core], 27 + 4 * its + k))
+            down_loads.append(load(source, down.at[its_core, its_x, its_far], 35 + 4 * its + k))
+    for copy in loads + up_loads:
         copy.wait()
-    for copy in weights:
-        copy.wait_recv()
-    half = rows // 2
-    to_y.wait_recv()
-    to_z.wait_recv()
-    scale_y.wait_recv()
-    scale_z.wait_recv()
-    both_y = send(act.at[pl.ds(2 * rows, half)], act.at[pl.ds(3 * rows, half)], Y)
-    both_z = send(act.at[pl.ds(rows + half, half)], act.at[pl.ds(3 * rows + half, half)], Z)
-    scale_both = send(scale.at[slot(2)], scale.at[slot(3)], Y)
 
     def columns(t):
         return pl.ds(pl.multiple_of(t * TILE, TILE), TILE)
@@ -483,7 +478,7 @@
 
     def hidden_of(pair):
         group = group_of(pair)
-        width = width_ref[group, :]
+        width = scale[group, :][:, 1:2]
 
         def scaled(i):
             at = pl.ds(pl.multiple_of(pair * 2 * rows + i * 32, 32), 32)
@@ -493,7 +488,7 @@
             at = columns(t)
             weight = up[:, :, :, :, :, :, at].reshape(dim, TILE)
             pre = jnp.maximum(dot(act[group, :], weight, ((1,), (0,))), 0.0)
-            pre = jnp.where(need_ref[:, at] <= width, pre, 0.0)
+            pre = jnp.where(router_ref[6:7, at] <= width, pre, 0.0)
             dpre[group, at] = pre.astype(bf16)
             hid[group, at] = (pre * pre).astype(bf16)
 
@@ -552,11 +547,10 @@
 
     def core_sum(k):
         cores[k].wait_recv()
-        load((down_core if k < 2 else up_core).at[k % 2], held, 13 + k).wait()
-
-        def add(i):
-            a, b, c, d = i // 8, (i // 4) % 2, (i // 2) % 2, i % 2
-            come = held[a, b, c, d].astype(f32)
+
+        def add(i, a, b):
+            c, d = i // 2, i % 2
+            come = held[c, d].astype(f32)
             if k < 2:
                 here = down_sum[core, a, b, c, d, :, side_of(k)].astype(f32)
                 down_sum[core, a, b, c, d, :, side_of(k)] = (here + come).astype(bf16)
@@ -564,7 +558,10 @@
                 here = up[a, b, c, d, core, :, side_of(k)].astype(f32)
                 up[a, b, c, d, core, :, side_of(k)] = (here + come).astype(bf16)
 
-        each(16, add)
+        for a in range(2):
+            for b in range(2):
+                load((down_core if k < 2 else up_core).at[k % 2, a, b], held, 15 + k).wait()
+                each(4, functools.partial(add, a=a, b=b))
         if k < 2:
             source = down_sum.at[core, 1 - x, :, :, :, :, side_of(k)]
             return send(source, down_near.at[:, :, :, :, side_of(k)], X)
@@ -612,62 +609,174 @@
 
     cores, nears, fars, keep = [], [], [], []
     hidden_of(0)
-    both_y.wait_recv()
-    both_z.wait_recv()
-    scale_both.wait_recv()
+    for copy in down_loads:
+        copy.wait()
+    mixed_of(0)
+    mixed_one = send(mixed.at[slot(1)], mixed_low.at[0], Y)
     hidden_of(1)
-    down_to_far.wait_recv()
-    down_slot = down.at[core, x, 1 - far]
-    down_to_x = send(down_slot, down_slot, X)
-    down_to_core = send(down_slot, down_slot, CORE)
+    mixed_of(1)
+    mixed_three = send(mixed.at[slot(3)], mixed_low.at[1], Y)
     cores.append(down_terms(0))
     cores.append(down_terms(1))
-    down_to_x.wait_recv()
-    down_slot = down.at[core, 1 - x, 1 - far]
-    down_last = send(down_slot, down_slot, CORE)
-    down_to_core.wait_recv()
-    down_last.wait_recv()
-    mixed_of(0)
-    mixed_one = send(mixed.at[slot(1)], mixed_low.at[0], Y)
-    nears.append(core_sum(0))
-    mixed_of(1)
-    mixed_three = send(mixed.at[slot(3)], mixed_low.at[1], Y)
-    nears.append(core_sum(1))
     dact_of(1)
     dact_two = send(dact.at[slot(2)], dact_low.at[0], Z)
     dact_three = send(dact.at[slot(3)], dact_low.at[1], Z)
+    nears.append(core_sum(0))
+    nears.append(core_sum(1))
     dact_of(0)
-    near_sum(0)
+    out_load = load(out_ref, down, 13)
+    x_load = load(x_ref, x_one, 14)
+    top_load = load(top_zero, hid.at[slot(0)], 0)
     cores.append(up_terms(2))
     cores.append(up_terms(3))
+    near_sum(0)
     nears.append(core_sum(2))
     nears.append(core_sum(3))
-
+    near_sum(1)
+
+    dact_two.wait_recv()
+    dact_three.wait_recv()
+    add_low(dact, 1, dact_low, 1)
+    dact_last = send(dact.at[slot(1)], dact_come, Y)
     mixed_one.wait_recv()
     mixed_three.wait_recv()
     add_low(mixed, 2, mixed_low, 1)
     mixed_last = send(mixed.at[slot(2)], mixed_come, Z)
-    near_sum(1)
     add_low(mixed, 0, mixed_low, 0)
-    keep.append(load(mixed.at[slot(0)], mixed_own, 17))
-    dact_two.wait_recv()
-    dact_three.wait_recv()
-    add_low(dact, 1, dact_low, 1)
-    dact_last = send(dact.at[slot(1)], dact_come, Y)
     add_low(dact, 0, dact_low, 0)
-    keep.append(load(dact.at[slot(0)], dact_own, 18))
     near_sum(2)
+
+    small[...] = jnp.zeros_like(small)
+    x_load.wait()
+    top_load.wait()
+    mixed_last.wait_recv()
+    dact_last.wait_recv()
+    gain, bias = router_ref[4:5, :], router_ref[5:6, :]
+
+    def back(i):
+        def part(k):
+            return pl.ds(pl.multiple_of(k * rows + i * 16, 16), 16)
+
+        at = part(0)
+        value = x_one[at, :]
+        center = value - jnp.mean(value, axis=-1, keepdims=True)
+        inv = lax.rsqrt(jnp.mean(center * center, axis=-1, keepdims=True) + norm_eps)
+        normed = center * inv
+        its_mixed = mixed[at, :].astype(f32) + mixed_come[at, :].astype(f32)
+        grad = dact[at, :].astype(f32) + dact_come[at, :].astype(f32)
+        top = hid[at, :].astype(f32)
+        hid[part(3), :] = (value + its_mixed * scale[at, :][:, :1]).astype(bf16)
+        logits = coef_ref[at, :] * jnp.sum(top * its_mixed, axis=-1, keepdims=True)
+        ln_out = normed * gain + bias
+        for c in range(WIDTHS):
+            one = logits[:, c : c + 1]
+            grad = grad + one * router_ref[c : c + 1, :]
+            small[3 + c : 4 + c, :] += jnp.sum(ln_out * one, axis=0, keepdims=True)
+        small[1:2, :] += jnp.sum(grad * normed, axis=0, keepdims=True)
+        small[2:3, :] += jnp.sum(grad, axis=0, keepdims=True)
+        grad = grad * gain
+        mean = jnp.mean(grad, axis=-1, keepdims=True)
+        along = jnp.mean(grad * normed, axis=-1, keepdims=True)
+        total = top + inv * (grad - mean - normed * along)
+        x_one[at, :] = total
+        hid[part(2), :] = total.astype(bf16)
+
+    each(rows // 16, back)
+    keep.append(load(x_one, grad_x, 23))
+    keep.append(load(hid.at[slot(2)], branch, 24))
+    keep.append(load(hid.at[slot(3)], block_out, 25))
+    out_load.wait()
+    cols = dim // 8
+
+    def dat_block(owner):
+        at = pl.ds(pl.multiple_of(owner * cols, cols), cols)
+        weight = down[owner // 4, (owner // 2) % 2, owner % 2]
+        hid[slot(1), at] = dot(hid[slot(2), :], weight, ((1,), (1,))).astype(bf16)
+        return hid.at[slot(1), at]
+
+    dats = []
+    for k in range(1, 8):
+        owner = (w + k) % 8
+        copy = pltpu.make_async_remote_copy(
+            src_ref=dat_block(owner),
+            dst_ref=dat_out.at[w],
+            send_sem=dat_send_sem.at[k - 1],
+            recv_sem=dat_recv_sem.at[k - 1],
+            device_id={"wide": owner},
+            device_id_type=MESH,
+        )
+        copy.start()
+        dats.append(copy)
+    keep.append(load(dat_block(w), dat_out.at[w], 26))
+
+    low_load = load(low_ref, hid.at[slot(0)], 1)
+    low_load.wait()
+    shard = dim // 32
+    half_rows = dim // 2
+
+    def out_block(i):
+        for k, place in enumerate((act, dpre)):
+            at = pl.ds(pl.multiple_of(k * half_rows + i * cols, cols), cols)
+            value = dot(hid[slot(0), at], hid[slot(2), :], ((0,), (0,))).astype(bf16)
+            place[pl.ds(pl.multiple_of(i * cols, cols), cols), :] = value
+
+    each(half_rows // cols, out_block)
+
+    def out_rows(i, its_core):
+        return pl.ds(pl.multiple_of((2 * (i % 8) + its_core) * shard, shard), shard)
+
+    outs = []
+    for i in range(16):
+        copy = pltpu.make_async_remote_copy(
+            src_ref=(act if i < 8 else dpre).at[out_rows(i, 1 - core)],
+            dst_ref=dmix.at[pl.ds(i * shard, shard)],
+            send_sem=out_send_sem.at[i],
+            recv_sem=out_recv_sem.at[i],
+            device_id=peers[CORE],
+            device_id_type=MESH,
+        )
+        copy.start()
+        outs.append(copy)
+    for copy in outs:
+        copy.wait_recv()
+
+    def out_add(i):
+        for k, place in enumerate((act, dpre)):
+            at = pl.ds(pl.multiple_of((k * 8 + i) * shard, shard), shard)
+            mine = place[out_rows(i, core), :].astype(f32)
+            dmix[at, :] = (mine + dmix[at, :].astype(f32)).astype(bf16)
+
+    each(8, out_add)
+    y = n // 2
+    for i in range(8):
+        keep.append(load(dmix.at[pl.ds((2 * i + y) * shard, shard)], out_own.at[i], 43 + i))
+    out_ys = []
+    for i in range(8):
+        source = dmix.at[pl.ds((2 * i + 1 - y) * shard, shard)]
+        if i < 4:
+            copy = pltpu.make_async_remote_copy(
+                src_ref=source,
+                dst_ref=out_come.at[i],
+                send_sem=side_send_sem.at[i],
+                recv_sem=side_recv_sem.at[i],
+                device_id=peers[Y],
+                device_id_type=MESH,
+            )
+            copy.start()
+            out_ys.append(copy)
+        else:
+            keep.append(load(source, out_other.at[i - 4], 51 + i))
     near_sum(3)
     for copy in keep:
         copy.wait()
-    for copy in [mixed_last, dact_last] + fars:
+    for copy in fars + dats + out_ys:
         copy.wait_recv()
-    for copy in started:
+    for copy in started + dats + outs + out_ys:
         copy.wait_send()
 
 
-def feed_forward(act, tops, chosen, width_all, need, ups, downs):
-    rows, dim = act.shape
+def feed_forward(act, tops, facts, ups, downs, down, x_one, low, out_full, coef, router):
+    rows, dim = x_one.shape
     any_space = pl.BlockSpec(memory_space=pl.ANY)
     in_vmem = pl.BlockSpec(memory_space=pltpu.VMEM)
     tokens = 4 * rows
@@ -679,13 +788,17 @@
 
     return pl.pallas_call(
         feed_kernel,
-        in_specs=[any_space] * 5 + [in_vmem] * 3 + [any_space] * 6,
-        out_specs=[any_space] * 10,
+        in_specs=[any_space] * 5 + [in_vmem] + [any_space] * 6 + [in_vmem] * 2,
+        out_specs=[in_vmem] + [any_space] * 13,
         out_shape=[
+            jax.ShapeDtypeStruct((8, dim), f32),
             shape(rows, dim),
+            jax.ShapeDtypeStruct((rows, dim), f32),
             shape(rows, dim),
-            shape(rows, dim),
-            shape(rows, dim),
+            shape(8, rows, dim // 8),
+            shape(8, shard, dim),
+            shape(4, shard, dim),
+            shape(4, shard, dim),
             shape(2, 2, shard, dim),
             shape(2, 2, shard, dim),
             shape(2, 2, shard, dim),
@@ -698,7 +811,6 @@
             pltpu.VMEM((2, 2, 2, dim // 8, dim), bf16),
             pltpu.VMEM((tokens, dim), bf16),
             pltpu.VMEM((tokens, dim), bf16),
-            pltpu.VMEM((tokens, 128), f32),
             pltpu.VMEM((tokens, dim), bf16),
             pltpu.VMEM((tokens, dim), bf16),
             pltpu.VMEM((tokens, dim), bf16),
@@ -707,19 +819,28 @@
             pltpu.VMEM((2, rows, dim), bf16),
             pltpu.VMEM((2, 2, 2, shard, dim), bf16),
             pltpu.VMEM((2, 2, 2, shard, dim), bf16),
-            pltpu.VMEM((2, 2, 2, 2, shard, cut), bf16),
+            pltpu.VMEM((2, 2, shard, cut), bf16),
             pltpu.VMEM((2, 2, 2, 2, 2, shard, dim), bf16),
-            pltpu.SemaphoreType.DMA((23,)),
+            pltpu.VMEM((rows, dim), bf16),
+            pltpu.VMEM((rows, dim), bf16),
+            pltpu.VMEM((rows, dim), f32),
+            pltpu.SemaphoreType.DMA((59,)),
             pltpu.SemaphoreType.DMA((36,)),
             pltpu.SemaphoreType.DMA((36,)),
+            pltpu.SemaphoreType.DMA((7,)),
+            pltpu.SemaphoreType.DMA((7,)),
+            pltpu.SemaphoreType.DMA((16,)),
+            pltpu.SemaphoreType.DMA((16,)),
+            pltpu.SemaphoreType.DMA((4,)),
+            pltpu.SemaphoreType.DMA((4,)),
         ],
         compiler_params=pltpu.CompilerParams(
-            collective_id=0, has_side_effects=True, vmem_limit_bytes=62 * 2**20
+            collective_id=0, has_side_effects=True, vmem_limit_bytes=63 * 2**20 + 2**19
         ),
         cost_estimate=pl.CostEstimate(
             flops=12 * tokens * dim * dim, bytes_accessed=2**25, transcendentals=0
         ),
-    )(act, *tops, chosen, width_all, need, *ups, *downs)
+    )(act, *tops, facts, ups, downs, down, x_one, low, out_full, coef, router)
 
 
 def ring_index(place):
@@ -737,27 +858,34 @@
     sin_ref,
     qkv_part,
     out_part,
-    up_blocks,
+    up_part,
     down_part,
     top_zero,
+    onehot_ref,
+    router_ref,
+    gain_two_ref,
+    bias_two_ref,
     qkv,
     att,
     lse,
+    x_one,
+    coef,
+    facts,
+    low_out,
+    act_many,
     act_out,
     weight_out,
-    low_out,
     out_full,
-    up_zero,
-    up_far,
-    up_next,
-    up_both,
-    down_next,
+    ups,
+    downs,
     top_one,
     top_two,
     top_three,
     act,
     weight,
     low,
+    out_held,
+    act_two,
     local_sem,
     send_sem,
     recv_sem,
@@ -765,6 +893,10 @@
     qkv_recv_sem,
     low_send_sem,
     low_recv_sem,
+    up_send_sem,
+    up_recv_sem,
+    up_local_sem,
+    out_sem,
 ):
     w = lax.axis_index("wide")
     n = lax.axis_index("narrow")
@@ -785,6 +917,8 @@
         pl.semaphore_signal(barrier, inc=1, device_id=peer, device_id_type=MESH)
     pl.semaphore_wait(barrier, len(peers))
     started, kept = [], []
+    up_zero, up_far, up_next, up_both = (ups.at[0, k] for k in range(4))
+    down_next = downs.at[0, 2]
 
     def send(source, target, peer):
         at = len(started)
@@ -840,13 +974,32 @@
     out_onward = send(out_part, out_full.at[w, n], right)
     out_back = send(out_part, out_full.at[w, n], left)
     out_own = keep(out_part, out_full.at[w, n])
+    out_y = [send(out_part, out_full.at[w, n], to_y)]
     team = z * 2 + y
-    swaps = [
-        send(up_blocks.at[z * 2 + 1 - y], up_zero.at[team], to_y),
-        send(up_blocks.at[(1 - z) * 2 + y], up_zero.at[team], to_z),
-        send(up_blocks.at[(1 - z) * 2 + 1 - y], up_zero.at[team], to_both),
-    ]
-    up_own = keep(up_blocks.at[team], up_zero.at[team])
+    piece = down_part.shape[0]
+
+    def up_block(its_z, its_y, share):
+        its_w = (share % 2) * 4 + its_z * 2 + (share // 2) % 2
+        its_n = its_y * 2 + share // 4
+        return up_part.at[:, pl.ds(pl.multiple_of((its_w * 4 + its_n) * piece, piece), piece)]
+
+    swaps, up_own = [], []
+    for share in range(8):
+        target = up_zero.at[team, :, pl.ds(share * piece, piece)]
+        for k, (its_z, its_y, peer) in enumerate(((z, 1 - y, to_y), (1 - z, y, to_z), (1 - z, 1 - y, to_both))):
+            copy = pltpu.make_async_remote_copy(
+                src_ref=up_block(its_z, its_y, share),
+                dst_ref=target,
+                send_sem=up_send_sem.at[k, share],
+                recv_sem=up_recv_sem.at[k, share],
+                device_id=peer,
+                device_id_type=MESH,
+            )
+            copy.start()
+            swaps.append(copy)
+        copy = pltpu.make_async_copy(up_block(z, y, share), target, up_local_sem.at[share])
+        copy.start()
+        up_own.append(copy)
 
     def ring_hop(step):
         nonlocal onward, back, out_onward, out_back
@@ -861,6 +1014,8 @@
             back = send(act.at[ahead, second], act.at[ahead, second], left)
         out_onward.wait_recv()
         out_back.wait_recv()
+        for owner in (behind, ahead):
+            out_y.append(send(out_full.at[owner, n], out_full.at[owner, n], to_y))
         if step < 3:
             out_onward = send(out_full.at[behind, n], out_full.at[behind, n], right)
             out_back = send(out_full.at[ahead, n], out_full.at[ahead, n], left)
@@ -903,10 +1058,13 @@
     ring_hop(3)
     for copy in swaps:
         copy.wait_recv()
-    up_own.wait()
+    for copy in up_own:
+        copy.wait()
     up_to_far = send(up_zero, up_far, to_far)
     up_to_x = send(up_zero, up_next, to_x)
     down_to_x = send(down_part, down_next, to_x)
+    cores = [send(up_zero, ups.at[1, 0], to_core), send(down_part, downs.at[1, 0], to_core)]
+    across = send(top_zero, top_two, to_z)
     project_pair(3)
     onward.wait_recv()
     back.wait_recv()
@@ -914,8 +1072,8 @@
     out_onward.wait_recv()
     out_back.wait_recv()
     out_own.wait()
-    out_y = send(out_full.at[:, n], out_full.at[:, n], to_y)
-    across = send(top_zero, top_two, to_z)
+    last = ring_index(place + 4)
+    out_y.append(send(out_full.at[last, n], out_full.at[last, n], to_y))
     keep(act, act_out)
     keep(weight, weight_out)
 
@@ -1005,18 +1163,28 @@
             def _():
                 low_keep(target).start()
 
-        if i == 2:
-            out_y.wait_recv()
+        if i == 0:
+            for copy in out_y:
+                copy.wait_recv()
             out_core = [
                 send(out_full.at[:, n], out_full.at[:, n], to_core),
                 send(out_full.at[:, (n + 2) % 4], out_full.at[:, (n + 2) % 4], to_core),
             ]
-    across.wait_recv()
-    both = send(top_two, top_three, to_y)
+        if i == 2:
+            across.wait_recv()
+            both = send(top_two, top_three, to_y)
+    part_rows = down_part.shape[0] // 2
+    parts = [pl.ds(0, part_rows), pl.ds(part_rows, part_rows)]
+    down_fars = [send(down_part.at[parts[0]], downs.at[0, 1, parts[0]], to_far)]
     up_to_far.wait_recv()
     up_to_both = send(up_far, up_both, to_x)
-    for copy in out_core + [beside, both, up_to_x, up_to_both, down_to_x]:
+    cores.append(send(up_far, ups.at[1, 1], to_core))
+    for copy in out_core:
         copy.wait_recv()
+    held = []
+    for k in range(8):
+        held.append(pltpu.make_async_copy(out_full.at[k], out_held.at[k], out_sem.at[k]))
+        held[-1].start()
     for target in range(8):
 
         @pl.when(w != target)
@@ -1028,14 +1196,92 @@
         def _():
             low_keep(target).wait()
 
+    down_fars.append(send(down_part.at[parts[1]], downs.at[0, 1, parts[1]], to_far))
+    for copy in held:
+        copy.wait()
+
+    def branch(t):
+        at = pl.ds(pl.multiple_of(t * 256, 256), 256)
+        value = dot(low_out[...], out_held[:, :, :, at].reshape(dim, 256), ((1,), (0,)))
+        x_one[:, at] = tokens_ref[:, at].astype(f32) + value
+
+    each(dim // 256, branch)
+    gain_two, bias_two = gain_two_ref[...], bias_two_ref[...]
+    lane = lax.broadcasted_iota(jnp.int32, (32, 8), 1)
+    wide_lane = lax.broadcasted_iota(jnp.int32, (32, 128), 1)
+
+    def normalize(i):
+        at = pl.ds(pl.multiple_of(i * 32, 32), 32)
+        value = x_one[at, :]
+        center = value - jnp.mean(value, axis=-1, keepdims=True)
+        inv = lax.rsqrt(jnp.mean(center * center, axis=-1, keepdims=True) + norm_eps)
+        ln_out = center * inv * gain_two + bias_two
+        act_two[at, :] = ln_out.astype(bf16)
+        logits = lax.dot_general(
+            ln_out, router_ref[...], (((1,), (1,)), ((), ())), precision=highest, preferred_element_type=f32
+        )
+        logits = jnp.where(lane < WIDTHS, logits, masked_score)
+        powers = jnp.exp(logits - jnp.max(logits, axis=-1, keepdims=True))
+        prob = powers / jnp.sum(powers, axis=-1, keepdims=True)
+        hot = onehot_ref[at, :]
+        chosen = jnp.sum(prob * hot, axis=-1, keepdims=True)
+        width = jnp.sum(hot * lane.astype(f32), axis=-1, keepdims=True)
+        coef[at, :] = chosen * (hot - prob)
+        facts[at, :] = jnp.where(wide_lane == 0, chosen, width)
+
+    each(rows // 32, normalize)
+
+    def slot(k):
+        return pl.ds(k * rows, rows)
+
+    act_y = send(act_two, act_many.at[slot(1)], to_y)
+    act_z = send(act_two, act_many.at[slot(2)], to_z)
+    mine = facts.at[slot(0)]
+    facts_y = send(mine, facts.at[slot(1)], to_y)
+    facts_z = send(mine, facts.at[slot(2)], to_z)
+    keep(act_two, act_many.at[slot(0)])
+    up_to_x.wait_recv()
+    cores.append(send(up_next, ups.at[1, 2], to_core))
+    down_to_x.wait_recv()
+    cores.append(send(down_next, downs.at[1, 2], to_core))
+    up_to_both.wait_recv()
+    cores.append(send(up_both, ups.at[1, 3], to_core))
+    down_boths = []
+
+    def down_hop(k):
+        down_fars[k].wait_recv()
+        down_boths.append(send(downs.at[0, 1, parts[k]], downs.at[0, 3, parts[k]], to_x))
+        cores.append(send(downs.at[0, 1, parts[k]], downs.at[1, 1, parts[k]], to_core))
+
+    down_hop(0)
+    act_y.wait_recv()
+    act_z.wait_recv()
+    half = rows // 2
+    boths = [
+        send(act_many.at[pl.ds(2 * rows, half)], act_many.at[pl.ds(3 * rows, half)], to_y),
+        send(act_many.at[pl.ds(rows + half, half)], act_many.at[pl.ds(3 * rows + half, half)], to_z),
+    ]
+    facts_y.wait_recv()
+    facts_z.wait_recv()
+    boths.append(send(facts.at[slot(2)], facts.at[slot(3)], to_y))
+    down_hop(1)
+    for copy in [beside, both] + boths:
+        copy.wait_recv()
+    for k in range(2):
+        down_boths[k].wait_recv()
+        cores.append(send(downs.at[0, 3, parts[k]], downs.at[1, 3, parts[k]], to_core))
+    for copy in cores:
+        copy.wait_recv()
     for copy in kept[3:]:
-        if copy is not up_own and copy is not out_own:
+        if copy is not out_own:
             copy.wait()
-    for copy in started + exchanges:
+    for copy in started + exchanges + swaps:
         copy.wait_send()
 
 
-def first_sums(split, limits, tokens, gain, cos2, sin2, w_qkv, w_out, up_blocks, w_down, top):
+def first_sums(
+    split, limits, tokens, gain, cos2, sin2, w_qkv, w_out, w_up, w_down, top, onehot, router, gain_two, bias_two
+):
     rows, dim = tokens.shape
     length = 8 * rows
     shard, wide_cols = w_qkv.shape
@@ -1048,24 +1294,28 @@
     def shape(*dims):
         return jax.ShapeDtypeStruct(dims, bf16)
 
+    def full(*dims):
+        return jax.ShapeDtypeStruct(dims, f32)
+
     flops = 6 * length * dim * cols + 4 * length * length * cols
     return pl.pallas_call(
         first_kernel,
-        in_specs=[smem] * 2 + [in_vmem] * 4 + [any_space] * 5,
-        out_specs=[in_vmem] * 3 + [any_space] * 12,
+        in_specs=[smem] * 2 + [in_vmem] * 4 + [any_space] * 5 + [in_vmem] * 4,
+        out_specs=[in_vmem] * 7 + [any_space] * 9,
         out_shape=[
             shape(length, 3 * cols),
-            jax.ShapeDtypeStruct((length, cols), f32),
-            jax.ShapeDtypeStruct((length, cols), f32),
+            full(length, cols),
+            full(length, cols),
+            full(rows, dim),
+            full(rows, 8),
+            full(4 * rows, 128),
+            shape(rows, dim),
+            shape(4 * rows, dim),
             shape(8, rows, dim),
             shape(8, 4, shard, 3 * cols),
-            shape(rows, dim),
             shape(8, 4, shard, dim),
-            shape(4, shard, dim),
-            shape(4, shard, dim),
-            shape(4, shard, dim),
-            shape(4, shard, dim),
-            shape(*w_down.shape),
+            shape(2, 4, 4, shard, dim),
+            shape(2, 4, *w_down.shape),
             shape(rows, dim),
             shape(rows, dim),
             shape(rows, dim),
@@ -1074,19 +1324,27 @@
             pltpu.VMEM((8, rows, dim), bf16),
             pltpu.VMEM((8, 4, shard, 3 * cols), bf16),
             pltpu.VMEM((length, cols), bf16),
+            pltpu.VMEM((8, 4, shard, dim), bf16),
+            pltpu.VMEM((rows, dim), bf16),
             dma((8,)),
-            dma((32,)),
-            dma((32,)),
+            dma((60,)),
+            dma((60,)),
             dma((7, 3)),
             dma((7, 3)),
             dma((8,)),
             dma((8,)),
+            dma((3, 8)),
+            dma((3, 8)),
+            dma((8,)),
+            dma((8,)),
         ],
         compiler_params=pltpu.CompilerParams(
-            collective_id=2, has_side_effects=True, vmem_limit_bytes=56 * 2**20
+            collective_id=2, has_side_effects=True, vmem_limit_bytes=60 * 2**20
         ),
         cost_estimate=pl.CostEstimate(flops=flops, bytes_accessed=2**25, transcendentals=2**22),
-    )(split, limits, tokens, gain, cos2, sin2, w_qkv, w_out, up_blocks, w_down, top)
+    )(
+        split, limits, tokens, gain, cos2, sin2, w_qkv, w_out, w_up, w_down, top, onehot, router, gain_two, bias_two
+    )
 
 
 STRIP = 128
@@ -1096,16 +1354,23 @@
     dproj,
     weight,
     act_ref,
-    out_terms,
+    out_own,
+    out_low,
+    out_high,
     small_ref,
     base_ref,
     tokens_ref,
     inv_ref,
     gain_ref,
+    up_zero,
+    up_one,
+    up_two,
+    up_three,
     input_grad,
     out_grad,
     qkv_grad,
     small_out,
+    up_grad,
     act_grad,
     qkv_come,
     act,
@@ -1118,6 +1383,7 @@
     out_recv,
     small_sum,
     small_recv,
+    out_come,
     load_sem,
     ring_send_sem,
     ring_recv_sem,
@@ -1137,6 +1403,7 @@
     other_core = {"narrow": n + 1 - 2 * core}
     other_y = {"narrow": (n + 2) % 4}
     others = [{"wide": (w + k) % 8} for k in range(1, 8)]
+    z = (w // 2) % 2
     barrier = pltpu.get_barrier_semaphore()
     for peer in others + [other_core, other_y]:
         pl.semaphore_signal(barrier, inc=1, device_id=peer, device_id_type=MESH)
@@ -1208,12 +1475,16 @@
                 each(STRIP // 32, add)
             if step < 7:
                 hop(step, stream).start()
+
+    def out_step(step):
         for stream in (4, 5):
             side = stream - 4
-            value = out_terms[owner_of(step, side), :, pl.ds(side * half, half)]
+            owner = owner_of(step, side)
+            at = pl.ds(side * half, half)
+            value = out_own[owner, :, at].astype(f32) + out_come[owner, :, at].astype(f32)
             if step > 0:
                 hop(step - 1, stream).wait_recv()
-                value = value.astype(f32) + out_recv[step - 1, side].astype(f32)
+                value = value + out_recv[step - 1, side].astype(f32)
             if step < 7:
                 out_send[step, side] = value.astype(bf16)
                 hop(step, stream).start()
@@ -1221,6 +1492,9 @@
                 out_grad[:, pl.ds(side * half, half)] = value
 
     ring_step(0)
+    out_come[0:4] = out_low[...]
+    out_come[4:8] = out_high[...]
+    out_step(0)
     load.wait()
     small_sum[0] = small_ref[...]
 
@@ -1252,6 +1526,7 @@
     pending = []
     small_step(0)
     ring_step(1)
+    out_step(1)
     to_core.wait_recv()
 
     def add_core(i):
@@ -1263,8 +1538,10 @@
     to_side = send(terms.at[:, 1 - y, core], side_come, other_y)
     small_step(1)
     ring_step(2)
+    out_step(2)
     small_step(2)
     ring_step(3)
+    out_step(3)
     to_side.wait_recv()
 
     def add_side(i):
@@ -1280,11 +1557,15 @@
         blocks.append(send(terms.at[target, y, core], qkv_come.at[w], peer))
     small_step(3)
     ring_step(4)
+    out_step(4)
     small_step(4)
     ring_step(5)
+    out_step(5)
     small_step(5)
     ring_step(6)
+    out_step(6)
     ring_step(7)
+    out_step(7)
 
     def finish(i):
         at = pl.ds(pl.multiple_of(i * 32, 32), 32)
@@ -1298,6 +1579,14 @@
     own.wait()
     for copy in blocks:
         copy.wait_recv()
+    piece = dim // 8
+    for k, block in enumerate((up_zero, up_one, up_two, up_three)):
+        its_z = z + (1 - 2 * z) * (k // 2)
+        its_y = y + (1 - 2 * y) * (k % 2)
+        for share in range(8):
+            its_w = (share % 2) * 4 + its_z * 2 + (share // 2) % 2
+            at = pl.multiple_of((its_w * 4 + its_y * 2 + share // 4) * piece, piece)
+            up_grad[:, pl.ds(at, piece)] = block[:, pl.ds(share * piece, piece)].astype(f32)
     cols = weight.shape[1] // 3
     for k in range(8):
         for part in range(3):
@@ -1310,7 +1599,7 @@
             hop(step, stream).wait_send()
 
 
-def last_sums(dproj, weight, act, out_terms, small, base, tokens_in, inv, gain):
+def last_sums(dproj, weight, act, out_own, out_come, small, base, tokens_in, inv, gain, ups):
     tokens, cols = dproj.shape
     dim = weight.shape[0]
     rows, shard, half = tokens // 8, dim // 32, dim // 2
@@ -1319,13 +1608,14 @@
     dma = pltpu.SemaphoreType.DMA
     return pl.pallas_call(
         last_kernel,
-        in_specs=[in_vmem, in_vmem, any_space] + [in_vmem] * 6,
-        out_specs=[in_vmem] * 4,
+        in_specs=[in_vmem, in_vmem, any_space] + [in_vmem] * 12,
+        out_specs=[in_vmem] * 5,
         out_shape=[
             jax.ShapeDtypeStruct((rows, dim), f32),
             jax.ShapeDtypeStruct((shard, dim), f32),
             jax.ShapeDtypeStruct((shard, 3 * dim), f32),
             jax.ShapeDtypeStruct((8, dim), f32),
+            jax.ShapeDtypeStruct((shard, 4 * dim), f32),
         ],
         scratch_shapes=[
             pltpu.VMEM((rows, dim), f32),
@@ -1340,11 +1630,12 @@
             pltpu.VMEM((7, 2, shard, half), bf16),
             pltpu.VMEM((6, 8, dim), f32),
             pltpu.VMEM((5, 8, dim), f32),
+            pltpu.VMEM((8, shard, dim), bf16),
             dma,
             dma((7, 6)),
             dma((7, 6)),
-            dma((16,)),
-            dma((16,)),
+            dma((20,)),
+            dma((20,)),
         ],
         compiler_params=pltpu.CompilerParams(
             collective_id=1, has_side_effects=True, vmem_limit_bytes=60 * 2**20
@@ -1352,7 +1643,7 @@
         cost_estimate=pl.CostEstimate(
             flops=4 * tokens * cols * dim, bytes_accessed=2**24, transcendentals=0
         ),
-    )(dproj, weight, act, out_terms, small, base, tokens_in, inv, gain)
+    )(dproj, weight, act, out_own, *out_come, small, base, tokens_in, inv, gain, *ups)
 
 
 def swap(array, axis, size, bits):
@@ -1457,11 +1748,11 @@
     def pick(array, at):
         return lax.dynamic_index_in_dim(array, at, 0, keepdims=False)
 
-    exponent = jnp.arange(HEAD_DIM // 2, dtype=f32) * (2.0 / HEAD_DIM)
-    angles = jnp.arange(length, dtype=f32)[:, None] * jnp.power(rope_base, -exponent)[None, :]
-    cosine, sine = jnp.cos(angles), jnp.sin(angles)
-    cos2 = jnp.concatenate([cosine, cosine], axis=1)
-    sin2 = jnp.concatenate([-sine, sine], axis=1)
+    exponent = np.arange(HEAD_DIM // 2, dtype=np.float64) * (2.0 / HEAD_DIM)
+    angles = np.arange(length, dtype=np.float64)[:, None] * np.power(rope_base, -exponent)[None, :]
+    cosine, sine = np.cos(angles).astype(np.float32), np.sin(angles).astype(np.float32)
+    cos2 = jnp.asarray(np.concatenate([cosine, cosine], axis=1))
+    sin2 = jnp.asarray(np.concatenate([-sine, sine], axis=1))
     split = pick_rows(doc_split)
     limits = jnp.concatenate(
         [pick_rows(head_count), jnp.full((my_rows, 1), head_at * my_heads, jnp.int32)], axis=1
@@ -1474,16 +1765,20 @@
 
     shard = w_qkv.shape[0]
     piece_rows = w_down.shape[0]
-    up_blocks = w_up.reshape(shard, upper, 2, 2, 2, 2, piece_rows).transpose(2, 4, 0, 5, 3, 1, 6)
-    up_blocks = up_blocks.reshape(4, shard, shares * piece_rows)
     top = out_grad.reshape(count, dim)
     width_flat = width_choice.reshape(count)
-    width_across = across(width_flat)
-    width_all = jnp.concatenate([width_flat, beside(width_flat), width_across, beside(width_across)])
+    share = jnp.arange(shares, dtype=jnp.int32)[:, None]
+    team = team_of(w_at, n_at)
+    units = (wide_of(share, team) * narrow + narrow_of(share, team)) * piece_rows
+    units = (units + jnp.arange(piece_rows, dtype=jnp.int32)[None, :]).reshape(1, -1)
+    need = units // (hidden // WIDTHS)
 
     kernels = wide == 8 and narrow == 4 and rows == 1
     if kernels:
-        qkv, att, lse, act_flat, my_qkv, att_low, out_full, *found = first_sums(
+        hot = (width_flat[:, None] == jnp.arange(2 * WIDTHS, dtype=jnp.int32)[None, :]).astype(f32)
+        need_row = need.astype(f32)
+        router_rows = jnp.concatenate([router.T, gain_two[None], bias_two[None], need_row, need_row])
+        found = first_sums(
             split,
             limits,
             tokens.reshape(count, dim),
@@ -1492,16 +1787,19 @@
             sin2,
             w_qkv,
             w_out,
-            up_blocks,
+            w_up,
             w_down,
             top,
+            hot,
+            router_rows,
+            gain_two[None],
+            bias_two[None],
         )
+        qkv, att, lse, x_one, coef, facts, att_low, act_many, act_flat, my_qkv, out_full, ups, downs, *tops = found
         qkv, att, lse = qkv[None], att[None], lse[None]
         act_flat = act_flat.reshape(length, dim)
         my_qkv = my_qkv.reshape(dim, 3 * cols)
-        out_full = out_full.reshape(dim, dim)
-        ups, downs = found[:4], [w_down, found[4]]
-        tops = (top, *found[5:])
+        onehot = hot[:, :WIDTHS]
     else:
         blocks = w_qkv.reshape(shard, 3, head_groups, cols).transpose(2, 0, 1, 3)
         blocks = jnp.tile(blocks.reshape(head_groups, shard, 3 * cols), (row_groups, 1, 1))
@@ -1510,7 +1808,8 @@
         out_parts = narrow_gather(lax.all_gather(w_out, "wide", axis=0, tiled=False))
         out_full = out_parts.transpose(1, 0, 2, 3).reshape(dim, dim)
 
-        up_part = team_swap(up_blocks)
+        up_blocks = w_up.reshape(shard, upper, 2, 2, 2, 2, piece_rows).transpose(2, 4, 0, 5, 3, 1, 6)
+        up_part = team_swap(up_blocks.reshape(4, shard, shares * piece_rows))
         top_beside = beside(top)
         act_all = jnp.zeros((my_rows, wide, part_len, dim), bf16)
         for owner, piece in ring.gather(act_one.reshape(count, dim)):
@@ -1550,23 +1849,17 @@
         down_found = down_found + [down_near] + down_far
         top_both = beside(top_across)
         tops = (top, top_beside, top_across, top_both)
-    x_one = inputs.reshape(count, dim) + dot(att_low, out_full, ((1,), (0,)))
-
-    center = x_one - jnp.mean(x_one, axis=-1, keepdims=True)
-    inv_two = lax.rsqrt(jnp.mean(center * center, axis=-1, keepdims=True) + norm_eps)
-    normed_two = center * inv_two
-    ln_out = normed_two * gain_two + bias_two
-    act_two = ln_out.astype(bf16)
-    onehot = (width_flat[:, None] == jnp.arange(WIDTHS, dtype=jnp.int32)[None, :]).astype(f32)
-    router_prob = jax.nn.softmax(jnp.dot(ln_out, router, precision=highest), axis=-1)
-    chosen = jnp.sum(router_prob * onehot, axis=-1)
-    grad_top = top.astype(f32)
-    share = jnp.arange(shares, dtype=jnp.int32)[:, None]
-    team = team_of(w_at, n_at)
-    units = (wide_of(share, team) * narrow + narrow_of(share, team)) * piece_rows
-    units = (units + jnp.arange(piece_rows, dtype=jnp.int32)[None, :]).reshape(1, -1)
-    need = units // (hidden // WIDTHS)
-
+        x_one = inputs.reshape(count, dim) + dot(att_low, out_full, ((1,), (0,)))
+
+        center = x_one - jnp.mean(x_one, axis=-1, keepdims=True)
+        inv_two = lax.rsqrt(jnp.mean(center * center, axis=-1, keepdims=True) + norm_eps)
+        normed_two = center * inv_two
+        ln_out = normed_two * gain_two + bias_two
+        act_two = ln_out.astype(bf16)
+        onehot = (width_flat[:, None] == jnp.arange(WIDTHS, dtype=jnp.int32)[None, :]).astype(f32)
+        router_prob = jax.nn.softmax(jnp.dot(ln_out, router, precision=highest), axis=-1)
+        chosen = jnp.sum(router_prob * onehot, axis=-1)
+        grad_top = top.astype(f32)
     def share_core(array):
         return pick(array, n_at & 1) + swap(pick(array, 1 - (n_at & 1)), "narrow", narrow, 1)
 
@@ -1581,20 +1874,29 @@
         return array[0]
 
     if kernels:
-        mixed, mixed_come, grad_act_two, dact_come, down_grad, down_come, up_sum, up_come, _, _ = feed_forward(
-            act_two,
-            tops,
-            jnp.broadcast_to(chosen[:, None], (count, 128)),
-            width_all[:, None].astype(f32),
-            need.astype(f32),
-            [piece.reshape(2, 2, shard, shares * piece_rows) for piece in ups],
+        small, block_out, grad_x_one, _, dat, out_own, *outs, down_grad, down_come, up_sum, up_come, _, _ = feed_forward(
+            act_many,
+            (top, *tops),
+            facts,
+            ups.reshape(2, 4, 2, 2, shard, shares * piece_rows),
             downs,
+            w_down,
+            x_one,
+            att_low,
+            out_full.reshape(2, 2, 2, dim // 8, dim),
+            coef,
+            router_rows,
         )
-        mixed = mixed.astype(f32) + mixed_come.astype(f32)
-        grad_act_two = grad_act_two.astype(f32) + dact_come.astype(f32)
+        dat = dat.reshape(1, length, cols)
         down_grad = (down_grad.astype(f32) + down_come.astype(f32)).reshape(piece_rows, dim)
-        up_sum = up_sum + up_come
-        up_sum = up_sum.reshape(4, shard, shares * piece_rows)
+        out_come = [outs[0], beside(outs[1])]
+        up_sum = (up_sum + up_come).reshape(4, shard, shares * piece_rows)
+        up_blocks = [pick(up_sum, team ^ k) for k in range(4)]
+        diagonal = [(i, i ^ (2 * narrow + 2)) for i in range(wide * narrow)]
+        up_blocks[1:3] = beside(up_blocks[1]), across(up_blocks[2])
+        up_blocks[3] = lax.ppermute(up_blocks[3], ("wide", "narrow"), diagonal)
+        counts = jnp.pad(jnp.sum(onehot, axis=0), (0, dim - WIDTHS))[None]
+        small = jnp.concatenate([small[:7], counts])
     else:
         up_found = up_found + [((w, n ^ 1), swap(piece, "narrow", narrow, 1)) for (w, n), piece in up_found]
         down_found = down_found + [((w, n ^ 1), swap(p, "narrow", narrow, 1)) for (w, n), p in down_found]
@@ -1623,7 +1925,7 @@
             return near + across(far.astype(bf16)).astype(f32)
 
         act_many = team_gather(act_two)
-        mask = need <= width_all[:, None]
+        mask = need <= team_gather(width_flat)[:, None]
         pre = jnp.maximum(dot(act_many, up_mine, ((1,), (0,))), 0.0)
         pre = jnp.where(mask, pre, 0.0).astype(bf16).astype(f32)
         hid = (pre * pre).astype(bf16)
@@ -1639,49 +1941,54 @@
         up_sum = up_sums(act_many, dpre, wide, narrow, shard)
         up_sum = share_far(share_near(share_core(up_sum)))
 
-    block_out = (x_one + mixed * chosen[:, None]).astype(bf16)
-    grad_prob = jnp.sum(grad_top * mixed, axis=-1)
-    grad_logits = (grad_prob * chosen)[:, None] * (onehot - router_prob)
-    grad_router = lax.dot_general(ln_out, grad_logits, (((0,), (0,)), ((), ())), precision=highest)
-    grad_ln = grad_act_two + jnp.dot(grad_logits, router.T, precision=highest)
-    grad_gain_two = jnp.sum(grad_ln * normed_two, axis=0)
-    grad_bias_two = jnp.sum(grad_ln, axis=0)
-    grad_normed = grad_ln * gain_two
-    grad_x_one = grad_top + inv_two * (
-        grad_normed
-        - jnp.mean(grad_normed, axis=-1, keepdims=True)
-        - normed_two * jnp.mean(grad_normed * normed_two, axis=-1, keepdims=True)
-    )
-
-    grad_branch = grad_x_one.astype(bf16)
-    grad_att = dot(grad_branch, out_full, ((1,), (1,))).astype(bf16)
-    sends = grad_att.reshape(row_groups, my_rows, part_len, head_groups, cols)
-    sends = sends.transpose(0, 3, 1, 2, 4).reshape(wide, my_rows, part_len, cols)
-    come = lax.all_to_all(sends, "wide", 0, 0, tiled=True)
-    dat = come.transpose(1, 0, 2, 3).reshape(my_rows, length, cols)
+
+        block_out = (x_one + mixed * chosen[:, None]).astype(bf16)
+        grad_prob = jnp.sum(grad_top * mixed, axis=-1)
+        grad_logits = (grad_prob * chosen)[:, None] * (onehot - router_prob)
+        grad_router = lax.dot_general(ln_out, grad_logits, (((0,), (0,)), ((), ())), precision=highest)
+        grad_ln = grad_act_two + jnp.dot(grad_logits, router.T, precision=highest)
+        grad_gain_two = jnp.sum(grad_ln * normed_two, axis=0)
+        grad_bias_two = jnp.sum(grad_ln, axis=0)
+        grad_normed = grad_ln * gain_two
+        grad_x_one = grad_top + inv_two * (
+            grad_normed
+            - jnp.mean(grad_normed, axis=-1, keepdims=True)
+            - normed_two * jnp.mean(grad_normed * normed_two, axis=-1, keepdims=True)
+        )
+
+        grad_branch = grad_x_one.astype(bf16)
+        grad_att = dot(grad_branch, out_full, ((1,), (1,))).astype(bf16)
+        sends = grad_att.reshape(row_groups, my_rows, part_len, head_groups, cols)
+        sends = sends.transpose(0, 3, 1, 2, 4).reshape(wide, my_rows, part_len, cols)
+        come = lax.all_to_all(sends, "wide", 0, 0, tiled=True)
+        dat = come.transpose(1, 0, 2, 3).reshape(my_rows, length, cols)
+        counts = jnp.pad(jnp.sum(onehot, axis=0), (0, dim - WIDTHS))[None]
+        small = [jnp.zeros((1, dim), f32), grad_gain_two[None], grad_bias_two[None], grad_router.T, counts]
+        small = jnp.concatenate(small)
+
     dproj = attend_back(qkv, att, lse, dat, split, limits, cos2, sin2, my_heads)
-    grad_out = dot(att_low, grad_branch, ((0,), (0,))).astype(bf16)
-    grad_out = narrow_scatter(grad_out.reshape(wide, narrow, shard, dim))
-    dproj, act_flat, grad_out = join(dproj, act_flat, grad_out)
-    up_sum = team_swap(up_sum)
-    up_grad = up_sum.reshape(2, 2, shard, 2, 2, upper, piece_rows).transpose(2, 5, 0, 4, 1, 3, 6)
-    up_grad = up_grad.reshape(shard, hidden).astype(f32)
+    if not kernels:
+        grad_out = dot(att_low, grad_branch, ((0,), (0,))).astype(bf16)
+        grad_out = narrow_scatter(grad_out.reshape(wide, narrow, shard, dim))
+    if not kernels:
+        up_sum = team_swap(up_sum)
+        up_grad = up_sum.reshape(2, 2, shard, 2, 2, upper, piece_rows).transpose(2, 5, 0, 4, 1, 3, 6)
+        up_grad = up_grad.reshape(shard, hidden).astype(f32)
     normed_flat = normed_one.reshape(count, dim)
-    counts = jnp.pad(jnp.sum(onehot, axis=0), (0, dim - WIDTHS))[None]
-    small = [grad_gain_two[None], grad_bias_two[None], grad_router.T, counts]
 
     if kernels:
-        small = jnp.concatenate([jnp.zeros((1, dim), f32)] + small)
-        input_grad, out_proj_grad, qkv_grad, small = last_sums(
+        input_grad, out_proj_grad, qkv_grad, small, up_grad = last_sums(
             dproj[0],
             my_qkv,
             act_flat,
-            grad_out,
+            out_own,
+            out_come,
             small,
             grad_x_one,
             tokens.reshape(count, dim),
             inv_one.reshape(count, 1),
             gain_one[None],
+            up_blocks,
         )
     else:
         half = dim // 2
@@ -1698,7 +2005,7 @@
         grad_act_one = jnp.concatenate(ring.scatter(one_term), axis=1)
         grad_qkv = dot(act_flat, dproj.reshape(my_rows * length, 3 * cols), ((0,), (0,)))
         gain_one_part = jnp.sum(grad_qkv * my_qkv.astype(f32), axis=1)
-        small = jnp.concatenate([gain_one_part[None]] + small)
+        small = small.at[0].set(gain_one_part)
         grad_qkv = narrow_scatter(grad_qkv.astype(bf16).reshape(wide, narrow, shard, 3 * cols))
         grad_qkv = lax.all_to_all(grad_qkv, "wide", 0, 0, tiled=True).astype(f32)
         for bits in (1, 2):

time: 750 us -> 705 us (0.940)
  Pallas kernels: 632 us -> 664 us
  local copies, waits for them, and re-layouts: 41 us -> 14.1 us
  matrix products: 21.9 us -> 0 us
  other arithmetic: 27.6 us -> 9.29 us
  starting transfers between devices: 16 us -> 5.49 us
    pallas_call x1, Pallas kernels: 211 us -> 272 us  [first_sums(): pl.pallas_call(first_kernel, in_specs=[smem] * 2 + [in_vmem] * 4 + [any_s...]
    pallas_call x1, Pallas kernels: 248 us -> 217 us  [feed_forward(): pl.pallas_call(feed_kernel, in_specs=[any_space] * 5 + [in_vmem] + [any_s...]
    dot_general x6 -> x0, matrix products: 21.9 us -> none  [the longest x3 14.3 us: dot(): lax.dot_general(a, b, (contract, ((), ())), preferred_element_type=f32)]
    reshape x4 -> x0, local copies, waits for them, and re-layouts: 9.98 us -> none  [the longest x2 6.11 us: on_device(): w_up.reshape(shard, upper, 2, 2, 2, 2, piece_rows)]
    convert_element_type x4 -> x0, local copies, waits for them, and re-layouts: 9.24 us -> none  [the longest x3 8.21 us: on_device(): up_grad = up_grad.reshape(shard, hidden).astype(f32)]
  transfers between devices with their start and end apart: 9 -> 4, of which waited for: 2 -> 0; matrix products, arithmetic and copies ran while one was open for 7% -> 0% of each run, Pallas kernels for 33% -> 5%
where the time goes in v4:
time: 705 us; the launch traced here: 695 us
  Pallas kernels  664 us (94%)
  local copies, waits for them, and re-layouts  14.1 us (2%)
  other arithmetic  9.29 us (1%)
    pallas_call x1, Pallas kernels, first_sums(): pl.pallas_call(first_kernel, in_specs=[smem] * 2 + [in_vmem] * 4 + [any_s...  272 us
    pallas_call x1, Pallas kernels, feed_forward(): pl.pallas_call(feed_kernel, in_specs=[any_space] * 5 + [in_vmem] + [any_s...  217 us
    pallas_call x1, Pallas kernels, last_sums(): pl.pallas_call(last_kernel, in_specs=[in_vmem, in_vmem, any_space] + [in_...  141 us
    pallas_call x1, Pallas kernels, attend_back(): pl.pallas_call(functools.partial(attend_back_kernel, heads, length), grid...  33.6 us
  transfers between devices with their start and end apart: 4, of which 0 were waited for; matrix products, arithmetic and copies ran while one was open for 0% of the time, Pallas kernels for 5%

profile of v4, /device:TPU:8, one launch (start us, length us, event | category | flops | bytes accessed | tf_op | source)
XLA Modules:
  0.0 694.6 jit_solution(13473831426483102508)
XLA Ops:
  0.8 1.4 fusion.onehot_ref
  2.9 1.2 pad_add_fusion.limit_ref
  4.2 1.5 concatenate.10.router_ref
  5.6 272.1 %shard_map.230 = (bf16[2048,768]{1,0:T(8,128)(2,1)}, f32[2048,256]{1,0:T(8,128)}, f32[2048,256]{1,0:T(8,128)}, f32[256,2048]{1,0:T(8,128)}, f32[256,8]{1,0:T(8,1...) custom-call(s32[1]{0:T(128)S(6)} %copy.33.split_ref, ...), custom_call_target="tpu_custom_call" | custom-call | flops 10737418240 | bytes 33554432 | tf_op jit(solution)/shard_map/pallas_call | solution.py:1301
  277.7 217.3 %shard_map.231 = (f32[8,2048]{1,0:T(8,128)}, bf16[256,2048]{1,0:T(8,128)(2,1)}, f32[256,2048]{1,0:T(8,128)}, bf16[256,2048]{1,0:T(8,128)(2,1)}, bf16[8,256,256]{...) custom-call(bf16[1024,2048]{1,0:T(8,128)(2,1)} %get-tuple-element.43, ...), custom_call_target="tpu_custom_call" | custom-call | flops 51539607552 | bytes 33554432 | tf_op jit(solution)/shard_map/pallas_call | solution.py:789
  495.1 2.0 add.165
  497.1 0.8 dynamic-slice_bitcast_fusion
  497.9 0.7 collective-permute-start.1
  498.6 3.3 collective-permute-start.2
  501.9 0.1 collective-permute-start.3
  502.1 1.3 collective-permute-start
  503.4 0.3 multiply_reduce_fusion
  503.7 33.6 %shard_map.232 = bf16[1,2048,768]{2,1,0:T(8,128)(2,1)} custom-call(s32[1]{0:T(128)S(6)} %copy.33.split_ref, s32[1,3]{1,0:T(1,128)} %pad_add_fusion.limit_ref, bf16[1,2048,768]{2,1,0:T(8,128)(2,1)} %bitcast.70, f32[1,2048,256]{2,1,0:T(8,128)} %bitcast.72, f32[1,2048,256]{2,1,0:T(8,128)} %bitcast.73, bf16[1,2048,256]{2,1,0:T(8,128)(2,1)} %bitcast.74, ...), custom_call_target="tpu_custom_call" | custom-call | flops 10737418240 | bytes 16777216 | tf_op jit(solution)/shard_map/pallas_call | solution.py:207
  537.4 1.7 convert_add_fusion
  539.1 0.8 copy.26.inv_ref
  539.9 0.6 pad_maximum_fusion.small_ref
  540.6 0.7 copy-done.12
  541.2 0.1 copy-done.13
  541.3 0.4 copy-done.11
  541.7 141.0 %shard_map.233 = (f32[256,2048]{1,0:T(8,128)}, f32[64,2048]{1,0:T(8,128)}, f32[64,6144]{1,0:T(8,128)}, f32[8,2048]{1,0:T(8,128)}, f32[64,8192]{1,0:T(8,128)}) custom-call(bf16[2048,768]{1,0:T(8,128)(2,1)} %bitcast.71, bf16[2048,768]{1,0:T(8,128)(2,1)} %bitcast.69, bf16[2048,2048]{1,0:T(8,128)(2,1)} %bitcast.66, ...), custom_call_target="tpu_custom_call" | custom-call | flops 12884901888 | bytes 16777216 | tf_op jit(solution)/shard_map/pallas_call | solution.py:1609
  682.7 1.7 fusion.10
  684.4 1.5 slice_bitcast_fusion
  685.8 1.2 convert_bitcast_fusion
  687.0 0.6 div.39
  687.7 1.0 copy.34
  688.6 1.3 copy.35
  690.0 0.8 copy-done.2
  690.8 1.1 copy.36
  691.9 0.2 copy-done.7
  692.2 0.8 copy.37
  693.0 0.2 copy-done
  693.1 1.3 copy.38
  (33 shorter events, 0.3 us)
Async XLA Ops:
  495.0 8.4 %copy-start.3 = (bf16[1,256,2048]{2,1,0:T(8,128)(2,1)S(1)}, bf16[1,256,2048]{2,1,0:T(8,128)(2,1)}, u32[]{:S(2)}) copy-start(bf16[1,256,2048]{2,1,0:T(8,128)(2,1)} %param.15) | copy-start | bytes 3145732
  497.9 42.6 %collective-permute-start.1 = (bf16[64,2048]{1,0:T(8,128)(2,1)S(1)}, bf16[64,2048]{1,0:T(8,128)(2,1)S(1)}, u32[]{:S(2)}, u32[]{:S(2)}) collective-permute-start(bf16[64,2048]{1,0:T(8,128)(2,1)S(1)} %get-tuple-element.77), channel_id=1, source_target_pairs={{0,2},{1,3},{2,0},{3,1},{4,6},{5,7},{6,4},{7,5},{8,10},{9,11},{10,... | collective-permute-start | bytes 786440 | tf_op jit(solution)/shard_map/ppermute | solution.py:1650
  498.6 41.9 %collective-permute-start.2 = (bf16[64,2048]{1,0:T(8,128)(2,1)S(1)}, bf16[64,2048]{1,0:T(8,128)(2,1)S(1)}, u32[]{:S(2)}, u32[]{:S(2)}) collective-permute-start(bf16[64,2048]{1,0:T(8,128)(2,1)S(1)} %get-tuple-element.76), channel_id=1, source_target_pairs={{0,8},{4,12},{8,0},{12,4},{16,24},{20,28},{24,16},{28,20},{1,9},{5... | collective-permute-start | bytes 786440 | tf_op jit(solution)/shard_map/ppermute | solution.py:1650
  501.9 38.6 %collective-permute-start.3 = (bf16[64,2048]{1,0:T(8,128)(2,1)S(1)}, bf16[64,2048]{1,0:T(8,128)(2,1)}, u32[]{:S(2)}, u32[]{:S(2)}) collective-permute-start(bf16[64,2048]{1,0:T(8,128)(2,1)S(1)} %get-tuple-element.75), channel_id=1, source_target_pairs={{0,10},{1,11},{2,8},{3,9},{4,14},{5,15},{6,12},{7,13},{8,2},{9,3},... | collective-permute-start | bytes 786440 | tf_op jit(solution)/shard_map/ppermute | solution.py:1897
  502.1 38.5 %collective-permute-start = (bf16[4,64,2048]{2,1,0:T(8,128)(2,1)}, bf16[4,64,2048]{2,1,0:T(8,128)(2,1)S(1)}, u32[]{:S(2)}, u32[]{:S(2)}) collective-permute-start(bf16[4,64,2048]{2,1,0:T(8,128)(2,1)} %get-tuple-element.63), channel_id=1, source_target_pairs={{0,2},{1,3},{2,0},{3,1},{4,6},{5,7},{6,4},{7,5},{8,10},{9,11},{10,... | collective-permute-start | bytes 3145736 | tf_op jit(solution)/shard_map/ppermute | solution.py:1650
  503.7 33.6 %copy-start.5 = (bf16[2,2,64,2048]{3,2,1,0:T(8,128)(2,1)S(1)}, bf16[2,2,64,2048]{3,2,1,0:T(8,128)(2,1)}, u32[]{:S(2)}) copy-start(bf16[2,2,64,2048]{3,2,1,0:T(8,128)(2,1)} %get-tuple-element.72) | copy-start | bytes 3145732
  503.7 33.6 %copy-start.6 = (bf16[2,2,64,2048]{3,2,1,0:T(8,128)(2,1)S(1)}, bf16[2,2,64,2048]{3,2,1,0:T(8,128)(2,1)}, u32[]{:S(2)}) copy-start(bf16[2,2,64,2048]{3,2,1,0:T(8,128)(2,1)} %get-tuple-element.73) | copy-start | bytes 3145732
  537.3 1.7 copy-start.8
  537.3 2.6 copy-start.9
  540.5 0.7 copy-start.12
  540.6 0.8 copy-start.13
  540.6 1.1 copy-start.11
  541.7 145.4 %copy-start.10 = (f32[2048]{0:T(1024)S(1)}, f32[2048]{0:T(1024)}, u32[]{:S(2)}) copy-start(f32[2048]{0:T(1024)} %param.16) | copy-start | bytes 24580
  541.7 146.0 %copy-start.4 = (bf16[256,2048]{1,0:T(8,128)(2,1)S(1)}, bf16[256,2048]{1,0:T(8,128)(2,1)}, u32[]{:S(2)}) copy-start(bf16[256,2048]{1,0:T(8,128)(2,1)} %get-tuple-element.54) | copy-start | bytes 3145732
  682.7 5.9 copy-start.1
  688.6 2.2 copy-start.2
  690.8 1.4 copy-start.7
  690.8 2.3 copy-start

commit v5 on v4

--- a/solution.py
+++ b/solution.py
@@ -126,72 +126,94 @@
     )(split, limits, proj, cos2, sin2)
 
 
-def attend_back_kernel(heads, length, split_ref, limit_ref, qkv_ref, att_ref, lse_ref, dat_ref, cos_ref, sin_ref, dproj_ref, datt_ref, delta_ref, dq_ref):
+def attend_back_kernel(
+    heads,
+    length,
+    split_ref,
+    limit_ref,
+    qkv_ref,
+    att_ref,
+    lse_ref,
+    dat_ref,
+    cos_ref,
+    sin_ref,
+    dproj_ref,
+    datt_ref,
+    delta_ref,
+    dq_ref,
+):
     row = pl.program_id(0)
     split = split_ref[row]
     scale = HEAD_DIM ** (-0.5)
     block = min(BLOCK, length)
     blocks = length // block
     width = heads * HEAD_DIM
-    for h in range(heads):
-        qcol = pl.ds(h * HEAD_DIM, HEAD_DIM)
-        kcol = pl.ds(width + h * HEAD_DIM, HEAD_DIM)
-        vcol = pl.ds(2 * width + h * HEAD_DIM, HEAD_DIM)
-
-        def prepare(i, carry):
-            rows = pl.ds(pl.multiple_of(i * block, block), block)
+    qcols = [pl.ds(h * HEAD_DIM, HEAD_DIM) for h in range(heads)]
+    kcols = [pl.ds(width + h * HEAD_DIM, HEAD_DIM) for h in range(heads)]
+    vcols = [pl.ds(2 * width + h * HEAD_DIM, HEAD_DIM) for h in range(heads)]
+
+    def rows_of(i):
+        return pl.ds(pl.multiple_of(i * block, block), block)
+
+    def prepare(i, carry):
+        rows = rows_of(i)
+        at = i * block + lax.broadcasted_iota(jnp.int32, (block, 1), 0)
+        limit = jnp.where(at < split, limit_ref[row, 0], limit_ref[row, 1])
+        for h in range(heads):
+            active = (limit_ref[row, 2] + h < limit).astype(f32)
+            datt = dat_ref[rows, qcols[h]].astype(f32) * active
+            datt_ref[h, rows, :] = datt.astype(bf16)
+            delta = jnp.sum(datt * att_ref[rows, qcols[h]], axis=1, keepdims=True)
+            delta_ref[h, rows, :] = jnp.broadcast_to(delta, (block, HEAD_DIM))
+            dq_ref[h, rows, :] = jnp.zeros((block, HEAD_DIM), f32)
+        return carry
+
+    lax.fori_loop(0, blocks, prepare, 0)
+
+    def key_block(j, carry):
+        keys = rows_of(j)
+        kat = j * block + lax.broadcasted_iota(jnp.int32, (block, block), 1)
+
+        def query_block(i, state):
+            rows = rows_of(i)
             at = i * block + lax.broadcasted_iota(jnp.int32, (block, 1), 0)
-            limit = jnp.where(at < split, limit_ref[row, 0], limit_ref[row, 1])
-            active = (limit_ref[row, 2] + h < limit).astype(f32)
-            datt = dat_ref[rows, qcol].astype(f32) * active
-            datt_ref[rows, :] = datt.astype(bf16)
-            delta = jnp.sum(datt * att_ref[rows, qcol], axis=1, keepdims=True)
-            delta_ref[rows, :] = jnp.broadcast_to(delta, (block, HEAD_DIM))
-            dq_ref[rows, :] = jnp.zeros((block, HEAD_DIM), f32)
-            return carry
-
-        lax.fori_loop(0, blocks, prepare, 0)
-
-        def key_block(j, carry):
-            keys = pl.ds(pl.multiple_of(j * block, block), block)
-            k = qkv_ref[keys, kcol]
-            v = qkv_ref[keys, vcol]
-            kat = j * block + lax.broadcasted_iota(jnp.int32, (block, block), 1)
-
-            def query_block(i, state):
-                dk, dv = state
-                rows = pl.ds(pl.multiple_of(i * block, block), block)
-                q = qkv_ref[rows, qcol]
-                datt = datt_ref[rows, :]
-                at = i * block + lax.broadcasted_iota(jnp.int32, (block, 1), 0)
-                low = first_key(split, at)
-                ok = (kat <= at) & (kat >= low)
+            ok = (kat <= at) & (kat >= first_key(split, at))
+            found = []
+            for h in range(heads):
+                dk, dv = state[h]
+                q, k, v = qkv_ref[rows, qcols[h]], qkv_ref[keys, kcols[h]], qkv_ref[keys, vcols[h]]
+                datt = datt_ref[h, rows, :]
                 s = dot(q, k, ((1,), (1,))) * (scale * LOG2E)
-                lse = lse_ref[rows, qcol][:, :1]
+                lse = lse_ref[rows, qcols[h]][:, :1]
                 p = jnp.exp2(jnp.where(ok, s - lse, masked_score))
                 dp = dot(datt, v, ((1,), (1,)))
-                ds = (p * (dp - delta_ref[rows, :][:, :1])).astype(bf16)
+                ds = (p * (dp - delta_ref[h, rows, :][:, :1])).astype(bf16)
                 dv = dv + dot(p.astype(bf16), datt, ((0,), (0,)))
                 dk = dk + dot(ds, q, ((0,), (0,)))
-                dq_ref[rows, :] += dot(ds, k, ((1,), (0,)))
-                return dk, dv
-
-            stop = jnp.where((j + 1) * block <= split, (split - 1) // block + 1, blocks)
-            zero = jnp.zeros((block, HEAD_DIM), f32)
-            dk, dv = lax.fori_loop(j, stop, query_block, (zero, zero))
-            dproj_ref[keys, kcol] = turn(dk * scale, cos_ref[keys, :], -sin_ref[keys, :]).astype(bf16)
-            dproj_ref[keys, vcol] = dv.astype(bf16)
-            return carry
-
-        lax.fori_loop(0, blocks, key_block, 0)
-
-        def finish(i, carry):
-            rows = pl.ds(pl.multiple_of(i * block, block), block)
-            dq = dq_ref[rows, :] * scale
-            dproj_ref[rows, qcol] = turn(dq, cos_ref[rows, :], -sin_ref[rows, :]).astype(bf16)
-            return carry
-
-        lax.fori_loop(0, blocks, finish, 0)
+                dq_ref[h, rows, :] += dot(ds, k, ((1,), (0,)))
+                found.append((dk, dv))
+            return tuple(found)
+
+        stop = jnp.where((j + 1) * block <= split, (split - 1) // block + 1, blocks)
+        zero = jnp.zeros((block, HEAD_DIM), f32)
+        state = lax.fori_loop(j, stop, query_block, ((zero, zero),) * heads)
+        for h in range(heads):
+            dk, dv = state[h]
+            turned = turn(dk * scale, cos_ref[keys, :], -sin_ref[keys, :])
+            dproj_ref[keys, kcols[h]] = turned.astype(bf16)
+            dproj_ref[keys, vcols[h]] = dv.astype(bf16)
+        return carry
+
+    lax.fori_loop(0, blocks, key_block, 0)
+
+    def finish(i, carry):
+        rows = rows_of(i)
+        for h in range(heads):
+            dq = dq_ref[h, rows, :] * scale
+            dproj_ref[rows, qcols[h]] = turn(dq, cos_ref[rows, :], -sin_ref[rows, :]).astype(bf16)
+        return carry
+
+    lax.fori_loop(0, blocks, finish, 0)
 
 
 def attend_back(qkv, att, lse, dat, split, limits, cos2, sin2, heads):
@@ -211,9 +233,9 @@
         out_specs=whole(3 * width),
         out_shape=jax.ShapeDtypeStruct((rows, length, 3 * width), bf16),
         scratch_shapes=[
-            pltpu.VMEM((length, HEAD_DIM), bf16),
-            pltpu.VMEM((length, HEAD_DIM), f32),
-            pltpu.VMEM((length, HEAD_DIM), f32),
+            pltpu.VMEM((heads, length, HEAD_DIM), bf16),
+            pltpu.VMEM((heads, length, HEAD_DIM), f32),
+            pltpu.VMEM((heads, length, HEAD_DIM), f32),
         ],
         compiler_params=pltpu.CompilerParams(vmem_limit_bytes=56 * 2**20),
         cost_estimate=pl.CostEstimate(flops=flops, bytes_accessed=2**24, transcendentals=flops // 1280),

time: 705 us -> 702 us (level)
  transfers between devices with their start and end apart: 4 -> 4, of which waited for: 0 -> 0; matrix products, arithmetic and copies ran while one was open for 0% -> 1% of each run, Pallas kernels for 5% -> 4%
where the time goes in v5:
time: 702 us; the launch traced here: 691 us
  Pallas kernels  660 us (94%)
  local copies, waits for them, and re-layouts  14.1 us (2%)
  other arithmetic  9.29 us (1%)
    pallas_call x1, Pallas kernels, first_sums(): pl.pallas_call(first_kernel, in_specs=[smem] * 2 + [in_vmem] * 4 + [any_s...  272 us
    pallas_call x1, Pallas kernels, feed_forward(): pl.pallas_call(feed_kernel, in_specs=[any_space] * 5 + [in_vmem] + [any_s...  217 us
    pallas_call x1, Pallas kernels, last_sums(): pl.pallas_call(last_kernel, in_specs=[in_vmem, in_vmem, any_space] + [in_...  141 us
    pallas_call x1, Pallas kernels, attend_back(): pl.pallas_call(functools.partial(attend_back_kernel, heads, length), grid...  29.8 us
  transfers between devices with their start and end apart: 4, of which 0 were waited for; matrix products, arithmetic and copies ran while one was open for 1% of the time, Pallas kernels for 4%

profile of v5, /device:TPU:8, one launch (start us, length us, event | category | flops | bytes accessed | tf_op | source)
XLA Modules:
  0.0 690.9 jit_solution(280363676294174240)
XLA Ops:
  0.8 1.4 fusion.onehot_ref
  2.9 1.2 pad_add_fusion.limit_ref
  4.2 1.5 concatenate.10.router_ref
  5.6 272.1 %shard_map.230 = (bf16[2048,768]{1,0:T(8,128)(2,1)}, f32[2048,256]{1,0:T(8,128)}, f32[2048,256]{1,0:T(8,128)}, f32[256,2048]{1,0:T(8,128)}, f32[256,8]{1,0:T(8,1...) custom-call(s32[1]{0:T(128)S(6)} %copy.33.split_ref, ...), custom_call_target="tpu_custom_call" | custom-call | flops 10737418240 | bytes 33554432 | tf_op jit(solution)/shard_map/pallas_call | solution.py:1323
  277.7 217.3 %shard_map.231 = (f32[8,2048]{1,0:T(8,128)}, bf16[256,2048]{1,0:T(8,128)(2,1)}, f32[256,2048]{1,0:T(8,128)}, bf16[256,2048]{1,0:T(8,128)(2,1)}, bf16[8,256,256]{...) custom-call(bf16[1024,2048]{1,0:T(8,128)(2,1)} %get-tuple-element.43, ...), custom_call_target="tpu_custom_call" | custom-call | flops 51539607552 | bytes 33554432 | tf_op jit(solution)/shard_map/pallas_call | solution.py:811
  495.1 2.0 add.165
  497.1 0.8 dynamic-slice_bitcast_fusion
  497.9 0.7 collective-permute-start.1
  498.6 3.3 collective-permute-start.2
  501.9 0.1 collective-permute-start.3
  502.1 1.3 collective-permute-start
  503.4 0.3 multiply_reduce_fusion
  503.7 29.8 %shard_map.232 = bf16[1,2048,768]{2,1,0:T(8,128)(2,1)} custom-call(s32[1]{0:T(128)S(6)} %copy.33.split_ref, s32[1,3]{1,0:T(1,128)} %pad_add_fusion.limit_ref, bf16[1,2048,768]{2,1,0:T(8,128)(2,1)} %bitcast.70, f32[1,2048,256]{2,1,0:T(8,128)} %bitcast.72, f32[1,2048,256]{2,1,0:T(8,128)} %bitcast.73, bf16[1,2048,256]{2,1,0:T(8,128)(2,1)} %bitcast.74, ...), custom_call_target="tpu_custom_call" | custom-call | flops 10737418240 | bytes 16777216 | tf_op jit(solution)/shard_map/pallas_call | solution.py:229
  533.6 1.7 convert_add_fusion
  535.3 0.8 copy.26.inv_ref
  536.1 0.6 pad_maximum_fusion.small_ref
  536.8 0.7 copy-done.12
  537.5 0.1 copy-done.13
  537.5 0.4 copy-done.11
  537.9 141.0 %shard_map.233 = (f32[256,2048]{1,0:T(8,128)}, f32[64,2048]{1,0:T(8,128)}, f32[64,6144]{1,0:T(8,128)}, f32[8,2048]{1,0:T(8,128)}, f32[64,8192]{1,0:T(8,128)}) custom-call(bf16[2048,768]{1,0:T(8,128)(2,1)} %bitcast.71, bf16[2048,768]{1,0:T(8,128)(2,1)} %bitcast.69, bf16[2048,2048]{1,0:T(8,128)(2,1)} %bitcast.66, ...), custom_call_target="tpu_custom_call" | custom-call | flops 12884901888 | bytes 16777216 | tf_op jit(solution)/shard_map/pallas_call | solution.py:1631
  678.9 1.7 fusion.10
  680.6 1.5 slice_bitcast_fusion
  682.1 1.2 convert_bitcast_fusion
  683.3 0.6 div.39
  683.9 1.0 copy.34
  684.9 1.3 copy.35
  686.2 0.8 copy-done.2
  687.0 1.1 copy.36
  688.2 0.2 copy-done.7
  688.4 0.8 copy.37
  689.2 0.2 copy-done
  689.4 1.3 copy.38
  (33 shorter events, 0.3 us)
Async XLA Ops:
  495.0 8.4 %copy-start.3 = (bf16[1,256,2048]{2,1,0:T(8,128)(2,1)S(1)}, bf16[1,256,2048]{2,1,0:T(8,128)(2,1)}, u32[]{:S(2)}) copy-start(bf16[1,256,2048]{2,1,0:T(8,128)(2,1)} %param.15) | copy-start | bytes 3145732
  497.9 38.9 %collective-permute-start.1 = (bf16[64,2048]{1,0:T(8,128)(2,1)S(1)}, bf16[64,2048]{1,0:T(8,128)(2,1)S(1)}, u32[]{:S(2)}, u32[]{:S(2)}) collective-permute-start(bf16[64,2048]{1,0:T(8,128)(2,1)S(1)} %get-tuple-element.77), channel_id=1, source_target_pairs={{0,2},{1,3},{2,0},{3,1},{4,6},{5,7},{6,4},{7,5},{8,10},{9,11},{10,... | collective-permute-start | bytes 786440 | tf_op jit(solution)/shard_map/ppermute | solution.py:1672
  498.6 38.2 %collective-permute-start.2 = (bf16[64,2048]{1,0:T(8,128)(2,1)S(1)}, bf16[64,2048]{1,0:T(8,128)(2,1)S(1)}, u32[]{:S(2)}, u32[]{:S(2)}) collective-permute-start(bf16[64,2048]{1,0:T(8,128)(2,1)S(1)} %get-tuple-element.76), channel_id=1, source_target_pairs={{0,8},{4,12},{8,0},{12,4},{16,24},{20,28},{24,16},{28,20},{1,9},{5... | collective-permute-start | bytes 786440 | tf_op jit(solution)/shard_map/ppermute | solution.py:1672
  501.9 34.9 %collective-permute-start.3 = (bf16[64,2048]{1,0:T(8,128)(2,1)S(1)}, bf16[64,2048]{1,0:T(8,128)(2,1)}, u32[]{:S(2)}, u32[]{:S(2)}) collective-permute-start(bf16[64,2048]{1,0:T(8,128)(2,1)S(1)} %get-tuple-element.75), channel_id=1, source_target_pairs={{0,10},{1,11},{2,8},{3,9},{4,14},{5,15},{6,12},{7,13},{8,2},{9,3},... | collective-permute-start | bytes 786440 | tf_op jit(solution)/shard_map/ppermute | solution.py:1919
  502.1 34.7 %collective-permute-start = (bf16[4,64,2048]{2,1,0:T(8,128)(2,1)}, bf16[4,64,2048]{2,1,0:T(8,128)(2,1)S(1)}, u32[]{:S(2)}, u32[]{:S(2)}) collective-permute-start(bf16[4,64,2048]{2,1,0:T(8,128)(2,1)} %get-tuple-element.63), channel_id=1, source_target_pairs={{0,2},{1,3},{2,0},{3,1},{4,6},{5,7},{6,4},{7,5},{8,10},{9,11},{10,... | collective-permute-start | bytes 3145736 | tf_op jit(solution)/shard_map/ppermute | solution.py:1672
  503.7 29.8 %copy-start.5 = (bf16[2,2,64,2048]{3,2,1,0:T(8,128)(2,1)S(1)}, bf16[2,2,64,2048]{3,2,1,0:T(8,128)(2,1)}, u32[]{:S(2)}) copy-start(bf16[2,2,64,2048]{3,2,1,0:T(8,128)(2,1)} %get-tuple-element.72) | copy-start | bytes 3145732
  503.7 29.8 %copy-start.6 = (bf16[2,2,64,2048]{3,2,1,0:T(8,128)(2,1)S(1)}, bf16[2,2,64,2048]{3,2,1,0:T(8,128)(2,1)}, u32[]{:S(2)}) copy-start(bf16[2,2,64,2048]{3,2,1,0:T(8,128)(2,1)} %get-tuple-element.73) | copy-start | bytes 3145732
  533.5 1.7 copy-start.8
  533.6 2.6 copy-start.9
  536.8 0.7 copy-start.12
  536.8 0.8 copy-start.13
  536.8 1.1 copy-start.11
  537.9 145.4 %copy-start.10 = (f32[2048]{0:T(1024)S(1)}, f32[2048]{0:T(1024)}, u32[]{:S(2)}) copy-start(f32[2048]{0:T(1024)} %param.16) | copy-start | bytes 24580
  537.9 146.0 %copy-start.4 = (bf16[256,2048]{1,0:T(8,128)(2,1)S(1)}, bf16[256,2048]{1,0:T(8,128)(2,1)}, u32[]{:S(2)}) copy-start(bf16[256,2048]{1,0:T(8,128)(2,1)} %get-tuple-element.54) | copy-start | bytes 3145732
  678.9 5.9 copy-start.1
  684.9 2.2 copy-start.2
  687.0 1.4 copy-start.7
  687.0 2.3 copy-start

commit v6 on v5

--- a/solution.py
+++ b/solution.py
@@ -730,6 +730,7 @@
         copy.start()
         dats.append(copy)
     keep.append(load(dat_block(w), dat_out.at[w], 26))
+    near_sum(3)
 
     low_load = load(low_ref, hid.at[slot(0)], 1)
     low_load.wait()
@@ -788,7 +789,6 @@
             out_ys.append(copy)
         else:
             keep.append(load(source, out_other.at[i - 4], 51 + i))
-    near_sum(3)
     for copy in keep:
         copy.wait()
     for copy in fars + dats + out_ys:

time: 702 us -> 702 us (level)
  no operation moved by 1% of the time
where the time goes in v6:
time: 702 us; the launch traced here: 691 us
  Pallas kernels  655 us (93%)
  local copies, waits for them, and re-layouts  14.1 us (2%)
  starting transfers between devices  11.4 us (2%)
  other arithmetic  9.29 us (1%)
    pallas_call x1, Pallas kernels, first_sums(): pl.pallas_call(first_kernel, in_specs=[smem] * 2 + [in_vmem] * 4 + [any_s...  272 us
    pallas_call x1, Pallas kernels, feed_forward(): pl.pallas_call(feed_kernel, in_specs=[any_space] * 5 + [in_vmem] + [any_s...  212 us
    pallas_call x1, Pallas kernels, last_sums(): pl.pallas_call(last_kernel, in_specs=[in_vmem, in_vmem, any_space] + [in_...  141 us
    pallas_call x1, Pallas kernels, attend_back(): pl.pallas_call(functools.partial(attend_back_kernel, heads, length), grid...  29.8 us
  transfers between devices with their start and end apart: 4, of which 0 were waited for; matrix products, arithmetic and copies ran while one was open for 1% of the time, Pallas kernels for 4%

profile of v6, /device:TPU:8, one launch (start us, length us, event | category | flops | bytes accessed | tf_op | source)
XLA Modules:
  0.0 691.4 jit_solution(1299685119136397536)
XLA Ops:
  0.8 1.4 fusion.onehot_ref
  2.9 1.2 pad_add_fusion.limit_ref
  4.2 1.5 concatenate.10.router_ref
  5.6 272.1 %shard_map.230 = (bf16[2048,768]{1,0:T(8,128)(2,1)}, f32[2048,256]{1,0:T(8,128)}, f32[2048,256]{1,0:T(8,128)}, f32[256,2048]{1,0:T(8,128)}, f32[256,8]{1,0:T(8,1...) custom-call(s32[1]{0:T(128)S(6)} %copy.33.split_ref, ...), custom_call_target="tpu_custom_call" | custom-call | flops 10737418240 | bytes 33554432 | tf_op jit(solution)/shard_map/pallas_call | solution.py:1323
  277.7 211.9 %shard_map.231 = (f32[8,2048]{1,0:T(8,128)}, bf16[256,2048]{1,0:T(8,128)(2,1)}, f32[256,2048]{1,0:T(8,128)}, bf16[256,2048]{1,0:T(8,128)(2,1)}, bf16[8,256,256]{...) custom-call(bf16[1024,2048]{1,0:T(8,128)(2,1)} %get-tuple-element.43, ...), custom_call_target="tpu_custom_call" | custom-call | flops 51539607552 | bytes 33554432 | tf_op jit(solution)/shard_map/pallas_call | solution.py:811
  489.6 2.0 add.165
  491.7 0.8 dynamic-slice_bitcast_fusion
  492.5 0.6 collective-permute-start.1
  493.1 9.3 %collective-permute-start.2 = (bf16[64,2048]{1,0:T(8,128)(2,1)S(1)}, bf16[64,2048]{1,0:T(8,128)(2,1)S(1)}, u32[]{:S(2)}, u32[]{:S(2)}) collective-permute-start(bf16[64,2048]{1,0:T(8,128)(2,1)S(1)} %get-tuple-element.76), channel_id=1, source_target_pairs={{0,8},{4,12},{8,0},{12,4},{16,24},{20,28},{24,16},{28,20},{1,9},{5... | collective-permute-start | bytes 786440 | tf_op jit(solution)/shard_map/ppermute | solution.py:1672
  502.5 0.1 collective-permute-start.3
  502.6 1.3 collective-permute-start
  503.9 0.3 multiply_reduce_fusion
  504.2 29.8 %shard_map.232 = bf16[1,2048,768]{2,1,0:T(8,128)(2,1)} custom-call(s32[1]{0:T(128)S(6)} %copy.33.split_ref, s32[1,3]{1,0:T(1,128)} %pad_add_fusion.limit_ref, bf16[1,2048,768]{2,1,0:T(8,128)(2,1)} %bitcast.70, f32[1,2048,256]{2,1,0:T(8,128)} %bitcast.72, f32[1,2048,256]{2,1,0:T(8,128)} %bitcast.73, bf16[1,2048,256]{2,1,0:T(8,128)(2,1)} %bitcast.74, ...), custom_call_target="tpu_custom_call" | custom-call | flops 10737418240 | bytes 16777216 | tf_op jit(solution)/shard_map/pallas_call | solution.py:229
  534.1 1.7 convert_add_fusion
  535.8 0.8 copy.26.inv_ref
  536.6 0.6 pad_maximum_fusion.small_ref
  537.3 0.7 copy-done.12
  538.0 0.1 copy-done.13
  538.1 0.4 copy-done.11
  538.4 141.0 %shard_map.233 = (f32[256,2048]{1,0:T(8,128)}, f32[64,2048]{1,0:T(8,128)}, f32[64,6144]{1,0:T(8,128)}, f32[8,2048]{1,0:T(8,128)}, f32[64,8192]{1,0:T(8,128)}) custom-call(bf16[2048,768]{1,0:T(8,128)(2,1)} %bitcast.71, bf16[2048,768]{1,0:T(8,128)(2,1)} %bitcast.69, bf16[2048,2048]{1,0:T(8,128)(2,1)} %bitcast.66, ...), custom_call_target="tpu_custom_call" | custom-call | flops 12884901888 | bytes 16777216 | tf_op jit(solution)/shard_map/pallas_call | solution.py:1631
  679.5 1.7 fusion.10
  681.1 1.5 slice_bitcast_fusion
  682.6 1.2 convert_bitcast_fusion
  683.8 0.6 div.39
  684.4 1.0 copy.34
  685.4 1.3 copy.35
  686.7 0.8 copy-done.2
  687.6 1.1 copy.36
  688.7 0.2 copy-done.7
  688.9 0.8 copy.37
  689.7 0.2 copy-done
  689.9 1.3 copy.38
  (33 shorter events, 0.3 us)
Async XLA Ops:
  489.6 14.3 %copy-start.3 = (bf16[1,256,2048]{2,1,0:T(8,128)(2,1)S(1)}, bf16[1,256,2048]{2,1,0:T(8,128)(2,1)}, u32[]{:S(2)}) copy-start(bf16[1,256,2048]{2,1,0:T(8,128)(2,1)} %param.15) | copy-start | bytes 3145732
  492.5 44.8 %collective-permute-start.1 = (bf16[64,2048]{1,0:T(8,128)(2,1)S(1)}, bf16[64,2048]{1,0:T(8,128)(2,1)S(1)}, u32[]{:S(2)}, u32[]{:S(2)}) collective-permute-start(bf16[64,2048]{1,0:T(8,128)(2,1)S(1)} %get-tuple-element.77), channel_id=1, source_target_pairs={{0,2},{1,3},{2,0},{3,1},{4,6},{5,7},{6,4},{7,5},{8,10},{9,11},{10,... | collective-permute-start | bytes 786440 | tf_op jit(solution)/shard_map/ppermute | solution.py:1672
  493.1 44.2 %collective-permute-start.2 = (bf16[64,2048]{1,0:T(8,128)(2,1)S(1)}, bf16[64,2048]{1,0:T(8,128)(2,1)S(1)}, u32[]{:S(2)}, u32[]{:S(2)}) collective-permute-start(bf16[64,2048]{1,0:T(8,128)(2,1)S(1)} %get-tuple-element.76), channel_id=1, source_target_pairs={{0,8},{4,12},{8,0},{12,4},{16,24},{20,28},{24,16},{28,20},{1,9},{5... | collective-permute-start | bytes 786440 | tf_op jit(solution)/shard_map/ppermute | solution.py:1672
  502.5 34.8 %collective-permute-start.3 = (bf16[64,2048]{1,0:T(8,128)(2,1)S(1)}, bf16[64,2048]{1,0:T(8,128)(2,1)}, u32[]{:S(2)}, u32[]{:S(2)}) collective-permute-start(bf16[64,2048]{1,0:T(8,128)(2,1)S(1)} %get-tuple-element.75), channel_id=1, source_target_pairs={{0,10},{1,11},{2,8},{3,9},{4,14},{5,15},{6,12},{7,13},{8,2},{9,3},... | collective-permute-start | bytes 786440 | tf_op jit(solution)/shard_map/ppermute | solution.py:1919
  502.6 34.7 %collective-permute-start = (bf16[4,64,2048]{2,1,0:T(8,128)(2,1)}, bf16[4,64,2048]{2,1,0:T(8,128)(2,1)S(1)}, u32[]{:S(2)}, u32[]{:S(2)}) collective-permute-start(bf16[4,64,2048]{2,1,0:T(8,128)(2,1)} %get-tuple-element.63), channel_id=1, source_target_pairs={{0,2},{1,3},{2,0},{3,1},{4,6},{5,7},{6,4},{7,5},{8,10},{9,11},{10,... | collective-permute-start | bytes 3145736 | tf_op jit(solution)/shard_map/ppermute | solution.py:1672
  504.2 29.8 %copy-start.5 = (bf16[2,2,64,2048]{3,2,1,0:T(8,128)(2,1)S(1)}, bf16[2,2,64,2048]{3,2,1,0:T(8,128)(2,1)}, u32[]{:S(2)}) copy-start(bf16[2,2,64,2048]{3,2,1,0:T(8,128)(2,1)} %get-tuple-element.72) | copy-start | bytes 3145732
  504.2 29.8 %copy-start.6 = (bf16[2,2,64,2048]{3,2,1,0:T(8,128)(2,1)S(1)}, bf16[2,2,64,2048]{3,2,1,0:T(8,128)(2,1)}, u32[]{:S(2)}) copy-start(bf16[2,2,64,2048]{3,2,1,0:T(8,128)(2,1)} %get-tuple-element.73) | copy-start | bytes 3145732
  534.1 1.7 copy-start.8
  534.1 2.6 copy-start.9
  537.3 0.7 copy-start.12
  537.3 0.8 copy-start.13
  537.3 1.1 copy-start.11
  538.4 145.4 %copy-start.10 = (f32[2048]{0:T(1024)S(1)}, f32[2048]{0:T(1024)}, u32[]{:S(2)}) copy-start(f32[2048]{0:T(1024)} %param.16) | copy-start | bytes 24580
  538.4 146.0 %copy-start.4 = (bf16[256,2048]{1,0:T(8,128)(2,1)S(1)}, bf16[256,2048]{1,0:T(8,128)(2,1)}, u32[]{:S(2)}) copy-start(bf16[256,2048]{1,0:T(8,128)(2,1)} %get-tuple-element.54) | copy-start | bytes 3145732
  679.5 5.9 copy-start.1
  685.4 2.2 copy-start.2
  687.5 1.4 copy-start.7
  687.5 2.3 copy-start
